TPU v7x, 1024 devices: a whole 4x4x32 slice. The times are simulated.
1024 devices in a mesh: exp: 64 (over x_lo, z), dp: 16 (over x_hi, y, core).
Axes of the slice: x: 4 (x_hi: 2, x_lo: 2; x = x_hi * 2 + x_lo), y: 4, z: 32, core: 2. Of those that a mesh axis runs over, the one named last changes fastest.
Arguments:
- hidden_acts: bfloat16 [64, 2048, 1024], P('exp', 'dp'), may hold values from -6 to 6
- train_rows: int32 [64, 2048], P('exp', 'dp'), may hold values from 0 to 255
- out_grad: bfloat16 [4096, 3584], P('dp'), may hold values from -0.1796875 to 0.1796875
- master: float32 [64, 1024, 3584], P('exp', 'dp'), may hold values from -0.1875 to 0.1875
- moment1: bfloat16 [64, 1024, 3584], P('exp', 'dp'), may hold values from -0.119628906 to 0.119628906
- moment2: bfloat16 [64, 1024, 3584], P('exp', 'dp'), may hold values from 0.0049743652 to 0.049804688
- gate_up: bfloat16 [64, 3584, 2, 1024], P('exp', 'dp'), may hold values from -0.09375 to 0.09375
- dec_tokens: bfloat16 [512, 3584], P('exp', 'dp'), may hold values from -6 to 6
- route_ids: int32 [512, 8], P('exp'), may hold values from 0 to 63, all different within a row; in each aligned block of 8 rows (0 to 7, 8 to 15, ...) at most 2 rows name the same one
- route_gates: float32 [512, 8], P('exp'), may hold values from 0.1 to 1
Outputs:
- moe_out: bfloat16 [512, 3584], P('exp', 'dp')
Inputs may be any that keep to these rules, and one draw needn't show every extreme that they name: `route_ids`: each row names 8 different experts; among the 8 rows of one index of exp no expert is named more than 2 times, a bound that some block reaches.
All inputs are finite; a program needn't handle non-finite values.
Results may differ from a plain program's by a relative error of at most 0.03.
Values may be sent and summed in bfloat16 or wider, within the bound.
No kernel may reach another device: no remote copies, remote signals or barrier semaphores. Data moves between devices by JAX's collectives and lax.ppermute only.
A program may use at most 64 MiB of HBM per device.

v0:
```python
import jax
import jax.numpy as jnp
from jax import lax
from jax.sharding import PartitionSpec as P

beta_one = 0.9
beta_two = 0.95
learn_rate = 0.1
weight_decay = 0.1
epsilon = 1e-08
bias_first = 1.0 - 0.9**20
bias_second = 1.0 - 0.95**20


def adam_tile(gradient, master_rows, first_old, second_old):
    first = beta_one * first_old.astype(jnp.float32) + (1.0 - beta_one) * gradient
    second = beta_two * second_old.astype(jnp.float32) + (1.0 - beta_two) * gradient * gradient
    update = first / bias_first / (jnp.sqrt(second / bias_second) + epsilon)
    return (master_rows * (1.0 - learn_rate * weight_decay) - learn_rate * update).astype(
        jnp.bfloat16
    )


def body(
    hidden_acts,
    train_rows,
    out_grad,
    master,
    moment1,
    moment2,
    gate_up,
    dec_tokens,
    route_ids,
    route_gates,
):
    activity = hidden_acts[0]
    selected = jnp.take(out_grad, train_rows[0], axis=0)
    gradient = lax.psum_scatter(
        lax.dot_general(
            activity, selected, (((0,), (0,)), ((), ())), preferred_element_type=jnp.float32
        ).astype(jnp.bfloat16),
        "dp",
        scatter_dimension=0,
        tiled=True,
    ).astype(jnp.float32)
    trainer_tile = adam_tile(gradient, master[0], moment1[0], moment2[0])
    server_tile = lax.all_to_all(trainer_tile, "dp", split_axis=1, concat_axis=0, tiled=True)
    token_count, local_width = dec_tokens.shape
    choices_per = route_ids.shape[1]
    expert_count = lax.axis_size("exp")
    capacity = min(token_count, max(2, 2 * choices_per * token_count // expert_count))
    slot_count = expert_count * capacity
    flat_ids = route_ids.reshape(-1)
    onehot = (flat_ids[:, None] == jnp.arange(expert_count, dtype=jnp.int32)[None, :]).astype(
        jnp.int32
    )
    earlier = jnp.cumsum(onehot, axis=0) - onehot
    position = jnp.sum(earlier * onehot, axis=1)
    slot_index = flat_ids * capacity + position
    placement = (slot_index[:, None] == jnp.arange(slot_count, dtype=jnp.int32)[None, :]).astype(
        jnp.bfloat16
    )
    repeated = jnp.repeat(dec_tokens, choices_per, axis=0)
    outgoing = jnp.einsum(
        "rs,rd->sd", placement, repeated, preferred_element_type=jnp.float32
    ).astype(jnp.bfloat16)
    weights_local = gate_up[0]
    arrived = lax.all_to_all(
        outgoing.reshape(expert_count, capacity, local_width),
        "exp",
        split_axis=0,
        concat_axis=0,
        tiled=True,
    )
    sources, within, _ = arrived.shape
    rows_in = arrived.reshape(sources * within, local_width)
    mixed = jnp.einsum("sd,dgf->sgf", rows_in, weights_local, preferred_element_type=jnp.float32)
    shares = lax.psum_scatter(
        mixed.astype(jnp.bfloat16), "dp", scatter_dimension=2, tiled=True
    ).astype(jnp.float32)
    partial_hidden = (jax.nn.silu(shares[:, 0]) * shares[:, 1]).astype(jnp.bfloat16)
    hidden = lax.all_gather(partial_hidden, "dp", axis=1, tiled=True)
    results = jnp.dot(hidden, server_tile, preferred_element_type=jnp.float32).astype(jnp.bfloat16)
    returned = lax.all_to_all(
        results.reshape(sources, within, local_width),
        "exp",
        split_axis=0,
        concat_axis=0,
        tiled=True,
    )
    back_rows = returned.reshape(slot_count, local_width)
    chosen = jnp.einsum("rs,sd->rd", placement, back_rows, preferred_element_type=jnp.float32)
    weighted = chosen.reshape(token_count, choices_per, local_width) * route_gates[:, :, None]
    return jnp.sum(weighted, axis=1).astype(jnp.bfloat16)


def solution(mesh):
    in_specs = (
        P("exp", "dp", None),
        P("exp", "dp"),
        P("dp", None),
        P("exp", "dp", None),
        P("exp", "dp", None),
        P("exp", "dp", None),
        P("exp", "dp", None, None),
        P("exp", "dp"),
        P("exp", None),
        P("exp", None),
    )
    out_specs = P("exp", "dp")
    return jax.shard_map(body, mesh=mesh, in_specs=in_specs, out_specs=out_specs, check_vma=False)
```

profile of v0, /device:TPU:4, one launch (start us, length us, event | category | flops | bytes accessed | tf_op | source)
XLA Modules:
  0.0 386.8 jit_solution(18088567967448955829)
XLA Ops:
  6.5 0.0 copy-start
  6.5 0.0 reduce-scatter.7.cloned.1.call-start
  6.5 0.8 fusion.28
  7.3 0.7 compare_and_fusion
  8.0 0.1 copy-done
  8.1 0.0 copy-start.3
  8.1 1.1 gather_fusion
  9.2 0.0 copy-done.3
  9.2 5.2 %fusion = bf16[1024,3584]{0,1:T(8,128)(2,1)} fusion(bf16[128,3584]{1,0:T(8,128)(2,1)S(1)} %gather_fusion, pred[128]{0:T(512)(128)(4,1)S(1)} %compare_and_fusion, bf16[1,128,1024]{2,1,0:T(8,128)(2,1)S(1)} %copy-done.3), kind=kOutput, calls=%fused_computation.2 | convolution fusion | flops 943652864 | bytes 8519808 | tf_op jit(solution)/shard_map/dot_general | solution.py:39
  14.4 10.0 %copy.37 = bf16[1024,3584]{1,0:T(8,128)(2,1)} copy(bf16[1024,3584]{0,1:T(8,128)(2,1)} %fusion) | data formatting | bytes 14680064
  24.4 0.0 copy-start.4
  24.4 0.0 copy-start.5
  24.4 0.0 copy-start.1
  24.4 0.0 reduce-scatter.7.cloned.1.call-update
  24.4 0.7 copy-done.4
  25.1 0.0 copy-start.2
  25.1 0.1 eq.50
  25.1 0.1 fusion.22
  25.2 0.1 reduce_window_sum.11
  25.3 0.2 select_reduce_fusion
  25.5 0.0 copy-done.5
  25.5 0.2 convolution_convert_fusion.3
  25.8 0.1 copy.24
  25.9 0.7 reshape.97
  26.6 30.0 %all-to-all-start = ((bf16[64,2,224]{2,1,0:T(2,128)(2,1)}), bf16[64,2,224]{2,1,0:T(2,128)(2,1)S(1)}, u32[]{:S(2)}, u32[]{:S(2)}) async-start(bf16[64,2,224]{2,1,0:T(2,128)(2,1)} %reshape.97), calls=%async_computation | async-start | bytes 131072 | tf_op jit(solution)/shard_map/all_to_all | solution.py:68
  56.5 0.0 reduce-scatter.5.cloned.1.call-start
  56.6 0.0 copy-done.1
  56.6 1.9 copy.27
  58.5 0.0 copy-done.2
  58.5 0.4 copy.28
  58.9 2.3 copy.29
  61.2 21.0 %all-to-all-done = bf16[64,2,224]{2,1,0:T(2,128)(2,1)S(1)} async-done(((bf16[64,2,224]{2,1,0:T(2,128)(2,1)}), bf16[64,2,224]{2,1,0:T(2,128)(2,1)S(1)}, u32[]{:S(2)}, u32[]{:S(2)}) %all-to-all-start) | async-done | bytes 57376 | tf_op jit(solution)/shard_map/all_to_all | solution.py:68
  82.2 0.1 reshape.98
  82.2 2.5 convolution_convert_fusion.1
  84.8 0.0 reduce-scatter.5.cloned.1.call-update
  84.8 93.2 %reduce-scatter.7.cloned.1.call-done = bf16[64,3584]{1,0:T(8,128)(2,1)} async-done(((bf16[1024,3584]{1,0:T(8,128)(2,1)}), bf16[64,3584]{1,0:T(8,128)(2,1)}) %reduce-scatter.7.cloned.1.call-update) | async-done | bytes 458768
  177.9 2.3 copy.38
  180.2 4.5 %fusion.10 = bf16[64,3584]{0,1:T(8,128)(2,1)} fusion(bf16[1,64,3584]{1,2,0:T(8,128)(2,1)} %copy.29, bf16[64,3584]{0,1:T(8,128)(2,1)} %copy.38, bf16[1,64,3584]{1,2,0:T(8,128)(2,1)S(1)} %copy.28, f32[1,64,3584]{1,2,0:T(8,128)} %copy.27), kind=kLoop, calls=%fused_computation.14 | loop fusion | flops 4128768 | bytes 2752512 | tf_op jit(solution)/shard_map/convert_element_type | solution.py:19
  184.8 0.0 copy-start.6
  184.8 2.3 copy.30
  187.1 6.7 %all-to-all-start.1 = ((bf16[64,16,224]{2,0,1:T(8,128)(2,1)}), bf16[64,16,224]{2,0,1:T(8,128)(2,1)S(1)}, u32[]{:S(2)}, u32[]{:S(2)}) async-start(bf16[64,16,224]{2,0,1:T(8,128)(2,1)} %copy.30), calls=%async_computation.2 | async-start | bytes 1048576 | tf_op jit(solution)/shard_map/all_to_all | solution.py:47
  193.7 110.5 %reduce-scatter.5.cloned.1.call-done = bf16[128,2,64]{0,2,1:T(8,128)(2,1)} async-done(((bf16[128,2,1024]{0,2,1:T(8,128)(2,1)}), bf16[128,2,64]{0,2,1:T(8,128)(2,1)}) %reduce-scatter.5.cloned.1.call-update) | async-done | bytes 32784 | tf_op jit(solution)/shard_map/reduce_scatter | solution.py:78
  304.2 0.8 convert_element_type.45
  305.0 22.3 %all_gather.3 = bf16[128,1024]{0,1:T(8,128)(2,1)S(1)} all-gather(bf16[128,64]{0,1:T(8,128)(2,1)S(1)} %fusion.20), channel_id=1, replica_groups=mesh['exp'=64,'dp'=16] {'dp'}, dimensions={1}, use_global_device_ids=true | all-gather | bytes 278528 | tf_op jit(solution)/shard_map/all_gather | solution.py:82
  327.4 0.0 all-to-all-done.1
  327.4 0.3 convolution_convert_fusion.2
  327.7 0.1 copy.31
  327.8 0.7 reshape.99
  328.5 24.2 %all-to-all-start.2 = ((bf16[64,2,224]{2,1,0:T(2,128)(2,1)}), bf16[64,2,224]{2,1,0:T(2,128)(2,1)S(1)}, u32[]{:S(2)}, u32[]{:S(2)}) async-start(bf16[64,2,224]{2,1,0:T(2,128)(2,1)} %reshape.99), calls=%async_computation.3 | async-start | bytes 131072 | tf_op jit(solution)/shard_map/all_to_all | solution.py:84
  352.7 0.1 reduce_sum.21
  352.8 26.3 %all-to-all-done.2 = bf16[64,2,224]{2,1,0:T(2,128)(2,1)S(1)} async-done(((bf16[64,2,224]{2,1,0:T(2,128)(2,1)}), bf16[64,2,224]{2,1,0:T(2,128)(2,1)S(1)}, u32[]{:S(2)}, u32[]{:S(2)}) %all-to-all-start.2) | async-done | bytes 57376 | tf_op jit(solution)/shard_map/all_to_all | solution.py:84
  379.1 0.1 reshape.100
  379.2 0.0 copy-done.6
  379.2 0.8 fusion.11
  (4 shorter events, 0.0 us)
Async XLA Ops:
  6.5 1.5 copy-start
  6.5 171.4 %reduce-scatter.7.cloned.1.call-start = ((), (), s32[]{:S(2)}) async-start(), calls=%async_computation.6 | async-start | bytes 7798784
  8.1 1.1 copy-start.3
  24.4 0.7 copy-start.4
  24.4 1.1 copy-start.5
  24.4 32.2 %copy-start.1 = (f32[1,64,3584]{2,1,0:T(8,128)S(1)}, f32[1,64,3584]{2,1,0:T(8,128)}, u32[]{:S(2)}) copy-start(f32[1,64,3584]{2,1,0:T(8,128)} %param.13) | copy-start | bytes 2752516
  25.1 33.4 %copy-start.2 = (bf16[1,64,3584]{2,1,0:T(8,128)(2,1)S(1)}, bf16[1,64,3584]{2,1,0:T(8,128)(2,1)}, u32[]{:S(2)}) copy-start(bf16[1,64,3584]{2,1,0:T(8,128)(2,1)} %param.14) | copy-start | bytes 1376260
  26.6 55.6 %all-to-all-start = ((bf16[64,2,224]{2,1,0:T(2,128)(2,1)}), bf16[64,2,224]{2,1,0:T(2,128)(2,1)S(1)}, u32[]{:S(2)}, u32[]{:S(2)}) async-start(bf16[64,2,224]{2,1,0:T(2,128)(2,1)} %reshape.97), calls=%async_computation | async-start | bytes 131072 | tf_op jit(solution)/shard_map/all_to_all | solution.py:68
  56.5 247.7 %reduce-scatter.5.cloned.1.call-start = ((), (), s32[]{:S(2)}) async-start(), calls=%async_computation.5 | async-start | bytes 557056 | tf_op jit(solution)/shard_map/reduce_scatter | solution.py:78
  184.8 194.4 %copy-start.6 = (f32[8,8]{1,0:T(8,128)S(1)}, f32[8,8]{1,0:T(8,128)}, u32[]{:S(2)}) copy-start(f32[8,8]{1,0:T(8,128)} %param.19) | copy-start | bytes 772
  187.1 140.3 %all-to-all-start.1 = ((bf16[64,16,224]{2,0,1:T(8,128)(2,1)}), bf16[64,16,224]{2,0,1:T(8,128)(2,1)S(1)}, u32[]{:S(2)}, u32[]{:S(2)}) async-start(bf16[64,16,224]{2,0,1:T(8,128)(2,1)} %copy.30), calls=%async_computation.2 | async-start | bytes 1048576 | tf_op jit(solution)/shard_map/all_to_all | solution.py:47
  328.5 50.6 %all-to-all-start.2 = ((bf16[64,2,224]{2,1,0:T(2,128)(2,1)}), bf16[64,2,224]{2,1,0:T(2,128)(2,1)S(1)}, u32[]{:S(2)}, u32[]{:S(2)}) async-start(bf16[64,2,224]{2,1,0:T(2,128)(2,1)} %reshape.99), calls=%async_computation.3 | async-start | bytes 131072 | tf_op jit(solution)/shard_map/all_to_all | solution.py:84
Sparse Core Ops, SparseCore 0:
  24.5 153.3 reduce-scatter.6
  183.7 120.5 reduce-scatter.4
where the time goes:
time: 388 us; the launch traced here: 387 us
  waiting for transfers between devices  251 us (65%)
  starting transfers between devices  60.9 us (16%)
  local copies, waits for them, and re-layouts  22.8 us (6%)
  blocking collectives  22.3 us (6%)
  between operations  13.5 us (3%)
  matrix products  9.14 us (2%)
  other arithmetic  7.15 us (2%)
    reduce_scatter x1, waiting for transfers between devices, body(): lax.psum_scatter(mixed.astype(jnp.bfloat16), 'dp', scatter_dimension=2, t...  111 us
    unnamed x3, waiting for transfers between devices  93.2 us
    all_to_all x1, starting transfers between devices, body(): lax.all_to_all(outgoing.reshape(expert_count, capacity, local_width), 'ex...  30 us
    all_to_all x1, waiting for transfers between devices, body(): lax.all_to_all(results.reshape(sources, within, local_width), 'exp', spli...  26.3 us
    all_to_all x1, starting transfers between devices, body(): lax.all_to_all(results.reshape(sources, within, local_width), 'exp', spli...  24.2 us
    all_gather x1, blocking collectives, body(): hidden = lax.all_gather(partial_hidden, 'dp', axis=1, tiled=True)  22.3 us
    all_to_all x1, waiting for transfers between devices, body(): lax.all_to_all(outgoing.reshape(expert_count, capacity, local_width), 'ex...  21 us
    unnamed x19, local copies, waits for them, and re-layouts  17.6 us
  transfers between devices with their start and end apart: 5, of which 4 were waited for; matrix products, arithmetic and copies ran while one was open for 5% of the time, Pallas kernels for 0%

commit v1 on v0

v1 whole, which is shorter than its diff:
```python
import functools

import jax
import jax.numpy as jnp
from jax import lax
from jax.experimental import pallas as pl
from jax.experimental.pallas import tpu as pltpu
from jax.sharding import PartitionSpec as P

beta_one = 0.9
beta_two = 0.95
learn_rate = 0.1
weight_decay = 0.1
epsilon = 1e-08
bias_first = 1.0 - 0.9**20
bias_second = 1.0 - 0.95**20

HALVES, RING, CORES = 2, 4, 2
SMEM = pl.BlockSpec(memory_space=pltpu.SMEM)
LIMIT = 48 * 2**20


def whole(*shape):
    return pl.BlockSpec(shape, lambda *_: (0,) * len(shape))


def contract_first(left, right):
    return lax.dot_general(
        left, right, (((0,), (0,)), ((), ())), preferred_element_type=jnp.float32
    )


def permutation(half_step, ring_step, core_step):
    pairs = []
    for half in range(HALVES):
        for ring in range(RING):
            for core in range(CORES):
                source = (half * RING + ring) * CORES + core
                target = (half ^ half_step) * RING + (ring + ring_step) % RING
                pairs.append((source, target * CORES + (core ^ core_step)))
    return pairs


def pack_kernel(place_ref, rows_ref, grad_ref, master_ref, first_ref, second_ref, *outs):
    table, columns = grad_ref.shape
    tokens = rows_ref.shape[1]
    rows = master_ref.shape[1]
    run = columns // (HALVES * RING)
    onehot = (lax.broadcasted_iota(jnp.int32, (table, tokens), 0) == rows_ref[...]).astype(
        jnp.float32
    ).astype(jnp.bfloat16)
    ring = place_ref[1]
    for here in range(RING):

        @pl.when(ring == here)
        def _(here=here):
            for step in range(RING):
                out = outs[step]
                for half in range(HALVES):
                    start = (half * RING + (here + step) % RING) * run
                    take = pl.ds(start, run)
                    put = pl.ds(half * run, run)
                    out[0:tokens, put] = contract_first(onehot, grad_ref[:, take]).astype(
                        jnp.bfloat16
                    )
                    at = tokens
                    out[at : at + rows, put] = master_ref[0, :, take].astype(jnp.bfloat16)
                    out[at + rows : at + 2 * rows, put] = first_ref[0, :, take]
                    out[at + 2 * rows : at + 3 * rows, put] = second_ref[0, :, take]


def pack(place, train_rows, out_grad, master, moment1, moment2):
    tokens = train_rows.shape[1]
    rows = master.shape[1]
    shape = (tokens + 3 * rows, out_grad.shape[1] // RING)
    return pl.pallas_call(
        pack_kernel,
        out_shape=[jax.ShapeDtypeStruct(shape, jnp.bfloat16)] * RING,
        in_specs=[SMEM] + [pl.BlockSpec(memory_space=pltpu.VMEM)] * 5,
        out_specs=[pl.BlockSpec(memory_space=pltpu.VMEM)] * RING,
        compiler_params=pltpu.CompilerParams(vmem_limit_bytes=LIMIT),
        cost_estimate=pl.CostEstimate(
            flops=2 * tokens * out_grad.size, bytes_accessed=7_000_000, transcendentals=0
        ),
    )(place, train_rows, out_grad, master, moment1, moment2)


def gradient_kernel(place_ref, acts_ref, *refs):
    parts, (theirs_ref, ours_ref) = refs[:RING], refs[RING:]
    ring, core = place_ref[1], place_ref[2]
    acts = [acts_ref[(ring - step + RING) % RING] for step in range(RING)]
    total = None
    for step in range(0, RING, 2):
        left = jnp.concatenate([acts[step], acts[step + 1]], axis=0)
        right = jnp.concatenate([parts[step][...], parts[step + 1][...]], axis=0)
        product = contract_first(left, right)
        total = product if total is None else total + product
    rows = total.shape[0] // 2
    upper, lower = total[:rows], total[rows:]
    ours_ref[0] = jnp.where(core == 0, upper, lower)
    theirs_ref[0] = jnp.where(core == 0, lower, upper).astype(jnp.bfloat16)


def gradients(place, acts, parts):
    ring_tokens, units = acts.shape
    tokens = ring_tokens // RING
    width = parts[0].shape[1]
    blocks = HALVES * RING
    block = units // blocks
    rows = block // 2
    return pl.pallas_call(
        gradient_kernel,
        grid=(blocks,),
        out_shape=[
            jax.ShapeDtypeStruct((blocks, rows, width), jnp.bfloat16),
            jax.ShapeDtypeStruct((blocks, rows, width), jnp.float32),
        ],
        in_specs=[SMEM, pl.BlockSpec((RING, tokens, block), lambda i: (0, 0, i))]
        + [whole(tokens, width)] * RING,
        out_specs=[pl.BlockSpec((1, rows, width), lambda i: (i, 0, 0))] * 2,
        compiler_params=pltpu.CompilerParams(vmem_limit_bytes=LIMIT),
        cost_estimate=pl.CostEstimate(
            flops=2 * units * width * ring_tokens, bytes_accessed=5_000_000, transcendentals=0
        ),
    )(place, acts.reshape(RING, tokens, units), *parts)


def adam_kernel(tokens, place_ref, ours_ref, near_ref, far_ref, *refs):
    states, outs = refs[:RING], refs[RING:]
    half, ring, core = place_ref[0], place_ref[1], place_ref[2]
    rows, columns = far_ref.shape[1:]
    width = columns // len(outs)
    for step in range(RING):
        source = (ring - step + RING) % RING
        block = half * RING + source
        gradient = (
            ours_ref[block]
            + near_ref[block].astype(jnp.float32)
            + far_ref[source].astype(jnp.float32)
        )
        state = states[step]
        master = state[tokens : tokens + rows, :].astype(jnp.float32)
        first_old = state[tokens + rows : tokens + 2 * rows, :].astype(jnp.float32)
        second_old = state[tokens + 2 * rows : tokens + 3 * rows, :].astype(jnp.float32)
        first = beta_one * first_old + (1.0 - beta_one) * gradient
        second = beta_two * second_old + (1.0 - beta_two) * gradient * gradient
        update = first / bias_first / (jnp.sqrt(second / bias_second) + epsilon)
        tile = (master * (1.0 - learn_rate * weight_decay) - learn_rate * update).astype(
            jnp.bfloat16
        )
        put = pl.ds(pl.multiple_of(source * rows, rows), rows)
        for here in range(HALVES * CORES):

            @pl.when(half * CORES + core == here)
            def _(here=here, put=put, tile=tile):
                for block in range(HALVES * CORES):
                    outs[block ^ here][put, :] = tile[:, block * width : (block + 1) * width]


def adam_tiles(tokens, place, ours, near, far, parts):
    rows, columns = far.shape[1:]
    groups = HALVES * CORES
    return pl.pallas_call(
        functools.partial(adam_kernel, tokens),
        out_shape=[jax.ShapeDtypeStruct((RING * rows, columns // groups), jnp.bfloat16)] * groups,
        in_specs=[SMEM] + [pl.BlockSpec(memory_space=pltpu.VMEM)] * (3 + RING),
        out_specs=[pl.BlockSpec(memory_space=pltpu.VMEM)] * groups,
        compiler_params=pltpu.CompilerParams(vmem_limit_bytes=LIMIT),
        cost_estimate=pl.CostEstimate(
            flops=20 * far.size, bytes_accessed=6_500_000, transcendentals=2 * far.size
        ),
    )(place, ours, near, far, *parts)


def results_kernel(place_ref, hidden_ref, *refs):
    tiles, out_ref = refs[:-1], refs[-1]
    half, core = place_ref[0], place_ref[2]
    total = None
    for relative, tile in enumerate(tiles):
        from_half = jnp.bitwise_xor(half, relative // CORES)
        from_core = jnp.bitwise_xor(core, relative % CORES)
        hidden = jnp.concatenate(
            [hidden_ref[(from_half * RING + ring) * CORES + from_core] for ring in range(RING)],
            axis=0,
        )
        product = contract_first(hidden, tile[...])
        total = product if total is None else total + product
    out_ref[...] = total.astype(jnp.bfloat16)


def expert_results(place, hidden, tiles):
    slots, width = hidden.shape[2], tiles[0].shape[1]
    return pl.pallas_call(
        results_kernel,
        out_shape=jax.ShapeDtypeStruct((slots, width), jnp.bfloat16),
        in_specs=[SMEM] + [pl.BlockSpec(memory_space=pltpu.VMEM)] * (1 + len(tiles)),
        out_specs=pl.BlockSpec(memory_space=pltpu.VMEM),
        compiler_params=pltpu.CompilerParams(vmem_limit_bytes=LIMIT),
        cost_estimate=pl.CostEstimate(
            flops=2 * hidden.size * width, bytes_accessed=800_000, transcendentals=0
        ),
    )(place, hidden, *tiles)


def body(
    hidden_acts,
    train_rows,
    out_grad,
    master,
    moment1,
    moment2,
    gate_up,
    dec_tokens,
    route_ids,
    route_gates,
):
    index = lax.axis_index("dp")
    shards = lax.axis_size("dp")
    half, ring, core = index >> 3, (index >> 1) & (RING - 1), index & (CORES - 1)
    place = jnp.stack([half, ring, core]).astype(jnp.int32)
    token_count, width = dec_tokens.shape
    tokens = train_rows.shape[1]

    rings = [
        [(h * RING + r) * CORES + c for r in range(RING)]
        for h in range(HALVES)
        for c in range(CORES)
    ]
    acts = lax.all_gather(hidden_acts[0], "dp", axis=0, tiled=True, axis_index_groups=rings)
    sends = pack(place, train_rows, out_grad, master, moment1, moment2)
    parts = [sends[0]] + [
        lax.ppermute(sends[step], "dp", permutation(0, step, 0)) for step in range(1, RING)
    ]

    choices_per = route_ids.shape[1]
    expert_count = lax.axis_size("exp")
    capacity = min(token_count, max(2, 2 * choices_per * token_count // expert_count))
    slot_count = expert_count * capacity
    flat_ids = route_ids.reshape(-1)
    onehot = (flat_ids[:, None] == jnp.arange(expert_count, dtype=jnp.int32)[None, :]).astype(
        jnp.int32
    )
    earlier = jnp.cumsum(onehot, axis=0) - onehot
    position = jnp.sum(earlier * onehot, axis=1)
    slot_index = flat_ids * capacity + position
    placement = (slot_index[:, None] == jnp.arange(slot_count, dtype=jnp.int32)[None, :]).astype(
        jnp.bfloat16
    )
    repeated = jnp.repeat(dec_tokens, choices_per, axis=0)
    outgoing = jnp.einsum(
        "rs,rd->sd", placement, repeated, preferred_element_type=jnp.float32
    ).astype(jnp.bfloat16)
    arrived = lax.all_to_all(
        outgoing.reshape(expert_count, capacity, width),
        "exp",
        split_axis=0,
        concat_axis=0,
        tiled=True,
    )
    rows_in = arrived.reshape(slot_count, width)

    mixed = jnp.einsum(
        "dgf,sd->gfs", gate_up[0], rows_in, preferred_element_type=jnp.float32
    ).astype(jnp.bfloat16)
    units = mixed.shape[1] // shards
    mixed = mixed.reshape(2, shards, units, slot_count).transpose(1, 0, 2, 3)
    shares = lax.all_to_all(mixed, "dp", split_axis=0, concat_axis=0, tiled=True)
    shares = jnp.sum(shares.astype(jnp.float32), axis=0)
    hidden_part = (jax.nn.silu(shares[0]) * shares[1]).astype(jnp.bfloat16)
    hidden = lax.all_to_all(
        jnp.broadcast_to(hidden_part[None], (shards, units, slot_count)),
        "dp",
        split_axis=0,
        concat_axis=0,
        tiled=True,
    )

    theirs, ours = gradients(place, acts, parts)
    near = lax.ppermute(theirs, "dp", permutation(0, 0, 1))
    other = (1 - half) * RING
    crossing = lax.dynamic_slice_in_dim(ours, other, RING, 0) + lax.dynamic_slice_in_dim(
        near, other, RING, 0
    ).astype(jnp.float32)
    far = lax.ppermute(crossing.astype(jnp.bfloat16), "dp", permutation(1, 0, 0))
    tiles = adam_tiles(tokens, place, ours, near, far, parts)
    tiles = [
        tiles[0],
        lax.ppermute(tiles[1], "dp", permutation(0, 0, 1)),
        lax.ppermute(tiles[2], "dp", permutation(1, 0, 0)),
        lax.ppermute(tiles[3], "dp", permutation(1, 0, 1)),
    ]

    results = expert_results(place, hidden, tiles)
    returned = lax.all_to_all(
        results.reshape(expert_count, capacity, width),
        "exp",
        split_axis=0,
        concat_axis=0,
        tiled=True,
    )
    back_rows = returned.reshape(slot_count, width)
    chosen = jnp.einsum("rs,sd->rd", placement, back_rows, preferred_element_type=jnp.float32)
    weighted = chosen.reshape(token_count, choices_per, width) * route_gates[:, :, None]
    return jnp.sum(weighted, axis=1).astype(jnp.bfloat16)


def solution(mesh):
    in_specs = (
        P("exp", "dp", None),
        P("exp", "dp"),
        P("dp", None),
        P("exp", "dp", None),
        P("exp", "dp", None),
        P("exp", "dp", None),
        P("exp", "dp", None, None),
        P("exp", "dp"),
        P("exp", None),
        P("exp", None),
    )
    out_specs = P("exp", "dp")
    return jax.shard_map(body, mesh=mesh, in_specs=in_specs, out_specs=out_specs, check_vma=False)
```

time: 388 us -> 190 us (0.49)
  the two profiles are of different devices: /device:TPU:4 before, /device:TPU:8 now
where the time goes in v1:
time: 190 us; the launch traced here: 189 us
  starting transfers between devices  86.9 us (46%)
  waiting for transfers between devices  47.3 us (25%)
  local copies, waits for them, and re-layouts  23.4 us (12%)
  between operations  13.6 us (7%)
  Pallas kernels  12.5 us (7%)
  other arithmetic  3.48 us (2%)
    all_to_all x1, waiting for transfers between devices, body(): lax.all_to_all(results.reshape(expert_count, capacity, width), 'exp', spl...  26.1 us
    ppermute x3, starting transfers between devices, body(): lax.ppermute(sends[step], 'dp', permutation(0, step, 0))  20.9 us
    all_to_all x1, starting transfers between devices, body(): lax.all_to_all(outgoing.reshape(expert_count, capacity, width), 'exp', sp...  20 us
    unnamed x46, local copies, waits for them, and re-layouts  18 us
    all_to_all x1, starting transfers between devices, body(): lax.all_to_all(results.reshape(expert_count, capacity, width), 'exp', spl...  17.2 us
    all_to_all x1, waiting for transfers between devices, body(): lax.all_to_all(outgoing.reshape(expert_count, capacity, width), 'exp', sp...  10.5 us
    all_to_all x1, starting transfers between devices, body(): lax.all_to_all(jnp.broadcast_to(hidden_part[None], (shards, units, slot_c...  7.45 us
    all_to_all x1, starting transfers between devices, body(): lax.all_to_all(mixed, 'dp', split_axis=0, concat_axis=0, tiled=True)  5.47 us
  transfers between devices with their start and end apart: 13, of which 7 were waited for; matrix products, arithmetic and copies ran while one was open for 5% of the time, Pallas kernels for 6%

profile of v1, /device:TPU:8, one launch (start us, length us, event | category | flops | bytes accessed | tf_op | source)
XLA Modules:
  0.0 188.7 jit_solution(7635776467617591423)
XLA Ops:
  6.5 0.7 all-gather.3.cloned.1.call-update
  7.3 0.1 pad_add_fusion.place_ref
  7.3 1.5 copy-done.1
  8.8 1.2 copy-done.2
  10.0 1.0 copy-done.14
  11.0 1.0 copy-done.15
  12.1 0.7 copy-done.18
  12.7 2.8 %shard_map.100 = (bf16[320,896]{1,0:T(8,128)(2,1)S(1)}, bf16[320,896]{1,0:T(8,128)(2,1)}, bf16[320,896]{1,0:T(8,128)(2,1)}, bf16[320,896]{1,0:T(8,128)(2,1)}) custom-call(s32[3]{0:T(128)S(1)} %pad_add_fusion.place_ref, s32[1,128]{1,0:T(1,128)S(1)} %copy-done.18, bf16[256,3584]{1,0:T(8,128)(2,1)S(1)} %copy-done.1, f32[1,64,3584]{2,1,0:T(8,128)S(1)} %copy-done.2, ...), custom_call_target="tpu_custom_call" | custom-call | flops 234881024 | bytes 7000000 | tf_op jit(solution)/shard_map/pallas_call | solution.py:76
  15.5 3.5 %collective-permute-start = (bf16[320,896]{1,0:T(8,128)(2,1)}, bf16[320,896]{1,0:T(8,128)(2,1)S(1)}, u32[]{:S(2)}, u32[]{:S(2)}) collective-permute-start(bf16[320,896]{1,0:T(8,128)(2,1)} %get-tuple-element.16), channel_id=1, source_target_pairs={{0,2},{1,3},{2,4},{3,5},{4,6},{5,7},{6,0},{7,1},{8,10},{9,11},{10,... | collective-permute-start | bytes 1720328 | tf_op jit(solution)/shard_map/ppermute | solution.py:232
  19.0 15.5 %collective-permute-start.1 = (bf16[320,896]{1,0:T(8,128)(2,1)}, bf16[320,896]{1,0:T(8,128)(2,1)S(1)}, u32[]{:S(2)}, u32[]{:S(2)}) collective-permute-start(bf16[320,896]{1,0:T(8,128)(2,1)} %get-tuple-element.17), channel_id=1, source_target_pairs={{0,4},{1,5},{2,6},{3,7},{4,0},{5,1},{6,2},{7,3},{8,12},{9,13},{10,... | collective-permute-start | bytes 1720328 | tf_op jit(solution)/shard_map/ppermute | solution.py:232
  34.5 1.9 %collective-permute-start.2 = (bf16[320,896]{1,0:T(8,128)(2,1)}, bf16[320,896]{1,0:T(8,128)(2,1)S(1)}, u32[]{:S(2)}, u32[]{:S(2)}) collective-permute-start(bf16[320,896]{1,0:T(8,128)(2,1)} %get-tuple-element.18), channel_id=1, source_target_pairs={{0,6},{1,7},{2,0},{3,1},{4,2},{5,3},{6,4},{7,5},{8,14},{9,15},{10,... | collective-permute-start | bytes 1720328 | tf_op jit(solution)/shard_map/ppermute | solution.py:232
  36.5 0.1 eq.50
  36.6 0.1 fusion.7
  36.6 0.1 reduce_window_sum.11
  36.7 0.2 select_reduce_fusion
  36.9 0.2 convolution_convert_fusion.1
  37.2 0.1 copy.18
  37.3 0.7 reshape.58
  38.0 20.0 %all-to-all-start = ((bf16[64,2,224]{2,1,0:T(2,128)(2,1)}), bf16[64,2,224]{2,1,0:T(2,128)(2,1)S(1)}, u32[]{:S(2)}, u32[]{:S(2)}) async-start(bf16[64,2,224]{2,1,0:T(2,128)(2,1)} %reshape.58), calls=%async_computation | async-start | bytes 131072 | tf_op jit(solution)/shard_map/all_to_all | solution.py:253
  58.0 0.0 collective-permute-done.refs_1_
  58.0 0.8 copy-done.5
  58.8 0.8 copy-done.8
  59.6 0.0 collective-permute-done.2.refs_3_
  59.6 0.8 copy-done.11
  60.4 0.8 all-gather.3.cloned.1.call-done
  61.2 1.1 copy-done.6
  62.3 1.1 copy-done.9
  63.3 1.1 copy-done.12
  64.4 1.2 copy-done.19
  65.6 5.1 %shard_map.101 = (bf16[8,64,896]{2,1,0:T(8,128)(2,1)}, f32[8,64,896]{2,1,0:T(8,128)S(1)}) custom-call(s32[3]{0:T(128)S(1)} %pad_add_fusion.place_ref, bf16[4,128,1024]{2,1,0:T(8,128)(2,1)S(1)} %bitcast.25, bf16[320,896]{1,0:T(8,128)(2,1)S(1)} %get-tuple-element.15.refs_0_, bf16[320,896]{1,0:T(8,128)(2,1)S(1)} %copy-done.6, bf16[320,896]{1,0:T(8,128)(2,1)S(1)} %copy-done.9, ...), custom_call_target="tpu_custom_call" | custom-call | flops 939524096 | bytes 5000000 | tf_op jit(solution)/shard_map/pallas_call | solution.py:111
  70.7 1.9 %collective-permute-start.3 = (bf16[8,64,896]{2,1,0:T(8,128)(2,1)}, bf16[8,64,896]{2,1,0:T(8,128)(2,1)}, u32[]{:S(2)}, u32[]{:S(2)}) collective-permute-start(bf16[8,64,896]{2,1,0:T(8,128)(2,1)} %get-tuple-element.20), channel_id=1, source_target_pairs={{0,1},{1,0},{2,3},{3,2},{4,5},{5,4},{6,7},{7,6},{8,9},{9,8},{10,11... | collective-permute-start | bytes 2752520 | tf_op jit(solution)/shard_map/ppermute | solution.py:279
  72.6 10.5 %all-to-all-done = bf16[64,2,224]{2,1,0:T(2,128)(2,1)S(1)} async-done(((bf16[64,2,224]{2,1,0:T(2,128)(2,1)}), bf16[64,2,224]{2,1,0:T(2,128)(2,1)S(1)}, u32[]{:S(2)}, u32[]{:S(2)}) %all-to-all-start) | async-done | bytes 57376 | tf_op jit(solution)/shard_map/all_to_all | solution.py:253
  83.1 0.1 reshape.59
  83.2 0.4 fusion
  83.7 1.0 copy.21
  84.7 1.9 %copy.22 = bf16[16,2,64,128]{3,2,1,0:T(8,128)(2,1)} copy(bf16[16,2,64,128]{3,2,0,1:T(8,128)(2,1)} %bitcast.26) | data formatting | bytes 1048576 | tf_op jit(solution)/shard_map/transpose | solution.py:266
  86.6 5.5 %all-to-all-start.1 = ((bf16[16,2,64,128]{3,2,1,0:T(8,128)(2,1)}), bf16[16,2,64,128]{3,2,1,0:T(8,128)(2,1)}, u32[]{:S(2)}, u32[]{:S(2)}) async-start(bf16[16,2,64,128]{3,2,1,0:T(8,128)(2,1)} %copy.22), calls=%async_computation.1 | async-start | bytes 1048576 | tf_op jit(solution)/shard_map/all_to_all | solution.py:267
  92.0 0.0 collective-permute-done.3.near_ref
  92.0 1.9 %add_convert_fusion = bf16[4,64,896]{2,1,0:T(8,128)(2,1)} fusion(f32[8,64,896]{2,1,0:T(8,128)S(1)} %get-tuple-element.19.ours_ref, s32[]{:T(128)S(6)} %select_n.4, bf16[8,64,896]{2,1,0:T(8,128)(2,1)} %collective-permute-done.3.near_ref), kind=kLoop, calls=%fused_computation.7 | loop fusion | flops 688128 | bytes 1835012 | tf_op jit(solution)/shard_map/convert_element_type | solution.py:284
  93.9 4.9 %collective-permute-start.4 = (bf16[4,64,896]{2,1,0:T(8,128)(2,1)}, bf16[4,64,896]{2,1,0:T(8,128)(2,1)S(1)}, u32[]{:S(2)}, u32[]{:S(2)}) collective-permute-start(bf16[4,64,896]{2,1,0:T(8,128)(2,1)} %add_convert_fusion), channel_id=1, source_target_pairs={{0,8},{1,9},{2,10},{3,11},{4,12},{5,13},{6,14},{7,15},{8,0},{9,1},... | collective-permute-start | bytes 1376264 | tf_op jit(solution)/shard_map/ppermute | solution.py:284
  98.8 2.1 %all-to-all-done.1 = bf16[16,2,64,128]{3,2,1,0:T(8,128)(2,1)} async-done(((bf16[16,2,64,128]{3,2,1,0:T(8,128)(2,1)}), bf16[16,2,64,128]{3,2,1,0:T(8,128)(2,1)}, u32[]{:S(2)}, u32[]{:S(2)}) %all-to-all-start.1) | async-done | bytes 524320 | tf_op jit(solution)/shard_map/all_to_all | solution.py:267
  100.9 1.1 convert_reduce_fusion
  102.1 0.7 broadcast_in_dim.8
  102.8 7.5 %all-to-all-start.2 = ((bf16[16,64,128]{2,1,0:T(8,128)(2,1)}), bf16[16,64,128]{2,1,0:T(8,128)(2,1)S(1)}, u32[]{:S(2)}, u32[]{:S(2)}) async-start(bf16[16,64,128]{2,1,0:T(8,128)(2,1)} %broadcast_in_dim.8), calls=%async_computation.2 | async-start | bytes 524288 | tf_op jit(solution)/shard_map/all_to_all | solution.py:270
  110.3 1.4 collective-permute-done.4.far_ref
  111.7 1.1 copy-done.4
  112.7 1.1 copy-done.7
  113.8 1.1 copy-done.10
  114.8 1.1 copy-done.13
  115.9 3.8 %shard_map.102 = (bf16[256,224]{1,0:T(8,128)(2,1)S(1)}, bf16[256,224]{1,0:T(8,128)(2,1)}, bf16[256,224]{1,0:T(8,128)(2,1)}, bf16[256,224]{1,0:T(8,128)(2,1)}) custom-call(s32[3]{0:T(128)S(1)} %pad_add_fusion.place_ref, f32[8,64,896]{2,1,0:T(8,128)S(1)} %get-tuple-element.19.ours_ref, bf16[8,64,896]{2,1,0:T(8,128)(2,1)} %collective-permute-done.3.near_ref, ...), custom_call_target="tpu_custom_call" | custom-call | flops 4587520 | bytes 6500000 | tf_op jit(solution)/shard_map/pallas_call | solution.py:163
  119.7 0.6 copy-done.16
  120.4 1.9 %collective-permute-start.5 = (bf16[256,224]{1,0:T(8,128)(2,1)}, bf16[256,224]{1,0:T(8,128)(2,1)S(1)}, u32[]{:S(2)}, u32[]{:S(2)}) collective-permute-start(bf16[256,224]{1,0:T(8,128)(2,1)} %get-tuple-element.22), channel_id=1, source_target_pairs={{0,1},{1,0},{2,3},{3,2},{4,5},{5,4},{6,7},{7,6},{8,9},{9,8},{10,11... | collective-permute-start | bytes 344072 | tf_op jit(solution)/shard_map/ppermute | solution.py:288
  122.3 3.7 %collective-permute-start.6 = (bf16[256,224]{1,0:T(8,128)(2,1)}, bf16[256,224]{1,0:T(8,128)(2,1)S(1)}, u32[]{:S(2)}, u32[]{:S(2)}) collective-permute-start(bf16[256,224]{1,0:T(8,128)(2,1)} %get-tuple-element.23), channel_id=1, source_target_pairs={{0,8},{1,9},{2,10},{3,11},{4,12},{5,13},{6,14},{7,15},{8,0},{9,1},... | collective-permute-start | bytes 344072 | tf_op jit(solution)/shard_map/ppermute | solution.py:289
  126.0 3.5 %collective-permute-start.7 = (bf16[256,224]{1,0:T(8,128)(2,1)}, bf16[256,224]{1,0:T(8,128)(2,1)S(1)}, u32[]{:S(2)}, u32[]{:S(2)}) collective-permute-start(bf16[256,224]{1,0:T(8,128)(2,1)} %get-tuple-element.24), channel_id=1, source_target_pairs={{0,9},{1,8},{2,11},{3,10},{4,13},{5,12},{6,15},{7,14},{8,1},{9,0},... | collective-permute-start | bytes 344072 | tf_op jit(solution)/shard_map/ppermute | solution.py:290
  129.5 2.3 %collective-permute-done.6.refs_2_ = bf16[256,224]{1,0:T(8,128)(2,1)S(1)} collective-permute-done((bf16[256,224]{1,0:T(8,128)(2,1)}, bf16[256,224]{1,0:T(8,128)(2,1)S(1)}, u32[]{:S(2)}, u32[]{:S(2)}) %collective-permute-start.6) | collective-permute-done | bytes 114720 | tf_op jit(solution)/shard_map/ppermute | solution.py:289
  131.8 3.4 %collective-permute-done.7.refs_3_ = bf16[256,224]{1,0:T(8,128)(2,1)S(1)} collective-permute-done((bf16[256,224]{1,0:T(8,128)(2,1)}, bf16[256,224]{1,0:T(8,128)(2,1)S(1)}, u32[]{:S(2)}, u32[]{:S(2)}) %collective-permute-start.7) | collective-permute-done | bytes 114720 | tf_op jit(solution)/shard_map/ppermute | solution.py:290
  135.2 0.9 copy-done.17
  136.1 0.8 shard_map.103
  136.9 0.7 reshape.62
  137.5 17.2 %all-to-all-start.3 = ((bf16[64,2,224]{2,1,0:T(2,128)(2,1)}), bf16[64,2,224]{2,1,0:T(2,128)(2,1)S(1)}, u32[]{:S(2)}, u32[]{:S(2)}) async-start(bf16[64,2,224]{2,1,0:T(2,128)(2,1)} %reshape.62), calls=%async_computation.3 | async-start | bytes 131072 | tf_op jit(solution)/shard_map/all_to_all | solution.py:294
  154.8 0.1 reduce_sum.30
  154.9 26.1 %all-to-all-done.3 = bf16[64,2,224]{2,1,0:T(2,128)(2,1)S(1)} async-done(((bf16[64,2,224]{2,1,0:T(2,128)(2,1)}), bf16[64,2,224]{2,1,0:T(2,128)(2,1)S(1)}, u32[]{:S(2)}, u32[]{:S(2)}) %all-to-all-start.3) | async-done | bytes 57376 | tf_op jit(solution)/shard_map/all_to_all | solution.py:294
  181.0 0.1 reshape.63
  181.0 0.8 fusion.1
  (35 shorter events, 0.1 us)
Async XLA Ops:
  6.5 76.7 %copy-start = (bf16[1,224,2,1024]{3,2,1,0:T(2,128)(2,1)S(1)}, bf16[1,224,2,1024]{3,2,1,0:T(2,128)(2,1)}, u32[]{:S(2)}) copy-start(bf16[1,224,2,1024]{3,2,1,0:T(2,128)(2,1)} %param.16) | copy-start | bytes 2752516
  6.5 54.7 %all-gather.3.cloned.1.call-start = ((), (), s32[]{:S(2)}) async-start(), calls=%async_computation.4 | async-start | bytes 1310720 | tf_op jit(solution)/shard_map/all_gather | solution.py:229
  7.3 1.5 copy-start.1
  8.8 1.2 copy-start.2
  10.0 1.0 copy-start.14
  11.0 1.0 copy-start.15
  12.1 0.7 copy-start.18
  12.7 23.8 %copy-start.20 = (s32[8,8]{1,0:T(8,128)S(1)}, s32[8,8]{1,0:T(8,128)}, u32[]{:S(2)}) copy-start(s32[8,8]{1,0:T(8,128)} %param.18) | copy-start | bytes 772
  12.7 24.2 %copy-start.21 = (bf16[8,224]{1,0:T(8,128)(2,1)S(1)}, bf16[8,224]{1,0:T(8,128)(2,1)}, u32[]{:S(2)}) copy-start(bf16[8,224]{1,0:T(8,128)(2,1)} %param.17) | copy-start | bytes 10756
  15.5 55.2 %copy-start.3 = (bf16[320,896]{1,0:T(8,128)(2,1)}, bf16[320,896]{1,0:T(8,128)(2,1)S(1)}, u32[]{:S(2)}) copy-start(bf16[320,896]{1,0:T(8,128)(2,1)S(1)} %get-tuple-element.15.refs_0_) | copy-start | bytes 1720324
  15.5 42.4 %collective-permute-start = (bf16[320,896]{1,0:T(8,128)(2,1)}, bf16[320,896]{1,0:T(8,128)(2,1)S(1)}, u32[]{:S(2)}, u32[]{:S(2)}) collective-permute-start(bf16[320,896]{1,0:T(8,128)(2,1)} %get-tuple-element.16), channel_id=1, source_target_pairs={{0,2},{1,3},{2,4},{3,5},{4,6},{5,7},{6,0},{7,1},{8,10},{9,11},{10,... | collective-permute-start | bytes 1720328 | tf_op jit(solution)/shard_map/ppermute | solution.py:232
  19.0 39.7 %collective-permute-start.1 = (bf16[320,896]{1,0:T(8,128)(2,1)}, bf16[320,896]{1,0:T(8,128)(2,1)S(1)}, u32[]{:S(2)}, u32[]{:S(2)}) collective-permute-start(bf16[320,896]{1,0:T(8,128)(2,1)} %get-tuple-element.17), channel_id=1, source_target_pairs={{0,4},{1,5},{2,6},{3,7},{4,0},{5,1},{6,2},{7,3},{8,12},{9,13},{10,... | collective-permute-start | bytes 1720328 | tf_op jit(solution)/shard_map/ppermute | solution.py:232
  34.5 25.1 %collective-permute-start.2 = (bf16[320,896]{1,0:T(8,128)(2,1)}, bf16[320,896]{1,0:T(8,128)(2,1)S(1)}, u32[]{:S(2)}, u32[]{:S(2)}) collective-permute-start(bf16[320,896]{1,0:T(8,128)(2,1)} %get-tuple-element.18), channel_id=1, source_target_pairs={{0,6},{1,7},{2,0},{3,1},{4,2},{5,3},{6,4},{7,5},{8,14},{9,15},{10,... | collective-permute-start | bytes 1720328 | tf_op jit(solution)/shard_map/ppermute | solution.py:232
  38.0 45.2 %all-to-all-start = ((bf16[64,2,224]{2,1,0:T(2,128)(2,1)}), bf16[64,2,224]{2,1,0:T(2,128)(2,1)S(1)}, u32[]{:S(2)}, u32[]{:S(2)}) async-start(bf16[64,2,224]{2,1,0:T(2,128)(2,1)} %reshape.58), calls=%async_computation | async-start | bytes 131072 | tf_op jit(solution)/shard_map/all_to_all | solution.py:253
  58.0 0.8 copy-start.5
  58.8 0.8 copy-start.8
  59.6 0.8 copy-start.11
  61.2 1.1 copy-start.6
  62.3 1.1 copy-start.9
  63.3 1.1 copy-start.12
  64.4 1.2 copy-start.19
  70.7 21.3 %collective-permute-start.3 = (bf16[8,64,896]{2,1,0:T(8,128)(2,1)}, bf16[8,64,896]{2,1,0:T(8,128)(2,1)}, u32[]{:S(2)}, u32[]{:S(2)}) collective-permute-start(bf16[8,64,896]{2,1,0:T(8,128)(2,1)} %get-tuple-element.20), channel_id=1, source_target_pairs={{0,1},{1,0},{2,3},{3,2},{4,5},{5,4},{6,7},{7,6},{8,9},{9,8},{10,11... | collective-permute-start | bytes 2752520 | tf_op jit(solution)/shard_map/ppermute | solution.py:279
  86.6 14.4 %all-to-all-start.1 = ((bf16[16,2,64,128]{3,2,1,0:T(8,128)(2,1)}), bf16[16,2,64,128]{3,2,1,0:T(8,128)(2,1)}, u32[]{:S(2)}, u32[]{:S(2)}) async-start(bf16[16,2,64,128]{3,2,1,0:T(8,128)(2,1)} %copy.22), calls=%async_computation.1 | async-start | bytes 1048576 | tf_op jit(solution)/shard_map/all_to_all | solution.py:267
  93.9 17.7 %collective-permute-start.4 = (bf16[4,64,896]{2,1,0:T(8,128)(2,1)}, bf16[4,64,896]{2,1,0:T(8,128)(2,1)S(1)}, u32[]{:S(2)}, u32[]{:S(2)}) collective-permute-start(bf16[4,64,896]{2,1,0:T(8,128)(2,1)} %add_convert_fusion), channel_id=1, source_target_pairs={{0,8},{1,9},{2,10},{3,11},{4,12},{5,13},{6,14},{7,15},{8,0},{9,1},... | collective-permute-start | bytes 1376264 | tf_op jit(solution)/shard_map/ppermute | solution.py:284
  102.8 26.6 %all-to-all-start.2 = ((bf16[16,64,128]{2,1,0:T(8,128)(2,1)}), bf16[16,64,128]{2,1,0:T(8,128)(2,1)S(1)}, u32[]{:S(2)}, u32[]{:S(2)}) async-start(bf16[16,64,128]{2,1,0:T(8,128)(2,1)} %broadcast_in_dim.8), calls=%async_computation.2 | async-start | bytes 524288 | tf_op jit(solution)/shard_map/all_to_all | solution.py:270
  111.6 1.1 copy-start.4
  112.7 1.1 copy-start.7
  113.8 1.1 copy-start.10
  114.8 1.1 copy-start.13
  115.9 65.1 %copy-start.22 = (f32[8,8]{1,0:T(8,128)S(1)}, f32[8,8]{1,0:T(8,128)}, u32[]{:S(2)}) copy-start(f32[8,8]{1,0:T(8,128)} %param.19) | copy-start | bytes 772
  119.7 0.7 copy-start.16
  120.4 9.1 %collective-permute-start.5 = (bf16[256,224]{1,0:T(8,128)(2,1)}, bf16[256,224]{1,0:T(8,128)(2,1)S(1)}, u32[]{:S(2)}, u32[]{:S(2)}) collective-permute-start(bf16[256,224]{1,0:T(8,128)(2,1)} %get-tuple-element.22), channel_id=1, source_target_pairs={{0,1},{1,0},{2,3},{3,2},{4,5},{5,4},{6,7},{7,6},{8,9},{9,8},{10,11... | collective-permute-start | bytes 344072 | tf_op jit(solution)/shard_map/ppermute | solution.py:288
  122.3 9.5 %collective-permute-start.6 = (bf16[256,224]{1,0:T(8,128)(2,1)}, bf16[256,224]{1,0:T(8,128)(2,1)S(1)}, u32[]{:S(2)}, u32[]{:S(2)}) collective-permute-start(bf16[256,224]{1,0:T(8,128)(2,1)} %get-tuple-element.23), channel_id=1, source_target_pairs={{0,8},{1,9},{2,10},{3,11},{4,12},{5,13},{6,14},{7,15},{8,0},{9,1},... | collective-permute-start | bytes 344072 | tf_op jit(solution)/shard_map/ppermute | solution.py:289
  126.0 9.2 %collective-permute-start.7 = (bf16[256,224]{1,0:T(8,128)(2,1)}, bf16[256,224]{1,0:T(8,128)(2,1)S(1)}, u32[]{:S(2)}, u32[]{:S(2)}) collective-permute-start(bf16[256,224]{1,0:T(8,128)(2,1)} %get-tuple-element.24), channel_id=1, source_target_pairs={{0,9},{1,8},{2,11},{3,10},{4,13},{5,12},{6,15},{7,14},{8,1},{9,0},... | collective-permute-start | bytes 344072 | tf_op jit(solution)/shard_map/ppermute | solution.py:290
  135.2 0.9 copy-start.17
  137.5 43.4 %all-to-all-start.3 = ((bf16[64,2,224]{2,1,0:T(2,128)(2,1)}), bf16[64,2,224]{2,1,0:T(2,128)(2,1)S(1)}, u32[]{:S(2)}, u32[]{:S(2)}) async-start(bf16[64,2,224]{2,1,0:T(2,128)(2,1)} %reshape.62), calls=%async_computation.3 | async-start | bytes 131072 | tf_op jit(solution)/shard_map/all_to_all | solution.py:294
Sparse Core Ops, SparseCore 0:
  10.0 51.1 all-gather.2

commit v2 on v0

v2 whole, which is shorter than its diff:
```python
import functools

import jax
import jax.numpy as jnp
from jax import lax
from jax.experimental import pallas as pl
from jax.experimental.pallas import tpu as pltpu
from jax.sharding import PartitionSpec as P

beta_one = 0.9
beta_two = 0.95
learn_rate = 0.1
weight_decay = 0.1
epsilon = 1e-08
bias_first = 1.0 - 0.9**20
bias_second = 1.0 - 0.95**20

HALVES, RING, CORES = 2, 4, 2
SMEM = pl.BlockSpec(memory_space=pltpu.SMEM)
VMEM = pl.BlockSpec(memory_space=pltpu.VMEM)
PARAMS = pltpu.CompilerParams(vmem_limit_bytes=62 * 2**20)


def cost(flops, size):
    return pl.CostEstimate(flops=flops, bytes_accessed=size, transcendentals=0)


def whole(*shape):
    return pl.BlockSpec(shape, lambda *_: (0,) * len(shape))


def contract_first(left, right):
    return lax.dot_general(
        left, right, (((0,), (0,)), ((), ())), preferred_element_type=jnp.float32
    )


def permutation(half_step, ring_step, core_step):
    pairs = []
    for half in range(HALVES):
        for ring in range(RING):
            for core in range(CORES):
                source = (half * RING + ring) * CORES + core
                target = (half ^ half_step) * RING + (ring + ring_step) % RING
                pairs.append((source, target * CORES + (core ^ core_step)))
    return pairs


def pack_kernel(place_ref, rows_ref, grad_ref, master_ref, first_ref, second_ref, *outs):
    table, columns = grad_ref.shape
    tokens = rows_ref.shape[1]
    rows = master_ref.shape[1]
    width = columns // (HALVES * RING * CORES)
    onehot = (
        (lax.broadcasted_iota(jnp.int32, (table, tokens), 0) == rows_ref[...])
        .astype(jnp.float32)
        .astype(jnp.bfloat16)
    )
    ring = place_ref[1]
    for here in range(RING):

        @pl.when(ring == here)
        def _(here=here):
            for step in range(RING):
                out = outs[step]
                for core in range(CORES):
                    for half in range(HALVES):
                        owner = (half * RING + (here + step) % RING) * CORES + core
                        take = pl.ds(owner * width, width)
                        put = pl.ds((core * HALVES + half) * width, width)
                        out[0:tokens, put] = contract_first(onehot, grad_ref[:, take]).astype(
                            jnp.bfloat16
                        )
                        at = tokens
                        out[at : at + rows, put] = master_ref[0, :, take].astype(jnp.bfloat16)
                        out[at + rows : at + 2 * rows, put] = first_ref[0, :, take]
                        out[at + 2 * rows : at + 3 * rows, put] = second_ref[0, :, take]


def pack(place, train_rows, out_grad, master, moment1, moment2):
    tokens = train_rows.shape[1]
    rows = master.shape[1]
    shape = (tokens + 3 * rows, out_grad.shape[1] // RING)
    return pl.pallas_call(
        pack_kernel,
        out_shape=[jax.ShapeDtypeStruct(shape, jnp.bfloat16)] * RING,
        in_specs=[SMEM] + [VMEM] * 5,
        out_specs=[VMEM] * RING,
        compiler_params=PARAMS,
        cost_estimate=cost(2 * tokens * out_grad.size, 7_000_000),
    )(place, train_rows, out_grad, master, moment1, moment2)


def split(flag, values):
    width = values.shape[-1] // 2
    low, high = values[..., :width], values[..., width:]
    return jnp.where(flag == 0, low, high), jnp.where(flag == 0, high, low)


def gradient_kernel(place_ref, acts_ref, *refs):
    parts, (ours_ref, theirs_ref) = refs[:RING], refs[RING:]
    ring, core = place_ref[1], place_ref[2]
    acts = [acts_ref[(ring - step + RING) % RING] for step in range(RING)]
    total = None
    for step in range(0, RING, 2):
        left = jnp.concatenate([acts[step], acts[step + 1]], axis=0)
        right = jnp.concatenate([parts[step][...], parts[step + 1][...]], axis=0)
        product = contract_first(left, right)
        total = product if total is None else total + product
    ours, theirs = split(core, total)
    ours_ref[...] = ours
    theirs_ref[...] = theirs.astype(jnp.bfloat16).reshape(theirs_ref.shape)


def gradients(place, acts, parts):
    ring_tokens, units = acts.shape
    tokens = ring_tokens // RING
    width = parts[0].shape[1]
    block = units // 8
    return pl.pallas_call(
        gradient_kernel,
        grid=(8,),
        out_shape=[
            jax.ShapeDtypeStruct((units, width // 2), jnp.float32),
            jax.ShapeDtypeStruct((16, block // 2, width // 2), jnp.bfloat16),
        ],
        in_specs=[SMEM, pl.BlockSpec((RING, tokens, block), lambda i: (0, 0, i))]
        + [whole(tokens, width)] * RING,
        out_specs=[
            pl.BlockSpec((block, width // 2), lambda i: (i, 0)),
            pl.BlockSpec((2, block // 2, width // 2), lambda i: (i, 0, 0)),
        ],
        compiler_params=PARAMS,
        cost_estimate=cost(2 * units * width * ring_tokens, 5_000_000),
    )(place, acts.reshape(RING, tokens, units), *parts)


def cross_kernel(place_ref, ours_ref, near_ref, kept_ref, cross_ref):
    kept, cross = split(place_ref[0], ours_ref[...] + near_ref[...].astype(jnp.float32))
    kept_ref[...] = kept
    cross_ref[...] = cross.astype(jnp.bfloat16).reshape(cross_ref.shape)


def add_cores(place, ours, near):
    units, width = ours.shape
    block = units // 4
    return pl.pallas_call(
        cross_kernel,
        grid=(4,),
        out_shape=[
            jax.ShapeDtypeStruct((units, width // 2), jnp.float32),
            jax.ShapeDtypeStruct((16, block // 4, width // 2), jnp.bfloat16),
        ],
        in_specs=[SMEM] + [pl.BlockSpec((block, width), lambda i: (i, 0))] * 2,
        out_specs=[
            pl.BlockSpec((block, width // 2), lambda i: (i, 0)),
            pl.BlockSpec((4, block // 4, width // 2), lambda i: (i, 0, 0)),
        ],
        compiler_params=PARAMS,
        cost_estimate=cost(2 * ours.size, 4_000_000),
    )(place, ours, near)


def state_core_kernel(tokens, place_ref, *refs):
    parts, out_ref = refs[:RING], refs[RING]
    ring, core = place_ref[1], place_ref[2]
    for step in range(RING):
        out_ref[(ring - step + RING) % RING] = split(core, parts[step][tokens:, :])[1]


def states_for_core(place, parts, tokens):
    rows, width = parts[0].shape
    return pl.pallas_call(
        functools.partial(state_core_kernel, tokens),
        out_shape=jax.ShapeDtypeStruct((RING, rows - tokens, width // 2), jnp.bfloat16),
        in_specs=[SMEM] + [VMEM] * RING,
        out_specs=VMEM,
        compiler_params=PARAMS,
        cost_estimate=cost(0, 3_000_000),
    )(place, *parts)


def state_half_kernel(tokens, place_ref, near_ref, *refs):
    parts, (kept_ref, cross_ref) = refs[:RING], refs[RING:]
    half, ring, core = place_ref[0], place_ref[1], place_ref[2]
    for step in range(RING):
        mine = split(core, parts[step][tokens:, :])[0]
        source = (ring - step + RING) % RING
        kept, cross = split(half, mine)
        kept_ref[0, source] = kept
        cross_ref[0, source] = cross
        kept, cross = split(half, near_ref[step])
        kept_ref[1, step] = kept
        cross_ref[1, step] = cross


def states_for_half(place, near, parts, tokens):
    rows, width = parts[0].shape
    shape = (CORES, RING, rows - tokens, width // 4)
    return pl.pallas_call(
        functools.partial(state_half_kernel, tokens),
        out_shape=[jax.ShapeDtypeStruct(shape, jnp.bfloat16)] * 2,
        in_specs=[SMEM] + [VMEM] * (1 + RING),
        out_specs=[VMEM] * 2,
        compiler_params=PARAMS,
        cost_estimate=cost(0, 4_500_000),
    )(place, near, *parts)


def adam_kernel(place_ref, kept_ref, far_ref, near_states_ref, far_states_ref, tile_ref):
    half, core = place_ref[0], place_ref[2]
    rows = near_states_ref.shape[2] // 3
    for half_step in range(HALVES):
        states = (near_states_ref, far_states_ref)[half_step]
        for core_step in range(CORES):
            for ring in range(RING):
                source = (
                    jnp.bitwise_xor(half, half_step) * RING + ring
                ) * CORES + jnp.bitwise_xor(core, core_step)
                at = pl.ds(pl.multiple_of(source * rows, rows), rows)
                gradient = kept_ref[at, :] + far_ref[at, :].astype(jnp.float32)
                state = states[core_step, ring].astype(jnp.float32)
                master, first_old, second_old = (
                    state[k * rows : (k + 1) * rows] for k in range(3)
                )
                first = beta_one * first_old + (1.0 - beta_one) * gradient
                second = beta_two * second_old + (1.0 - beta_two) * gradient * gradient
                update = first / bias_first / (jnp.sqrt(second / bias_second) + epsilon)
                tile_ref[at, :] = (
                    master * (1.0 - learn_rate * weight_decay) - learn_rate * update
                ).astype(jnp.bfloat16)


def adam_tile(place, kept, far, near_states, far_states):
    return pl.pallas_call(
        adam_kernel,
        out_shape=jax.ShapeDtypeStruct(kept.shape, jnp.bfloat16),
        in_specs=[SMEM] + [VMEM] * 4,
        out_specs=VMEM,
        compiler_params=PARAMS,
        cost_estimate=cost(20 * kept.size, 4_000_000),
    )(place, kept, far, near_states, far_states)


def turn_kernel(mixed_ref, out_ref):
    gates, slots, units = mixed_ref.shape
    width = out_ref.shape[2]
    for gate in range(gates):
        for pair in range(units // (2 * width)):
            turned = mixed_ref[gate, :, pair * 2 * width : (pair + 1) * 2 * width].T
            turned = turned.astype(jnp.bfloat16)
            out_ref[2 * pair, gate] = turned[:width]
            out_ref[2 * pair + 1, gate] = turned[width:]


def turn(mixed, shards):
    gates, slots, units = mixed.shape
    return pl.pallas_call(
        turn_kernel,
        out_shape=jax.ShapeDtypeStruct((shards, gates, units // shards, slots), jnp.bfloat16),
        in_specs=[VMEM],
        out_specs=VMEM,
        compiler_params=PARAMS,
        cost_estimate=cost(0, 1_500_000),
    )(mixed)


def hidden_kernel(shares_ref, out_ref):
    sums = jnp.sum(shares_ref[...].astype(jnp.float32), axis=0)
    hidden = (jax.nn.silu(sums[0]) * sums[1]).astype(jnp.bfloat16)
    for shard in range(out_ref.shape[0]):
        out_ref[shard] = hidden


def hidden_units(shares):
    shards, _, units, slots = shares.shape
    return pl.pallas_call(
        hidden_kernel,
        out_shape=jax.ShapeDtypeStruct((shards, units, slots), jnp.bfloat16),
        in_specs=[VMEM],
        out_specs=VMEM,
        compiler_params=PARAMS,
        cost_estimate=cost(shares.size, 800_000),
    )(shares)


def results_kernel(hidden_ref, tile_ref, out_ref):
    out_ref[...] = contract_first(hidden_ref[...], tile_ref[...]).astype(jnp.bfloat16)


def expert_results(hidden, tile):
    return pl.pallas_call(
        results_kernel,
        out_shape=jax.ShapeDtypeStruct((hidden.shape[1], tile.shape[1]), jnp.bfloat16),
        in_specs=[VMEM] * 2,
        out_specs=VMEM,
        compiler_params=PARAMS,
        cost_estimate=cost(2 * hidden.size * tile.shape[1], 800_000),
    )(hidden, tile)


def body(
    hidden_acts,
    train_rows,
    out_grad,
    master,
    moment1,
    moment2,
    gate_up,
    dec_tokens,
    route_ids,
    route_gates,
):
    index = lax.axis_index("dp")
    shards = lax.axis_size("dp")
    half, ring, core = index >> 3, (index >> 1) & (RING - 1), index & (CORES - 1)
    place = jnp.stack([half, ring, core]).astype(jnp.int32)
    token_count, width = dec_tokens.shape
    tokens = train_rows.shape[1]

    rings = [
        [(h * RING + r) * CORES + c for r in range(RING)]
        for h in range(HALVES)
        for c in range(CORES)
    ]
    acts = lax.all_gather(hidden_acts[0], "dp", axis=0, tiled=True, axis_index_groups=rings)
    sends = pack(place, train_rows, out_grad, master, moment1, moment2)
    parts = [sends[0]] + [
        lax.ppermute(sends[step], "dp", permutation(0, step, 0)) for step in range(1, RING)
    ]

    choices_per = route_ids.shape[1]
    expert_count = lax.axis_size("exp")
    capacity = min(token_count, max(2, 2 * choices_per * token_count // expert_count))
    slot_count = expert_count * capacity
    flat_ids = route_ids.reshape(-1)
    onehot = (flat_ids[:, None] == jnp.arange(expert_count, dtype=jnp.int32)[None, :]).astype(
        jnp.int32
    )
    earlier = jnp.cumsum(onehot, axis=0) - onehot
    position = jnp.sum(earlier * onehot, axis=1)
    slot_index = flat_ids * capacity + position
    placement = (slot_index[:, None] == jnp.arange(slot_count, dtype=jnp.int32)[None, :]).astype(
        jnp.bfloat16
    )
    repeated = jnp.repeat(dec_tokens, choices_per, axis=0)
    outgoing = jnp.einsum(
        "rs,rd->sd", placement, repeated, preferred_element_type=jnp.float32
    ).astype(jnp.bfloat16)
    arrived = lax.all_to_all(
        outgoing.reshape(expert_count, capacity, width),
        "exp",
        split_axis=0,
        concat_axis=0,
        tiled=True,
    )
    rows_in = arrived.reshape(slot_count, width)

    mixed = jnp.einsum(
        "dgf,sd->gsf", gate_up[0], rows_in, preferred_element_type=jnp.float32
    )
    shares = lax.all_to_all(
        turn(mixed, shards), "dp", split_axis=0, concat_axis=0, tiled=True
    )
    hidden = lax.all_to_all(
        hidden_units(shares), "dp", split_axis=0, concat_axis=0, tiled=True
    ).reshape(-1, slot_count)

    across_cores, across_halves = permutation(0, 0, 1), permutation(1, 0, 0)
    ours, theirs = gradients(place, acts, parts)
    near = lax.ppermute(theirs, "dp", across_cores).reshape(ours.shape)
    near_states = lax.ppermute(states_for_core(place, parts, tokens), "dp", across_cores)
    kept_states, cross_states = states_for_half(place, near_states, parts, tokens)
    far_states = lax.ppermute(cross_states, "dp", across_halves)
    kept, cross = add_cores(place, ours, near)
    far = lax.ppermute(cross, "dp", across_halves).reshape(kept.shape)
    tile = adam_tile(place, kept, far, kept_states, far_states)

    results = expert_results(hidden, tile)
    returned = lax.all_to_all(
        results.reshape(expert_count, capacity, width),
        "exp",
        split_axis=0,
        concat_axis=0,
        tiled=True,
    )
    back_rows = returned.reshape(slot_count, width)
    chosen = jnp.einsum("rs,sd->rd", placement, back_rows, preferred_element_type=jnp.float32)
    weighted = chosen.reshape(token_count, choices_per, width) * route_gates[:, :, None]
    return jnp.sum(weighted, axis=1).astype(jnp.bfloat16)


def solution(mesh):
    in_specs = (
        P("exp", "dp", None),
        P("exp", "dp"),
        P("dp", None),
        P("exp", "dp", None),
        P("exp", "dp", None),
        P("exp", "dp", None),
        P("exp", "dp", None, None),
        P("exp", "dp"),
        P("exp", None),
        P("exp", None),
    )
    out_specs = P("exp", "dp")
    return jax.shard_map(body, mesh=mesh, in_specs=in_specs, out_specs=out_specs, check_vma=False)
```

time: 388 us -> 194 us (0.50)
  waiting for transfers between devices: 251 us -> 49.6 us
  Pallas kernels: 0 us -> 34.7 us
  starting transfers between devices: 60.9 us -> 86.6 us
  blocking collectives: 22.3 us -> 0 us
  local copies, waits for them, and re-layouts: 22.8 us -> 4.87 us
  matrix products: 9.14 us -> 2.47 us
  other arithmetic: 7.15 us -> 1.01 us
    reduce_scatter x1 -> x0, waiting for transfers between devices: 111 us -> none  [body(): lax.psum_scatter(mixed.astype(jnp.bfloat16), 'dp', scatter_dimension=2, t...]
    unnamed x3 -> x1, waiting for transfers between devices: 93.2 us -> 0.71 us
    pallas_call x0 -> x9, Pallas kernels: none -> 34.7 us  [the longest x1 7.69 us: gradients(): pl.pallas_call(gradient_kernel, grid=(8,), out_shape=[jax.ShapeDtypeStruc...]
    ppermute x0 -> x7, starting transfers between devices: none -> 23.2 us  [the longest x3 11.5 us: body(): lax.ppermute(sends[step], 'dp', permutation(0, step, 0))]
    all_gather x1 -> x0, blocking collectives: 22.3 us -> none  [body(): hidden = lax.all_gather(partial_hidden, 'dp', axis=1, tiled=True)]
    unnamed x19 -> x16, local copies, waits for them, and re-layouts: 17.6 us -> 2.32 us
    all_to_all x3 -> x4, waiting for transfers between devices: 47.3 us -> 32.8 us  [the longest x1 25 us: body(): lax.all_to_all(results.reshape(expert_count, capacity, width), 'exp', spl...]
    ppermute x0 -> x7, waiting for transfers between devices: none -> 13.8 us  [the longest x1 11.1 us: body(): far = lax.ppermute(cross, 'dp', across_halves).reshape(kept.shape)]
  transfers between devices with their start and end apart: 5 -> 12, of which waited for: 4 -> 5; matrix products, arithmetic and copies ran while one was open for 5% -> 2% of each run, Pallas kernels for 0% -> 17%
where the time goes in v2:
time: 194 us; the launch traced here: 193 us
  starting transfers between devices  86.6 us (45%)
  waiting for transfers between devices  49.6 us (26%)
  Pallas kernels  34.7 us (18%)
  between operations  13.6 us (7%)
  local copies, waits for them, and re-layouts  4.87 us (3%)
  matrix products  2.47 us (1%)
    all_to_all x1, starting transfers between devices, body(): lax.all_to_all(outgoing.reshape(expert_count, capacity, width), 'exp', sp...  30 us
    all_to_all x1, waiting for transfers between devices, body(): lax.all_to_all(results.reshape(expert_count, capacity, width), 'exp', spl...  25 us
    all_to_all x1, starting transfers between devices, body(): lax.all_to_all(results.reshape(expert_count, capacity, width), 'exp', spl...  20.9 us
    ppermute x3, starting transfers between devices, body(): lax.ppermute(sends[step], 'dp', permutation(0, step, 0))  11.5 us
    ppermute x1, waiting for transfers between devices, body(): far = lax.ppermute(cross, 'dp', across_halves).reshape(kept.shape)  11.1 us
    all_to_all x1, waiting for transfers between devices, body(): lax.all_to_all(outgoing.reshape(expert_count, capacity, width), 'exp', sp...  7.8 us
    pallas_call x1, Pallas kernels, gradients(): pl.pallas_call(gradient_kernel, grid=(8,), out_shape=[jax.ShapeDtypeStruc...  7.69 us
    all_to_all x1, starting transfers between devices, body(): lax.all_to_all(hidden_units(shares), 'dp', split_axis=0, concat_axis=0, t...  7.23 us
  transfers between devices with their start and end apart: 12, of which 5 were waited for; matrix products, arithmetic and copies ran while one was open for 2% of the time, Pallas kernels for 17%

profile of v2, /device:TPU:4, one launch (start us, length us, event | category | flops | bytes accessed | tf_op | source)
XLA Modules:
  0.0 192.9 jit_solution(2560716269482287164)
XLA Ops:
  6.5 0.0 copy-start
  6.5 0.0 copy-start.5
  6.5 0.0 copy-start.6
  6.5 0.0 all-gather.3.cloned.1.call-start
  6.5 0.7 all-gather.3.cloned.1.call-update
  7.3 0.6 pad_add_fusion.place_ref
  7.9 6.2 %shard_map.102 = (bf16[320,896]{1,0:T(8,128)(2,1)}, bf16[320,896]{1,0:T(8,128)(2,1)}, bf16[320,896]{1,0:T(8,128)(2,1)}, bf16[320,896]{1,0:T(8,128)(2,1)}) custom-call(s32[3]{0:T(128)} %pad_add_fusion.place_ref, s32[1,128]{1,0:T(1,128)} %rows_ref.1, bf16[256,3584]{1,0:T(8,128)(2,1)} %grad_ref.1, f32[1,64,3584]{2,1,0:T(8,128)} %master_ref.1, ...), custom_call_target="tpu_custom_call" | custom-call | flops 234881024 | bytes 7000000 | tf_op jit(solution)/shard_map/pallas_call | solution.py:84
  14.1 3.9 %collective-permute-start = (bf16[320,896]{1,0:T(8,128)(2,1)}, bf16[320,896]{1,0:T(8,128)(2,1)S(1)}, u32[]{:S(2)}, u32[]{:S(2)}) collective-permute-start(bf16[320,896]{1,0:T(8,128)(2,1)} %get-tuple-element.16), channel_id=1, source_target_pairs={{0,2},{1,3},{2,4},{3,5},{4,6},{5,7},{6,0},{7,1},{8,10},{9,11},{10,... | collective-permute-start | bytes 1720328 | tf_op jit(solution)/shard_map/ppermute | solution.py:329
  18.0 4.8 %collective-permute-start.1 = (bf16[320,896]{1,0:T(8,128)(2,1)}, bf16[320,896]{1,0:T(8,128)(2,1)}, u32[]{:S(2)}, u32[]{:S(2)}) collective-permute-start(bf16[320,896]{1,0:T(8,128)(2,1)} %get-tuple-element.17), channel_id=1, source_target_pairs={{0,4},{1,5},{2,6},{3,7},{4,0},{5,1},{6,2},{7,3},{8,12},{9,13},{10,... | collective-permute-start | bytes 1720328 | tf_op jit(solution)/shard_map/ppermute | solution.py:329
  22.8 2.8 %collective-permute-start.2 = (bf16[320,896]{1,0:T(8,128)(2,1)}, bf16[320,896]{1,0:T(8,128)(2,1)}, u32[]{:S(2)}, u32[]{:S(2)}) collective-permute-start(bf16[320,896]{1,0:T(8,128)(2,1)} %get-tuple-element.18), channel_id=1, source_target_pairs={{0,6},{1,7},{2,0},{3,1},{4,2},{5,3},{6,4},{7,5},{8,14},{9,15},{10,... | collective-permute-start | bytes 1720328 | tf_op jit(solution)/shard_map/ppermute | solution.py:329
  25.7 0.0 copy-done.5
  25.7 0.1 eq.50
  25.7 0.1 fusion.5
  25.8 0.1 reduce_window_sum.11
  25.9 0.2 select_reduce_fusion
  26.1 0.0 copy-done.6
  26.1 0.2 convolution_convert_fusion
  26.4 0.1 copy.13
  26.5 0.7 reshape.64
  27.1 30.0 %all-to-all-start = ((bf16[64,2,224]{2,1,0:T(2,128)(2,1)}), bf16[64,2,224]{2,1,0:T(2,128)(2,1)S(1)}, u32[]{:S(2)}, u32[]{:S(2)}) async-start(bf16[64,2,224]{2,1,0:T(2,128)(2,1)} %reshape.64), calls=%async_computation | async-start | bytes 131072 | tf_op jit(solution)/shard_map/all_to_all | solution.py:350
  57.1 0.0 collective-permute-done.refs_1_
  57.1 0.0 copy-start.1
  57.2 0.0 collective-permute-done.1.refs_2_
  57.2 0.0 collective-permute-done.2.refs_3_
  57.2 2.3 %all-gather.3.cloned.1.call-done = bf16[1,512,1024]{2,1,0:T(8,128)(2,1)} async-done(((bf16[1,128,1024]{2,1,0:T(8,128)(2,1)}), bf16[1,512,1024]{2,1,0:T(8,128)(2,1)}) %all-gather.3.cloned.1.call-update) | async-done | bytes 1048592 | tf_op jit(solution)/shard_map/all_gather | solution.py:326
  59.5 0.0 copy-done.1
  59.5 7.7 %shard_map.103 = (f32[1024,448]{1,0:T(8,128)}, bf16[16,64,448]{2,1,0:T(8,128)(2,1)}) custom-call(s32[3]{0:T(128)} %pad_add_fusion.place_ref, bf16[4,128,1024]{2,1,0:T(8,128)(2,1)} %bitcast.25, bf16[320,896]{1,0:T(8,128)(2,1)} %get-tuple-element.15.refs_0_, bf16[320,896]{1,0:T(8,128)(2,1)} %copy-done.1, bf16[320,896]{1,0:T(8,128)(2,1)} %collective-permute-done.1.refs_2_, ...), custom_call_target="tpu_custom_call" | custom-call | flops 939524096 | bytes 5000000 | tf_op jit(solution)/shard_map/pallas_call | solution.py:120
  67.2 1.9 collective-permute-start.3
  69.1 2.8 %shard_map.105 = bf16[4,192,448]{2,1,0:T(8,128)(2,1)} custom-call(s32[3]{0:T(128)} %pad_add_fusion.place_ref, bf16[320,896]{1,0:T(8,128)(2,1)} %get-tuple-element.15.refs_0_, bf16[320,896]{1,0:T(8,128)(2,1)} %copy-done.1, bf16[320,896]{1,0:T(8,128)(2,1)} %collective-permute-done.1.refs_2_, bf16[320,896]{1,0:T(8,128)(2,1)} %collective-permute-done.2.refs_3_), custom_call_target="tpu_custom_call" | custom-call | bytes 3000000 | tf_op jit(solution)/shard_map/pallas_call | solution.py:173
  71.9 2.4 %collective-permute-start.5 = (bf16[4,192,448]{2,1,0:T(8,128)(2,1)}, bf16[4,192,448]{2,1,0:T(8,128)(2,1)}, u32[]{:S(2)}, u32[]{:S(2)}) collective-permute-start(bf16[4,192,448]{2,1,0:T(8,128)(2,1)} %shard_map.105), channel_id=1, source_target_pairs={{0,1},{1,0},{2,3},{3,2},{4,5},{5,4},{6,7},{7,6},{8,9},{9,8},{10,11... | collective-permute-start | bytes 2064392 | tf_op jit(solution)/shard_map/ppermute | solution.py:372
  74.3 7.8 %all-to-all-done = bf16[64,2,224]{2,1,0:T(2,128)(2,1)S(1)} async-done(((bf16[64,2,224]{2,1,0:T(2,128)(2,1)}), bf16[64,2,224]{2,1,0:T(2,128)(2,1)S(1)}, u32[]{:S(2)}, u32[]{:S(2)}) %all-to-all-start) | async-done | bytes 57376 | tf_op jit(solution)/shard_map/all_to_all | solution.py:350
  82.1 0.1 reshape.65
  82.2 0.0 copy-done
  82.2 1.4 convolution_bitcast_fusion.mixed_ref
  83.6 2.2 %shard_map.100 = bf16[16,2,64,128]{3,2,1,0:T(8,128)(2,1)} custom-call(f32[2,128,1024]{2,1,0:T(8,128)} %convolution_bitcast_fusion.mixed_ref), custom_call_target="tpu_custom_call" | custom-call | bytes 1500000 | tf_op jit(solution)/shard_map/pallas_call | solution.py:258
  85.8 5.4 %all-to-all-start.1 = ((bf16[16,2,64,128]{3,2,1,0:T(8,128)(2,1)}), bf16[16,2,64,128]{3,2,1,0:T(8,128)(2,1)S(1)}, u32[]{:S(2)}, u32[]{:S(2)}) async-start(bf16[16,2,64,128]{3,2,1,0:T(8,128)(2,1)} %shard_map.100), calls=%async_computation.1 | async-start | bytes 1048576 | tf_op jit(solution)/shard_map/all_to_all | solution.py:362
  91.2 0.0 collective-permute-done.5.near_ref
  91.2 3.9 %shard_map.106 = (bf16[2,4,192,224]{3,2,1,0:T(8,128)(2,1)}, bf16[2,4,192,224]{3,2,1,0:T(8,128)(2,1)}) custom-call(s32[3]{0:T(128)} %pad_add_fusion.place_ref, bf16[4,192,448]{2,1,0:T(8,128)(2,1)} %collective-permute-done.5.near_ref, bf16[320,896]{1,0:T(8,128)(2,1)} %get-tuple-element.15.refs_0_, bf16[320,896]{1,0:T(8,128)(2,1)} %copy-done.1, ...), custom_call_target="tpu_custom_call" | custom-call | bytes 4500000 | tf_op jit(solution)/shard_map/pallas_call | solution.py:200
  95.1 2.0 %collective-permute-start.6 = (bf16[2,4,192,224]{3,2,1,0:T(8,128)(2,1)}, bf16[2,4,192,224]{3,2,1,0:T(8,128)(2,1)}, u32[]{:S(2)}, u32[]{:S(2)}) collective-permute-start(bf16[2,4,192,224]{3,2,1,0:T(8,128)(2,1)} %get-tuple-element.24), channel_id=1, source_target_pairs={{0,8},{1,9},{2,10},{3,11},{4,12},{5,13},{6,14},{7,15},{8,0},{9,1},... | collective-permute-start | bytes 2064392 | tf_op jit(solution)/shard_map/ppermute | solution.py:374
  97.1 0.0 collective-permute-done.3
  97.1 4.2 %shard_map.104 = (f32[1024,224]{1,0:T(8,128)}, bf16[16,64,224]{2,1,0:T(8,128)(2,1)}) custom-call(s32[3]{0:T(128)} %pad_add_fusion.place_ref, f32[1024,448]{1,0:T(8,128)} %get-tuple-element.19.ours_ref, bf16[1024,448]{1,0:T(8,128)(2,1)} %bitcast.10.near_ref), custom_call_target="tpu_custom_call" | custom-call | flops 917504 | bytes 4000000 | tf_op jit(solution)/shard_map/pallas_call | solution.py:147
  101.3 5.3 %collective-permute-start.4 = (bf16[16,64,224]{2,1,0:T(8,128)(2,1)}, bf16[16,64,224]{2,1,0:T(8,128)(2,1)S(1)}, u32[]{:S(2)}, u32[]{:S(2)}) collective-permute-start(bf16[16,64,224]{2,1,0:T(8,128)(2,1)} %get-tuple-element.22), channel_id=1, source_target_pairs={{0,8},{1,9},{2,10},{3,11},{4,12},{5,13},{6,14},{7,15},{8,0},{9,1},... | collective-permute-start | bytes 1376264 | tf_op jit(solution)/shard_map/ppermute | solution.py:376
  106.7 0.0 all-to-all-done.1.shares_ref
  106.7 0.0 copy-start.2
  106.7 0.8 copy-done.2
  107.5 1.8 shard_map.101
  109.3 7.2 %all-to-all-start.2 = ((bf16[16,64,128]{2,1,0:T(8,128)(2,1)}), bf16[16,64,128]{2,1,0:T(8,128)(2,1)S(1)}, u32[]{:S(2)}, u32[]{:S(2)}) async-start(bf16[16,64,128]{2,1,0:T(8,128)(2,1)} %shard_map.101), calls=%async_computation.2 | async-start | bytes 524288 | tf_op jit(solution)/shard_map/all_to_all | solution.py:365
  116.6 2.6 %collective-permute-done.6.far_states_ref = bf16[2,4,192,224]{3,2,1,0:T(8,128)(2,1)} collective-permute-done((bf16[2,4,192,224]{3,2,1,0:T(8,128)(2,1)}, bf16[2,4,192,224]{3,2,1,0:T(8,128)(2,1)}, u32[]{:S(2)}, u32[]{:S(2)}) %collective-permute-start.6) | collective-permute-done | bytes 688160 | tf_op jit(solution)/shard_map/ppermute | solution.py:374
  119.2 11.1 %collective-permute-done.4 = bf16[16,64,224]{2,1,0:T(8,128)(2,1)S(1)} collective-permute-done((bf16[16,64,224]{2,1,0:T(8,128)(2,1)}, bf16[16,64,224]{2,1,0:T(8,128)(2,1)S(1)}, u32[]{:S(2)}, u32[]{:S(2)}) %collective-permute-start.4) | collective-permute-done | bytes 458784 | tf_op jit(solution)/shard_map/ppermute | solution.py:376
  130.3 0.0 copy-start.4
  130.3 0.8 copy-done.4
  131.1 0.0 copy-start.7
  131.1 3.8 %shard_map.107.tile_ref = bf16[1024,224]{1,0:T(8,128)(2,1)} custom-call(s32[3]{0:T(128)} %pad_add_fusion.place_ref, f32[1024,224]{1,0:T(8,128)} %get-tuple-element.21.kept_ref, bf16[1024,224]{1,0:T(8,128)(2,1)} %bitcast.24, bf16[2,4,192,224]{3,2,1,0:T(8,128)(2,1)} %get-tuple-element.23.near_states_ref, ...), custom_call_target="tpu_custom_call" | custom-call | flops 4587520 | bytes 4000000 | tf_op jit(solution)/shard_map/pallas_call | solution.py:235
  134.9 0.0 all-to-all-done.2
  134.9 0.0 copy-start.3
  134.9 0.7 copy-done.3
  135.6 2.0 %shard_map.108 = bf16[128,224]{1,0:T(8,128)(2,1)} custom-call(bf16[1024,128]{1,0:T(8,128)(2,1)} %bitcast.23, bf16[1024,224]{1,0:T(8,128)(2,1)} %shard_map.107.tile_ref), custom_call_target="tpu_custom_call" | custom-call | flops 58720256 | bytes 800000 | tf_op jit(solution)/shard_map/pallas_call | solution.py:292
  137.6 1.5 reshape.70
  139.1 20.9 %all-to-all-start.3 = ((bf16[64,2,224]{2,1,0:T(2,128)(2,1)}), bf16[64,2,224]{2,1,0:T(2,128)(2,1)S(1)}, u32[]{:S(2)}, u32[]{:S(2)}) async-start(bf16[64,2,224]{2,1,0:T(2,128)(2,1)} %reshape.70), calls=%async_computation.3 | async-start | bytes 131072 | tf_op jit(solution)/shard_map/all_to_all | solution.py:380
  160.1 0.1 reduce_sum.21
  160.1 25.0 %all-to-all-done.3 = bf16[64,2,224]{2,1,0:T(2,128)(2,1)S(1)} async-done(((bf16[64,2,224]{2,1,0:T(2,128)(2,1)}), bf16[64,2,224]{2,1,0:T(2,128)(2,1)S(1)}, u32[]{:S(2)}, u32[]{:S(2)}) %all-to-all-start.3) | async-done | bytes 57376 | tf_op jit(solution)/shard_map/all_to_all | solution.py:380
  185.1 0.1 reshape.71
  185.2 0.0 copy-done.7
  185.2 0.8 fusion
  (2 shorter events, 0.0 us)
Async XLA Ops:
  6.5 75.7 %copy-start = (bf16[1,224,2,1024]{3,2,1,0:T(2,128)(2,1)S(1)}, bf16[1,224,2,1024]{3,2,1,0:T(2,128)(2,1)}, u32[]{:S(2)}) copy-start(bf16[1,224,2,1024]{3,2,1,0:T(2,128)(2,1)} %param.16) | copy-start | bytes 2752516
  6.5 19.1 %copy-start.5 = (s32[8,8]{1,0:T(8,128)S(1)}, s32[8,8]{1,0:T(8,128)}, u32[]{:S(2)}) copy-start(s32[8,8]{1,0:T(8,128)} %param.18) | copy-start | bytes 772
  6.5 19.6 %copy-start.6 = (bf16[8,224]{1,0:T(8,128)(2,1)S(1)}, bf16[8,224]{1,0:T(8,128)(2,1)}, u32[]{:S(2)}) copy-start(bf16[8,224]{1,0:T(8,128)(2,1)} %param.17) | copy-start | bytes 10756
  6.5 52.9 %all-gather.3.cloned.1.call-start = ((), (), s32[]{:S(2)}) async-start(), calls=%async_computation.4 | async-start | bytes 1310720 | tf_op jit(solution)/shard_map/all_gather | solution.py:326
  14.1 43.0 %collective-permute-start = (bf16[320,896]{1,0:T(8,128)(2,1)}, bf16[320,896]{1,0:T(8,128)(2,1)S(1)}, u32[]{:S(2)}, u32[]{:S(2)}) collective-permute-start(bf16[320,896]{1,0:T(8,128)(2,1)} %get-tuple-element.16), channel_id=1, source_target_pairs={{0,2},{1,3},{2,4},{3,5},{4,6},{5,7},{6,0},{7,1},{8,10},{9,11},{10,... | collective-permute-start | bytes 1720328 | tf_op jit(solution)/shard_map/ppermute | solution.py:329
  18.0 39.1 %collective-permute-start.1 = (bf16[320,896]{1,0:T(8,128)(2,1)}, bf16[320,896]{1,0:T(8,128)(2,1)}, u32[]{:S(2)}, u32[]{:S(2)}) collective-permute-start(bf16[320,896]{1,0:T(8,128)(2,1)} %get-tuple-element.17), channel_id=1, source_target_pairs={{0,4},{1,5},{2,6},{3,7},{4,0},{5,1},{6,2},{7,3},{8,12},{9,13},{10,... | collective-permute-start | bytes 1720328 | tf_op jit(solution)/shard_map/ppermute | solution.py:329
  22.8 34.3 %collective-permute-start.2 = (bf16[320,896]{1,0:T(8,128)(2,1)}, bf16[320,896]{1,0:T(8,128)(2,1)}, u32[]{:S(2)}, u32[]{:S(2)}) collective-permute-start(bf16[320,896]{1,0:T(8,128)(2,1)} %get-tuple-element.18), channel_id=1, source_target_pairs={{0,6},{1,7},{2,0},{3,1},{4,2},{5,3},{6,4},{7,5},{8,14},{9,15},{10,... | collective-permute-start | bytes 1720328 | tf_op jit(solution)/shard_map/ppermute | solution.py:329
  27.1 55.0 %all-to-all-start = ((bf16[64,2,224]{2,1,0:T(2,128)(2,1)}), bf16[64,2,224]{2,1,0:T(2,128)(2,1)S(1)}, u32[]{:S(2)}, u32[]{:S(2)}) async-start(bf16[64,2,224]{2,1,0:T(2,128)(2,1)} %reshape.64), calls=%async_computation | async-start | bytes 131072 | tf_op jit(solution)/shard_map/all_to_all | solution.py:350
  57.1 2.3 %copy-start.1 = (bf16[320,896]{1,0:T(8,128)(2,1)}, bf16[320,896]{1,0:T(8,128)(2,1)S(1)}, u32[]{:S(2)}) copy-start(bf16[320,896]{1,0:T(8,128)(2,1)S(1)} %collective-permute-done.refs_1_) | copy-start | bytes 1720324
  67.2 29.9 %collective-permute-start.3 = (bf16[16,64,448]{2,1,0:T(8,128)(2,1)}, bf16[16,64,448]{2,1,0:T(8,128)(2,1)}, u32[]{:S(2)}, u32[]{:S(2)}) collective-permute-start(bf16[16,64,448]{2,1,0:T(8,128)(2,1)} %get-tuple-element.20), channel_id=1, source_target_pairs={{0,1},{1,0},{2,3},{3,2},{4,5},{5,4},{6,7},{7,6},{8,9},{9,8},{10,11... | collective-permute-start | bytes 2752520 | tf_op jit(solution)/shard_map/ppermute | solution.py:371
  71.9 19.3 %collective-permute-start.5 = (bf16[4,192,448]{2,1,0:T(8,128)(2,1)}, bf16[4,192,448]{2,1,0:T(8,128)(2,1)}, u32[]{:S(2)}, u32[]{:S(2)}) collective-permute-start(bf16[4,192,448]{2,1,0:T(8,128)(2,1)} %shard_map.105), channel_id=1, source_target_pairs={{0,1},{1,0},{2,3},{3,2},{4,5},{5,4},{6,7},{7,6},{8,9},{9,8},{10,11... | collective-permute-start | bytes 2064392 | tf_op jit(solution)/shard_map/ppermute | solution.py:372
  85.8 20.8 %all-to-all-start.1 = ((bf16[16,2,64,128]{3,2,1,0:T(8,128)(2,1)}), bf16[16,2,64,128]{3,2,1,0:T(8,128)(2,1)S(1)}, u32[]{:S(2)}, u32[]{:S(2)}) async-start(bf16[16,2,64,128]{3,2,1,0:T(8,128)(2,1)} %shard_map.100), calls=%async_computation.1 | async-start | bytes 1048576 | tf_op jit(solution)/shard_map/all_to_all | solution.py:362
  95.1 24.1 %collective-permute-start.6 = (bf16[2,4,192,224]{3,2,1,0:T(8,128)(2,1)}, bf16[2,4,192,224]{3,2,1,0:T(8,128)(2,1)}, u32[]{:S(2)}, u32[]{:S(2)}) collective-permute-start(bf16[2,4,192,224]{3,2,1,0:T(8,128)(2,1)} %get-tuple-element.24), channel_id=1, source_target_pairs={{0,8},{1,9},{2,10},{3,11},{4,12},{5,13},{6,14},{7,15},{8,0},{9,1},... | collective-permute-start | bytes 2064392 | tf_op jit(solution)/shard_map/ppermute | solution.py:374
  101.3 29.0 %collective-permute-start.4 = (bf16[16,64,224]{2,1,0:T(8,128)(2,1)}, bf16[16,64,224]{2,1,0:T(8,128)(2,1)S(1)}, u32[]{:S(2)}, u32[]{:S(2)}) collective-permute-start(bf16[16,64,224]{2,1,0:T(8,128)(2,1)} %get-tuple-element.22), channel_id=1, source_target_pairs={{0,8},{1,9},{2,10},{3,11},{4,12},{5,13},{6,14},{7,15},{8,0},{9,1},... | collective-permute-start | bytes 1376264 | tf_op jit(solution)/shard_map/ppermute | solution.py:376
  106.7 0.8 copy-start.2
  109.3 25.6 %all-to-all-start.2 = ((bf16[16,64,128]{2,1,0:T(8,128)(2,1)}), bf16[16,64,128]{2,1,0:T(8,128)(2,1)S(1)}, u32[]{:S(2)}, u32[]{:S(2)}) async-start(bf16[16,64,128]{2,1,0:T(8,128)(2,1)} %shard_map.101), calls=%async_computation.2 | async-start | bytes 524288 | tf_op jit(solution)/shard_map/all_to_all | solution.py:365
  130.3 0.8 copy-start.4
  131.1 54.1 %copy-start.7 = (f32[8,8]{1,0:T(8,128)S(1)}, f32[8,8]{1,0:T(8,128)}, u32[]{:S(2)}) copy-start(f32[8,8]{1,0:T(8,128)} %param.19) | copy-start | bytes 772
  134.9 0.7 copy-start.3
  139.1 46.0 %all-to-all-start.3 = ((bf16[64,2,224]{2,1,0:T(2,128)(2,1)}), bf16[64,2,224]{2,1,0:T(2,128)(2,1)S(1)}, u32[]{:S(2)}, u32[]{:S(2)}) async-start(bf16[64,2,224]{2,1,0:T(2,128)(2,1)} %reshape.70), calls=%async_computation.3 | async-start | bytes 131072 | tf_op jit(solution)/shard_map/all_to_all | solution.py:380
Sparse Core Ops, SparseCore 0:
  10.0 49.3 all-gather.2

commit v3 on v0

v3 whole, which is shorter than its diff:
```python
import functools

import jax
import jax.numpy as jnp
from jax import lax
from jax.experimental import pallas as pl
from jax.experimental.pallas import tpu as pltpu
from jax.sharding import PartitionSpec as P

beta_one = 0.9
beta_two = 0.95
learn_rate = 0.1
weight_decay = 0.1
epsilon = 1e-08
bias_first = 1.0 - 0.9**20
bias_second = 1.0 - 0.95**20

HALVES, RING, CORES = 2, 4, 2
PIECES = 4
SMEM = pl.BlockSpec(memory_space=pltpu.SMEM)
VMEM = pl.BlockSpec(memory_space=pltpu.VMEM)
PARAMS = pltpu.CompilerParams(vmem_limit_bytes=62 * 2**20)
SMALL = pltpu.CompilerParams(vmem_limit_bytes=24 * 2**20)


def cost(flops, size):
    return pl.CostEstimate(flops=flops, bytes_accessed=size, transcendentals=0)


def whole(*shape):
    return pl.BlockSpec(shape, lambda *_: (0,) * len(shape))


def contract_first(left, right):
    return lax.dot_general(
        left, right, (((0,), (0,)), ((), ())), preferred_element_type=jnp.float32
    )


def permutation(half_step, ring_step, core_step):
    pairs = []
    for half in range(HALVES):
        for ring in range(RING):
            for core in range(CORES):
                source = (half * RING + ring) * CORES + core
                target = (half ^ half_step) * RING + (ring + ring_step) % RING
                pairs.append((source, target * CORES + (core ^ core_step)))
    return pairs


def pack_kernel(place_ref, rows_ref, grad_ref, master_ref, first_ref, second_ref, *outs):
    table, columns = grad_ref.shape
    tokens = rows_ref.shape[1]
    rows = master_ref.shape[1]
    owners = HALVES * RING * CORES // PIECES
    width = columns // owners
    onehot = (
        (lax.broadcasted_iota(jnp.int32, (table, tokens), 0) == rows_ref[...])
        .astype(jnp.float32)
        .astype(jnp.bfloat16)
    )
    ring = place_ref[1]
    for here in range(RING):
        for piece in range(PIECES):

            @pl.when((ring == here) & (pl.program_id(0) == piece))
            def _(here=here, piece=piece):
                for local in range(owners):
                    owner = piece * owners + local
                    half, place = owner // (RING * CORES), owner // CORES % RING
                    out = outs[(place - here) % RING]
                    take = pl.ds(local * width, width)
                    put = pl.ds((owner % CORES * HALVES + half) * width, width)
                    out[0:tokens, put] = contract_first(onehot, grad_ref[:, take]).astype(
                        jnp.bfloat16
                    )
                    at = tokens
                    out[at : at + rows, put] = master_ref[0, :, take].astype(jnp.bfloat16)
                    out[at + rows : at + 2 * rows, put] = first_ref[0, :, take]
                    out[at + 2 * rows : at + 3 * rows, put] = second_ref[0, :, take]


def pack(place, train_rows, out_grad, master, moment1, moment2):
    tokens = train_rows.shape[1]
    rows = master.shape[1]
    table, columns = out_grad.shape
    shape = (tokens + 3 * rows, columns // RING)
    state = pl.BlockSpec((1, rows, columns // PIECES), lambda i: (0, 0, i))
    return pl.pallas_call(
        pack_kernel,
        grid=(PIECES,),
        out_shape=[jax.ShapeDtypeStruct(shape, jnp.bfloat16)] * RING,
        in_specs=[
            SMEM,
            whole(1, tokens),
            pl.BlockSpec((table, columns // PIECES), lambda i: (0, i)),
            state,
            state,
            state,
        ],
        out_specs=[whole(*shape)] * RING,
        compiler_params=PARAMS,
        cost_estimate=cost(2 * tokens * out_grad.size, 7_000_000),
    )(place, train_rows, out_grad, master, moment1, moment2)


def split(flag, values):
    width = values.shape[-1] // 2
    low, high = values[..., :width], values[..., width:]
    return jnp.where(flag == 0, low, high), jnp.where(flag == 0, high, low)


def core_kernel(place_ref, *refs):
    parts, (mine_ref, theirs_ref) = refs[:RING], refs[RING:]
    ring, core = place_ref[1], place_ref[2]
    for step in range(RING):
        mine, theirs = split(core, parts[step][...])
        source = (ring - step + RING) % RING
        mine_ref[source] = mine
        theirs_ref[source] = theirs


def split_cores(place, parts):
    rows, width = parts[0].shape
    block = 64
    return pl.pallas_call(
        core_kernel,
        grid=(rows // block,),
        out_shape=[jax.ShapeDtypeStruct((RING, rows, width // 2), jnp.bfloat16)] * 2,
        in_specs=[SMEM] + [pl.BlockSpec((block, width), lambda i: (i, 0))] * RING,
        out_specs=[pl.BlockSpec((RING, block, width // 2), lambda i: (0, i, 0))] * 2,
        compiler_params=PARAMS,
        cost_estimate=cost(0, 5_000_000),
    )(place, *parts)


def gradient_kernel(place_ref, acts_ref, mine_ref, near_ref, out_ref):
    core = place_ref[2]
    total = None
    for ring in range(RING):
        left = jnp.concatenate(
            [acts_ref[ring * CORES + core], acts_ref[ring * CORES + 1 - core]], axis=0
        )
        right = jnp.concatenate([mine_ref[ring], near_ref[ring]], axis=0)
        product = contract_first(left, right)
        total = product if total is None else total + product
    out_ref[...] = total.astype(out_ref.dtype).reshape(out_ref.shape)


def gradient_rows(place, acts, mine, near, tokens, other_half, dtype):
    group_tokens, units = acts.shape
    sources = RING * CORES
    blocks = 2
    block = units // HALVES // blocks
    width = mine.shape[2]
    rows = units // HALVES // sources
    operand = pl.BlockSpec((RING, tokens, width), lambda i, place: (0, 0, 0))
    return pl.pallas_call(
        gradient_kernel,
        out_shape=jax.ShapeDtypeStruct((sources, rows, width), dtype),
        grid_spec=pltpu.PrefetchScalarGridSpec(
            num_scalar_prefetch=1,
            grid=(blocks,),
            in_specs=[
                pl.BlockSpec(
                    (sources, tokens, block),
                    lambda i, place: (
                        0,
                        0,
                        jnp.bitwise_xor(place[0], other_half) * blocks + i,
                    ),
                ),
                operand,
                operand,
            ],
            out_specs=pl.BlockSpec(
                (sources // blocks, rows, width), lambda i, place: (i, 0, 0)
            ),
        ),
        compiler_params=PARAMS,
        cost_estimate=cost(2 * block * blocks * width * group_tokens, 4_000_000),
    )(place, acts.reshape(sources, tokens, units), mine, near)


def adam_kernel(tokens, place_ref, kept_ref, far_ref, mine_ref, near_ref, tile_ref):
    rows = kept_ref.shape[1]
    for step, states in enumerate((mine_ref, near_ref)):
        core = jnp.bitwise_xor(place_ref[2], step)
        gradient = kept_ref[core] + far_ref[core].astype(jnp.float32)
        master, first_old, second_old = (
            states[0, tokens + k * rows : tokens + (k + 1) * rows, :].astype(jnp.float32)
            for k in range(3)
        )
        first = beta_one * first_old + (1.0 - beta_one) * gradient
        second = beta_two * second_old + (1.0 - beta_two) * gradient * gradient
        update = first / bias_first / (jnp.sqrt(second / bias_second) + epsilon)
        tile_ref[core] = (
            master * (1.0 - learn_rate * weight_decay) - learn_rate * update
        ).astype(jnp.bfloat16)


def adam_tile(tokens, place, kept, far, mine, near):
    sources, rows, width = kept.shape
    pair = pl.BlockSpec((CORES, rows, width), lambda i: (i, 0, 0))
    states = pl.BlockSpec((1, mine.shape[1], width), lambda i: (i, 0, 0))
    return pl.pallas_call(
        functools.partial(adam_kernel, tokens),
        grid=(RING,),
        out_shape=jax.ShapeDtypeStruct(kept.shape, jnp.bfloat16),
        in_specs=[SMEM, pair, pair, states, states],
        out_specs=pair,
        compiler_params=PARAMS,
        cost_estimate=cost(20 * kept.size, 5_000_000),
    )(place, kept, far, mine, near)


def turn_kernel(mixed_ref, out_ref):
    gates, slots, units = mixed_ref.shape
    width = out_ref.shape[2]
    for gate in range(gates):
        for pair in range(units // (2 * width)):
            turned = mixed_ref[gate, :, pair * 2 * width : (pair + 1) * 2 * width].T
            turned = turned.astype(jnp.bfloat16)
            out_ref[2 * pair, gate] = turned[:width]
            out_ref[2 * pair + 1, gate] = turned[width:]


def turn(mixed, shards):
    gates, slots, units = mixed.shape
    return pl.pallas_call(
        turn_kernel,
        out_shape=jax.ShapeDtypeStruct((shards, gates, units // shards, slots), jnp.bfloat16),
        in_specs=[VMEM],
        out_specs=VMEM,
        compiler_params=SMALL,
        cost_estimate=cost(0, 1_500_000),
    )(mixed)


def hidden_kernel(shares_ref, out_ref):
    sums = jnp.sum(shares_ref[...].astype(jnp.float32), axis=0)
    hidden = (jax.nn.silu(sums[0]) * sums[1]).astype(jnp.bfloat16)
    for shard in range(out_ref.shape[0]):
        out_ref[shard] = hidden


def hidden_units(shares, copies):
    _, _, units, slots = shares.shape
    return pl.pallas_call(
        hidden_kernel,
        out_shape=jax.ShapeDtypeStruct((copies, units, slots), jnp.bfloat16),
        in_specs=[VMEM],
        out_specs=VMEM,
        compiler_params=SMALL,
        cost_estimate=cost(shares.size, 800_000),
    )(shares)


def results_kernel(place_ref, hidden_ref, tile_ref, kept_ref, cross_ref):
    total = contract_first(hidden_ref[...], tile_ref[...])
    kept, cross = split(place_ref[0], total)
    kept_ref[...] = kept.reshape(kept_ref.shape)
    cross_ref[...] = cross.astype(jnp.bfloat16).reshape(cross_ref.shape)


def expert_results(place, hidden, tile):
    shape = (2, hidden.shape[1] // 2, tile.shape[1] // 2)
    return pl.pallas_call(
        results_kernel,
        out_shape=[
            jax.ShapeDtypeStruct(shape, jnp.float32),
            jax.ShapeDtypeStruct(shape, jnp.bfloat16),
        ],
        in_specs=[SMEM, VMEM, VMEM],
        out_specs=[VMEM] * 2,
        compiler_params=SMALL,
        cost_estimate=cost(2 * hidden.size * tile.shape[1], 900_000),
    )(place, hidden, tile)


def body(
    hidden_acts,
    train_rows,
    out_grad,
    master,
    moment1,
    moment2,
    gate_up,
    dec_tokens,
    route_ids,
    route_gates,
):
    index = lax.axis_index("dp")
    shards = lax.axis_size("dp")
    half, ring, core = index >> 3, (index >> 1) & (RING - 1), index & (CORES - 1)
    place = jnp.stack([half, ring, core]).astype(jnp.int32)
    token_count, width = dec_tokens.shape
    tokens = train_rows.shape[1]

    sides = [[h * RING * CORES + k for k in range(RING * CORES)] for h in range(HALVES)]
    acts = lax.all_gather(hidden_acts[0], "dp", axis=0, tiled=True, axis_index_groups=sides)
    sends = pack(place, train_rows, out_grad, master, moment1, moment2)
    parts = [sends[0]] + [
        lax.ppermute(sends[step], "dp", permutation(0, step, 0)) for step in range(1, RING)
    ]

    choices_per = route_ids.shape[1]
    expert_count = lax.axis_size("exp")
    capacity = min(token_count, max(2, 2 * choices_per * token_count // expert_count))
    slot_count = expert_count * capacity
    flat_ids = route_ids.reshape(-1)
    onehot = (flat_ids[:, None] == jnp.arange(expert_count, dtype=jnp.int32)[None, :]).astype(
        jnp.int32
    )
    earlier = jnp.cumsum(onehot, axis=0) - onehot
    position = jnp.sum(earlier * onehot, axis=1)
    slot_index = flat_ids * capacity + position
    placement = (slot_index[:, None] == jnp.arange(slot_count, dtype=jnp.int32)[None, :]).astype(
        jnp.bfloat16
    )
    repeated = jnp.repeat(dec_tokens, choices_per, axis=0)
    outgoing = jnp.einsum(
        "rs,rd->sd", placement, repeated, preferred_element_type=jnp.float32
    ).astype(jnp.bfloat16)
    arrived = lax.all_to_all(
        outgoing.reshape(expert_count, capacity, width),
        "exp",
        split_axis=0,
        concat_axis=0,
        tiled=True,
    )
    rows_in = arrived.reshape(slot_count, width)

    mixed = jnp.einsum(
        "dgf,sd->gsf", gate_up[0], rows_in, preferred_element_type=jnp.float32
    )
    shares = lax.all_to_all(
        turn(mixed, shards), "dp", split_axis=0, concat_axis=0, tiled=True
    )
    hidden = lax.all_to_all(
        hidden_units(shares, RING * CORES),
        "dp",
        split_axis=0,
        concat_axis=0,
        tiled=True,
        axis_index_groups=sides,
    ).reshape(-1, slot_count)

    across_cores, across_halves = permutation(0, 0, 1), permutation(1, 0, 0)
    mine, theirs = split_cores(place, parts)
    near = lax.ppermute(theirs, "dp", across_cores)
    cross = gradient_rows(place, acts, mine, near, tokens, 1, jnp.bfloat16)
    far = lax.ppermute(cross, "dp", across_halves)
    kept = gradient_rows(place, acts, mine, near, tokens, 0, jnp.float32)
    tile = adam_tile(tokens, place, kept, far, mine, near)

    kept_results, cross_results = expert_results(place, hidden, tile.reshape(-1, 2 * width))
    far_results = lax.ppermute(cross_results, "dp", across_halves)
    results = (kept_results + far_results.astype(jnp.float32)).astype(jnp.bfloat16)
    returned = lax.all_to_all(
        results.reshape(expert_count, capacity, width),
        "exp",
        split_axis=0,
        concat_axis=0,
        tiled=True,
    )
    back_rows = returned.reshape(slot_count, width)
    chosen = jnp.einsum("rs,sd->rd", placement, back_rows, preferred_element_type=jnp.float32)
    weighted = chosen.reshape(token_count, choices_per, width) * route_gates[:, :, None]
    return jnp.sum(weighted, axis=1).astype(jnp.bfloat16)


def solution(mesh):
    in_specs = (
        P("exp", "dp", None),
        P("exp", "dp"),
        P("dp", None),
        P("exp", "dp", None),
        P("exp", "dp", None),
        P("exp", "dp", None),
        P("exp", "dp", None, None),
        P("exp", "dp"),
        P("exp", None),
        P("exp", None),
    )
    out_specs = P("exp", "dp")
    return jax.shard_map(body, mesh=mesh, in_specs=in_specs, out_specs=out_specs, check_vma=False)
```

time: 388 us -> 201 us (0.52)
  waiting for transfers between devices: 251 us -> 59.1 us
  blocking collectives: 22.3 us -> 62.1 us
  starting transfers between devices: 60.9 us -> 33.9 us
  Pallas kernels: 0 us -> 25.7 us
  local copies, waits for them, and re-layouts: 22.8 us -> 2.96 us
  matrix products: 9.14 us -> 1.49 us
  other arithmetic: 7.15 us -> 0.94 us
    reduce_scatter x1 -> x0, waiting for transfers between devices: 111 us -> none  [body(): lax.psum_scatter(mixed.astype(jnp.bfloat16), 'dp', scatter_dimension=2, t...]
    unnamed x3 -> x1, waiting for transfers between devices: 93.2 us -> 0.71 us
    all_to_all x0 -> x1, blocking collectives: none -> 62.1 us  [body(): lax.all_to_all(outgoing.reshape(expert_count, capacity, width), 'exp', sp...]
    all_to_all x3, starting transfers between devices: 60.9 us -> 16 us  [the longest x1 8.01 us: body(): lax.all_to_all(turn(mixed, shards), 'dp', split_axis=0, concat_axis=0, ti...]
    ppermute x0 -> x6, waiting for transfers between devices: none -> 30.3 us  [the longest x3 21 us: body(): lax.ppermute(sends[step], 'dp', permutation(0, step, 0))]
    pallas_call x0 -> x8, Pallas kernels: none -> 25.7 us  [the longest x2 7.59 us: gradient_rows(): pl.pallas_call(gradient_kernel, out_shape=jax.ShapeDtypeStruct((sources,...]
    all_gather x1 -> x0, blocking collectives: 22.3 us -> none  [body(): hidden = lax.all_gather(partial_hidden, 'dp', axis=1, tiled=True)]
    all_to_all x3, waiting for transfers between devices: 47.3 us -> 28.1 us  [the longest x1 24.4 us: body(): lax.all_to_all(results.reshape(expert_count, capacity, width), 'exp', spl...]
  transfers between devices with their start and end apart: 5 -> 10, of which waited for: 4 -> 7; matrix products, arithmetic and copies ran while one was open for 5% -> 1% of each run, Pallas kernels for 0% -> 12%
where the time goes in v3:
time: 201 us; the launch traced here: 200 us
  blocking collectives  62.1 us (31%)
  waiting for transfers between devices  59.1 us (29%)
  starting transfers between devices  33.9 us (17%)
  Pallas kernels  25.7 us (13%)
  between operations  13.6 us (7%)
  local copies, waits for them, and re-layouts  2.96 us (1%)
    all_to_all x1, blocking collectives, body(): lax.all_to_all(outgoing.reshape(expert_count, capacity, width), 'exp', sp...  62.1 us
    all_to_all x1, waiting for transfers between devices, body(): lax.all_to_all(results.reshape(expert_count, capacity, width), 'exp', spl...  24.4 us
    ppermute x3, waiting for transfers between devices, body(): lax.ppermute(sends[step], 'dp', permutation(0, step, 0))  21 us
    ppermute x3, starting transfers between devices, body(): lax.ppermute(sends[step], 'dp', permutation(0, step, 0))  11.7 us
    all_to_all x1, starting transfers between devices, body(): lax.all_to_all(turn(mixed, shards), 'dp', split_axis=0, concat_axis=0, ti...  8.01 us
    pallas_call x2, Pallas kernels, gradient_rows(): pl.pallas_call(gradient_kernel, out_shape=jax.ShapeDtypeStruct((sources,...  7.59 us
    pallas_call x1, Pallas kernels, pack(): pl.pallas_call(pack_kernel, grid=(PIECES,), out_shape=[jax.ShapeDtypeStru...  5.73 us
    ppermute x1, waiting for transfers between devices, body(): far_results = lax.ppermute(cross_results, 'dp', across_halves)  5.37 us
  transfers between devices with their start and end apart: 10, of which 7 were waited for; matrix products, arithmetic and copies ran while one was open for 1% of the time, Pallas kernels for 12%

profile of v3, /device:TPU:4, one launch (start us, length us, event | category | flops | bytes accessed | tf_op | source)
XLA Modules:
  0.0 199.7 jit_solution(18262179355910043713)
XLA Ops:
  6.5 0.0 copy-start
  6.5 0.0 all-gather.3.cloned.1.call-start
  6.5 0.7 all-gather.3.cloned.1.call-update
  7.3 0.6 pad_add_fusion.place_ref
  7.8 0.0 copy-start.5
  7.8 5.7 %shard_map.102 = (bf16[320,896]{1,0:T(8,128)(2,1)}, bf16[320,896]{1,0:T(8,128)(2,1)}, bf16[320,896]{1,0:T(8,128)(2,1)}, bf16[320,896]{1,0:T(8,128)(2,1)}) custom-call(s32[3]{0:T(128)} %pad_add_fusion.place_ref, s32[1,128]{1,0:T(1,128)} %rows_ref.1, bf16[256,3584]{1,0:T(8,128)(2,1)} %grad_ref.1, f32[1,64,3584]{2,1,0:T(8,128)} %master_ref.1, ...), custom_call_target="tpu_custom_call" | custom-call | flops 234881024 | bytes 7000000 | tf_op jit(solution)/shard_map/pallas_call | solution.py:89
  13.6 0.0 copy-start.6
  13.6 3.6 %collective-permute-start = (bf16[320,896]{1,0:T(8,128)(2,1)}, bf16[320,896]{1,0:T(8,128)(2,1)S(1)}, u32[]{:S(2)}, u32[]{:S(2)}) collective-permute-start(bf16[320,896]{1,0:T(8,128)(2,1)} %get-tuple-element.14), channel_id=1, source_target_pairs={{0,2},{1,3},{2,4},{3,5},{4,6},{5,7},{6,0},{7,1},{8,10},{9,11},{10,... | collective-permute-start | bytes 1720328 | tf_op jit(solution)/shard_map/ppermute | solution.py:304
  17.2 4.8 %collective-permute-start.1 = (bf16[320,896]{1,0:T(8,128)(2,1)}, bf16[320,896]{1,0:T(8,128)(2,1)}, u32[]{:S(2)}, u32[]{:S(2)}) collective-permute-start(bf16[320,896]{1,0:T(8,128)(2,1)} %get-tuple-element.15), channel_id=1, source_target_pairs={{0,4},{1,5},{2,6},{3,7},{4,0},{5,1},{6,2},{7,3},{8,12},{9,13},{10,... | collective-permute-start | bytes 1720328 | tf_op jit(solution)/shard_map/ppermute | solution.py:304
  22.0 3.3 %collective-permute-start.2 = (bf16[320,896]{1,0:T(8,128)(2,1)}, bf16[320,896]{1,0:T(8,128)(2,1)}, u32[]{:S(2)}, u32[]{:S(2)}) collective-permute-start(bf16[320,896]{1,0:T(8,128)(2,1)} %get-tuple-element.16), channel_id=1, source_target_pairs={{0,6},{1,7},{2,0},{3,1},{4,2},{5,3},{6,4},{7,5},{8,14},{9,15},{10,... | collective-permute-start | bytes 1720328 | tf_op jit(solution)/shard_map/ppermute | solution.py:304
  25.3 0.0 copy-done.5
  25.3 0.1 eq.50
  25.3 0.1 fusion.5
  25.4 0.1 reduce_window_sum.11
  25.5 0.2 select_reduce_fusion
  25.7 6.1 %collective-permute-done.refs_1_ = bf16[320,896]{1,0:T(8,128)(2,1)S(1)} collective-permute-done((bf16[320,896]{1,0:T(8,128)(2,1)}, bf16[320,896]{1,0:T(8,128)(2,1)S(1)}, u32[]{:S(2)}, u32[]{:S(2)}) %collective-permute-start) | collective-permute-done | bytes 573472 | tf_op jit(solution)/shard_map/ppermute | solution.py:304
  31.8 0.0 copy-start.3
  31.8 13.6 %collective-permute-done.1.refs_2_ = bf16[320,896]{1,0:T(8,128)(2,1)} collective-permute-done((bf16[320,896]{1,0:T(8,128)(2,1)}, bf16[320,896]{1,0:T(8,128)(2,1)}, u32[]{:S(2)}, u32[]{:S(2)}) %collective-permute-start.1) | collective-permute-done | bytes 573472 | tf_op jit(solution)/shard_map/ppermute | solution.py:304
  45.3 1.4 collective-permute-done.2.refs_3_
  46.7 0.0 copy-done.3
  46.7 5.2 %shard_map.103 = (bf16[4,320,448]{2,1,0:T(8,128)(2,1)}, bf16[4,320,448]{2,1,0:T(8,128)(2,1)}) custom-call(s32[3]{0:T(128)} %pad_add_fusion.place_ref, bf16[320,896]{1,0:T(8,128)(2,1)} %get-tuple-element.13.refs_0_, bf16[320,896]{1,0:T(8,128)(2,1)} %copy-done.3, bf16[320,896]{1,0:T(8,128)(2,1)} %collective-permute-done.1.refs_2_, ...), custom_call_target="tpu_custom_call" | custom-call | bytes 5000000 | tf_op jit(solution)/shard_map/pallas_call | solution.py:126
  51.9 1.9 collective-permute-start.3
  53.8 0.0 copy-done.6
  53.8 0.2 convolution_convert_fusion
  54.1 0.1 copy.13
  54.2 62.1 %all_to_all.20 = bf16[64,2,224]{2,1,0:T(2,128)(2,1)S(1)} all-to-all(bf16[64,2,224]{2,1,0:T(2,128)(2,1)S(1)} %reshape.62), channel_id=1, replica_groups=mesh['exp'=64,'dp'=16] {'exp'}, dimensions={0} | all-to-all | bytes 114688 | tf_op jit(solution)/shard_map/all_to_all | solution.py:325
  116.4 0.1 reshape.63
  116.4 0.0 copy-done
  116.4 0.4 convolution_bitcast_fusion.mixed_ref
  116.9 1.0 shard_map.100
  117.9 8.0 %all-to-all-start.1 = ((bf16[16,2,64,128]{3,2,1,0:T(8,128)(2,1)}), bf16[16,2,64,128]{3,2,1,0:T(8,128)(2,1)S(1)}, u32[]{:S(2)}, u32[]{:S(2)}) async-start(bf16[16,2,64,128]{3,2,1,0:T(8,128)(2,1)} %shard_map.100), calls=%async_computation.1 | async-start | bytes 1048576 | tf_op jit(solution)/shard_map/all_to_all | solution.py:337
  125.9 0.0 collective-permute-done.3.near_ref
  125.9 0.0 all-gather.3.cloned.1.call-done
  125.9 3.7 %shard_map.105 = bf16[8,64,448]{2,1,0:T(8,128)(2,1)} custom-call(s32[3]{0:T(128)} %pad_add_fusion.place_ref, bf16[8,128,1024]{2,1,0:T(8,128)(2,1)} %bitcast.24, bf16[4,320,448]{2,1,0:T(8,128)(2,1)} %get-tuple-element.17.mine_ref, bf16[4,320,448]{2,1,0:T(8,128)(2,1)} %collective-permute-done.3.near_ref), custom_call_target="tpu_custom_call" | custom-call | flops 469762048 | bytes 4000000 | tf_op jit(solution)/shard_map/pallas_call | solution.py:158
  129.7 2.0 %collective-permute-start.4 = (bf16[8,64,448]{2,1,0:T(8,128)(2,1)}, bf16[8,64,448]{2,1,0:T(8,128)(2,1)S(1)}, u32[]{:S(2)}, u32[]{:S(2)}) collective-permute-start(bf16[8,64,448]{2,1,0:T(8,128)(2,1)} %shard_map.105), channel_id=1, source_target_pairs={{0,8},{1,9},{2,10},{3,11},{4,12},{5,13},{6,14},{7,15},{8,0},{9,1},... | collective-permute-start | bytes 1376264 | tf_op jit(solution)/shard_map/ppermute | solution.py:353
  131.7 3.7 %all-to-all-done.1.shares_ref = bf16[16,2,64,128]{3,2,1,0:T(8,128)(2,1)S(1)} async-done(((bf16[16,2,64,128]{3,2,1,0:T(8,128)(2,1)}), bf16[16,2,64,128]{3,2,1,0:T(8,128)(2,1)S(1)}, u32[]{:S(2)}, u32[]{:S(2)}) %all-to-all-start.1) | async-done | bytes 524320 | tf_op jit(solution)/shard_map/all_to_all | solution.py:337
  135.4 0.7 shard_map.101
  136.1 3.4 %all-to-all-start.2 = ((bf16[8,64,128]{2,1,0:T(8,128)(2,1)}), bf16[8,64,128]{2,1,0:T(8,128)(2,1)S(1)}, u32[]{:S(2)}, u32[]{:S(2)}) async-start(bf16[8,64,128]{2,1,0:T(8,128)(2,1)} %shard_map.101), calls=%async_computation.2 | async-start | bytes 262144 | tf_op jit(solution)/shard_map/all_to_all | solution.py:340
  139.5 3.8 %shard_map.104.kept_ref = f32[8,64,448]{2,1,0:T(8,128)} custom-call(s32[3]{0:T(128)} %pad_add_fusion.place_ref, bf16[8,128,1024]{2,1,0:T(8,128)(2,1)} %bitcast.25, bf16[4,320,448]{2,1,0:T(8,128)(2,1)} %get-tuple-element.17.mine_ref, bf16[4,320,448]{2,1,0:T(8,128)(2,1)} %collective-permute-done.3.near_ref), custom_call_target="tpu_custom_call" | custom-call | flops 469762048 | bytes 4000000 | tf_op jit(solution)/shard_map/pallas_call | solution.py:158
  143.4 0.0 copy-start.2
  143.4 3.9 %collective-permute-done.4.far_ref = bf16[8,64,448]{2,1,0:T(8,128)(2,1)S(1)} collective-permute-done((bf16[8,64,448]{2,1,0:T(8,128)(2,1)}, bf16[8,64,448]{2,1,0:T(8,128)(2,1)S(1)}, u32[]{:S(2)}, u32[]{:S(2)}) %collective-permute-start.4) | collective-permute-done | bytes 458784 | tf_op jit(solution)/shard_map/ppermute | solution.py:353
  147.3 0.0 copy-start.4
  147.3 0.8 copy-done.4
  148.1 0.0 copy-start.7
  148.1 4.4 %shard_map.106 = bf16[8,64,448]{2,1,0:T(8,128)(2,1)} custom-call(s32[3]{0:T(128)} %pad_add_fusion.place_ref, f32[8,64,448]{2,1,0:T(8,128)} %shard_map.104.kept_ref, bf16[8,64,448]{2,1,0:T(8,128)(2,1)} %copy-done.4, bf16[4,320,448]{2,1,0:T(8,128)(2,1)} %get-tuple-element.17.mine_ref, bf16[4,320,448]{2,1,0:T(8,128)(2,1)} %collective-permute-done.3.near_ref), custom_call_target="tpu_custom_call" | custom-call | flops 4587520 | bytes 5000000 | tf_op jit(solution)/shard_map/pallas_call | solution.py:206
  152.5 0.0 all-to-all-done.2
  152.5 0.0 copy-done.2
  152.5 0.0 copy-start.1
  152.5 1.0 copy-done.1
  153.6 1.0 shard_map.107
  154.5 2.3 %collective-permute-start.5 = (bf16[2,64,224]{2,1,0:T(8,128)(2,1)S(1)}, bf16[2,64,224]{2,1,0:T(8,128)(2,1)S(1)}, u32[]{:S(2)}, u32[]{:S(2)}) collective-permute-start(bf16[2,64,224]{2,1,0:T(8,128)(2,1)S(1)} %get-tuple-element.20), channel_id=1, source_target_pairs={{0,8},{1,9},{2,10},{3,11},{4,12},{5,13},{6,14},{7,15},{8,0},{9,1},... | collective-permute-start | bytes 172040 | tf_op jit(solution)/shard_map/ppermute | solution.py:358
  156.8 5.4 %collective-permute-done.5 = bf16[2,64,224]{2,1,0:T(8,128)(2,1)S(1)} collective-permute-done((bf16[2,64,224]{2,1,0:T(8,128)(2,1)S(1)}, bf16[2,64,224]{2,1,0:T(8,128)(2,1)S(1)}, u32[]{:S(2)}, u32[]{:S(2)}) %collective-permute-start.5) | collective-permute-done | bytes 57376 | tf_op jit(solution)/shard_map/ppermute | solution.py:358
  162.2 0.7 reshape.67
  162.9 4.6 %all-to-all-start.3 = ((bf16[64,2,224]{2,1,0:T(2,128)(2,1)}), bf16[64,2,224]{2,1,0:T(2,128)(2,1)S(1)}, u32[]{:S(2)}, u32[]{:S(2)}) async-start(bf16[64,2,224]{2,1,0:T(2,128)(2,1)} %reshape.67), calls=%async_computation.3 | async-start | bytes 131072 | tf_op jit(solution)/shard_map/all_to_all | solution.py:360
  167.5 0.1 reduce_sum.21
  167.6 24.4 %all-to-all-done.3 = bf16[64,2,224]{2,1,0:T(2,128)(2,1)S(1)} async-done(((bf16[64,2,224]{2,1,0:T(2,128)(2,1)}), bf16[64,2,224]{2,1,0:T(2,128)(2,1)S(1)}, u32[]{:S(2)}, u32[]{:S(2)}) %all-to-all-start.3) | async-done | bytes 57376 | tf_op jit(solution)/shard_map/all_to_all | solution.py:360
  192.0 0.1 reshape.68
  192.0 0.0 copy-done.7
  192.1 0.8 fusion
  (4 shorter events, 0.1 us)
Async XLA Ops:
  6.5 109.9 %copy-start = (bf16[1,224,2,1024]{3,2,1,0:T(2,128)(2,1)S(1)}, bf16[1,224,2,1024]{3,2,1,0:T(2,128)(2,1)}, u32[]{:S(2)}) copy-start(bf16[1,224,2,1024]{3,2,1,0:T(2,128)(2,1)} %param.16) | copy-start | bytes 2752516
  6.5 119.4 %all-gather.3.cloned.1.call-start = ((), (), s32[]{:S(2)}) async-start(), calls=%async_computation.4 | async-start | bytes 2359296 | tf_op jit(solution)/shard_map/all_gather | solution.py:301
  7.8 17.4 %copy-start.5 = (s32[8,8]{1,0:T(8,128)S(1)}, s32[8,8]{1,0:T(8,128)}, u32[]{:S(2)}) copy-start(s32[8,8]{1,0:T(8,128)} %param.18) | copy-start | bytes 772
  13.6 40.3 %copy-start.6 = (bf16[8,224]{1,0:T(8,128)(2,1)S(1)}, bf16[8,224]{1,0:T(8,128)(2,1)}, u32[]{:S(2)}) copy-start(bf16[8,224]{1,0:T(8,128)(2,1)} %param.17) | copy-start | bytes 10756
  13.6 18.2 %collective-permute-start = (bf16[320,896]{1,0:T(8,128)(2,1)}, bf16[320,896]{1,0:T(8,128)(2,1)S(1)}, u32[]{:S(2)}, u32[]{:S(2)}) collective-permute-start(bf16[320,896]{1,0:T(8,128)(2,1)} %get-tuple-element.14), channel_id=1, source_target_pairs={{0,2},{1,3},{2,4},{3,5},{4,6},{5,7},{6,0},{7,1},{8,10},{9,11},{10,... | collective-permute-start | bytes 1720328 | tf_op jit(solution)/shard_map/ppermute | solution.py:304
  17.2 28.2 %collective-permute-start.1 = (bf16[320,896]{1,0:T(8,128)(2,1)}, bf16[320,896]{1,0:T(8,128)(2,1)}, u32[]{:S(2)}, u32[]{:S(2)}) collective-permute-start(bf16[320,896]{1,0:T(8,128)(2,1)} %get-tuple-element.15), channel_id=1, source_target_pairs={{0,4},{1,5},{2,6},{3,7},{4,0},{5,1},{6,2},{7,3},{8,12},{9,13},{10,... | collective-permute-start | bytes 1720328 | tf_op jit(solution)/shard_map/ppermute | solution.py:304
  22.0 24.7 %collective-permute-start.2 = (bf16[320,896]{1,0:T(8,128)(2,1)}, bf16[320,896]{1,0:T(8,128)(2,1)}, u32[]{:S(2)}, u32[]{:S(2)}) collective-permute-start(bf16[320,896]{1,0:T(8,128)(2,1)} %get-tuple-element.16), channel_id=1, source_target_pairs={{0,6},{1,7},{2,0},{3,1},{4,2},{5,3},{6,4},{7,5},{8,14},{9,15},{10,... | collective-permute-start | bytes 1720328 | tf_op jit(solution)/shard_map/ppermute | solution.py:304
  31.8 14.9 %copy-start.3 = (bf16[320,896]{1,0:T(8,128)(2,1)}, bf16[320,896]{1,0:T(8,128)(2,1)S(1)}, u32[]{:S(2)}) copy-start(bf16[320,896]{1,0:T(8,128)(2,1)S(1)} %collective-permute-done.refs_1_) | copy-start | bytes 1720324
  51.9 74.0 %collective-permute-start.3 = (bf16[4,320,448]{2,1,0:T(8,128)(2,1)}, bf16[4,320,448]{2,1,0:T(8,128)(2,1)}, u32[]{:S(2)}, u32[]{:S(2)}) collective-permute-start(bf16[4,320,448]{2,1,0:T(8,128)(2,1)} %get-tuple-element.18), channel_id=1, source_target_pairs={{0,1},{1,0},{2,3},{3,2},{4,5},{5,4},{6,7},{7,6},{8,9},{9,8},{10,11... | collective-permute-start | bytes 3440648 | tf_op jit(solution)/shard_map/ppermute | solution.py:351
  117.9 17.5 %all-to-all-start.1 = ((bf16[16,2,64,128]{3,2,1,0:T(8,128)(2,1)}), bf16[16,2,64,128]{3,2,1,0:T(8,128)(2,1)S(1)}, u32[]{:S(2)}, u32[]{:S(2)}) async-start(bf16[16,2,64,128]{3,2,1,0:T(8,128)(2,1)} %shard_map.100), calls=%async_computation.1 | async-start | bytes 1048576 | tf_op jit(solution)/shard_map/all_to_all | solution.py:337
  129.7 17.6 %collective-permute-start.4 = (bf16[8,64,448]{2,1,0:T(8,128)(2,1)}, bf16[8,64,448]{2,1,0:T(8,128)(2,1)S(1)}, u32[]{:S(2)}, u32[]{:S(2)}) collective-permute-start(bf16[8,64,448]{2,1,0:T(8,128)(2,1)} %shard_map.105), channel_id=1, source_target_pairs={{0,8},{1,9},{2,10},{3,11},{4,12},{5,13},{6,14},{7,15},{8,0},{9,1},... | collective-permute-start | bytes 1376264 | tf_op jit(solution)/shard_map/ppermute | solution.py:353
  136.1 16.4 %all-to-all-start.2 = ((bf16[8,64,128]{2,1,0:T(8,128)(2,1)}), bf16[8,64,128]{2,1,0:T(8,128)(2,1)S(1)}, u32[]{:S(2)}, u32[]{:S(2)}) async-start(bf16[8,64,128]{2,1,0:T(8,128)(2,1)} %shard_map.101), calls=%async_computation.2 | async-start | bytes 262144 | tf_op jit(solution)/shard_map/all_to_all | solution.py:340
  143.4 9.2 %copy-start.2 = (s32[3]{0:T(128)S(1)}, s32[3]{0:T(128)}, u32[]{:S(2)}) copy-start(s32[3]{0:T(128)} %pad_add_fusion.place_ref) | copy-start | bytes 40
  147.3 0.8 copy-start.4
  148.1 44.0 %copy-start.7 = (f32[8,8]{1,0:T(8,128)S(1)}, f32[8,8]{1,0:T(8,128)}, u32[]{:S(2)}) copy-start(f32[8,8]{1,0:T(8,128)} %param.19) | copy-start | bytes 772
  152.5 1.0 copy-start.1
  154.5 7.7 %collective-permute-start.5 = (bf16[2,64,224]{2,1,0:T(8,128)(2,1)S(1)}, bf16[2,64,224]{2,1,0:T(8,128)(2,1)S(1)}, u32[]{:S(2)}, u32[]{:S(2)}) collective-permute-start(bf16[2,64,224]{2,1,0:T(8,128)(2,1)S(1)} %get-tuple-element.20), channel_id=1, source_target_pairs={{0,8},{1,9},{2,10},{3,11},{4,12},{5,13},{6,14},{7,15},{8,0},{9,1},... | collective-permute-start | bytes 172040 | tf_op jit(solution)/shard_map/ppermute | solution.py:358
  162.9 29.1 %all-to-all-start.3 = ((bf16[64,2,224]{2,1,0:T(2,128)(2,1)}), bf16[64,2,224]{2,1,0:T(2,128)(2,1)S(1)}, u32[]{:S(2)}, u32[]{:S(2)}) async-start(bf16[64,2,224]{2,1,0:T(2,128)(2,1)} %reshape.67), calls=%async_computation.3 | async-start | bytes 131072 | tf_op jit(solution)/shard_map/all_to_all | solution.py:360
Sparse Core Ops, SparseCore 0:
  10.1 50.5 all-gather.2

commit v4 on v3

--- a/solution.py
+++ b/solution.py
@@ -329,6 +329,7 @@
         concat_axis=0,
         tiled=True,
     )
+    arrived, held = lax.optimization_barrier((arrived, parts))
     rows_in = arrived.reshape(slot_count, width)
 
     mixed = jnp.einsum(
@@ -347,7 +348,7 @@
     ).reshape(-1, slot_count)
 
     across_cores, across_halves = permutation(0, 0, 1), permutation(1, 0, 0)
-    mine, theirs = split_cores(place, parts)
+    mine, theirs = split_cores(place, held)
     near = lax.ppermute(theirs, "dp", across_cores)
     cross = gradient_rows(place, acts, mine, near, tokens, 1, jnp.bfloat16)
     far = lax.ppermute(cross, "dp", across_halves)

time: 201 us -> 170 us (0.85)
  waiting for transfers between devices: 59.1 us -> 38.1 us
  blocking collectives: 62.1 us -> 54.7 us
  starting transfers between devices: 33.9 us -> 30.8 us
    ppermute x3, waiting for transfers between devices: 21 us -> 0.01 us  [body(): lax.ppermute(sends[step], 'dp', permutation(0, step, 0))]
    all_to_all x1, blocking collectives: 62.1 us -> 54.7 us  [body(): lax.all_to_all(outgoing.reshape(expert_count, capacity, width), 'exp', sp...]
    all_to_all x1, starting transfers between devices: 8.01 us -> 5.04 us  [body(): lax.all_to_all(turn(mixed, shards), 'dp', split_axis=0, concat_axis=0, ti...]
  transfers between devices with their start and end apart: 10 -> 10, of which waited for: 7 -> 4; matrix products, arithmetic and copies ran while one was open for 1% -> 1% of each run, Pallas kernels for 12% -> 15%
where the time goes in v4:
time: 170 us; the launch traced here: 169 us
  blocking collectives  54.7 us (32%)
  waiting for transfers between devices  38.1 us (22%)
  starting transfers between devices  30.8 us (18%)
  Pallas kernels  25.7 us (15%)
  between operations  13.6 us (8%)
  local copies, waits for them, and re-layouts  3.77 us (2%)
    all_to_all x1, blocking collectives, body(): lax.all_to_all(outgoing.reshape(expert_count, capacity, width), 'exp', sp...  54.7 us
    all_to_all x1, waiting for transfers between devices, body(): lax.all_to_all(results.reshape(expert_count, capacity, width), 'exp', spl...  24.4 us
    ppermute x3, starting transfers between devices, body(): lax.ppermute(sends[step], 'dp', permutation(0, step, 0))  11.5 us
    pallas_call x2, Pallas kernels, gradient_rows(): pl.pallas_call(gradient_kernel, out_shape=jax.ShapeDtypeStruct((sources,...  7.59 us
    pallas_call x1, Pallas kernels, pack(): pl.pallas_call(pack_kernel, grid=(PIECES,), out_shape=[jax.ShapeDtypeStru...  5.74 us
    ppermute x1, waiting for transfers between devices, body(): far_results = lax.ppermute(cross_results, 'dp', across_halves)  5.36 us
    pallas_call x1, Pallas kernels, split_cores(): pl.pallas_call(core_kernel, grid=(rows // block,), out_shape=[jax.ShapeDt...  5.15 us
    all_to_all x1, starting transfers between devices, body(): lax.all_to_all(turn(mixed, shards), 'dp', split_axis=0, concat_axis=0, ti...  5.04 us
  transfers between devices with their start and end apart: 10, of which 4 were waited for; matrix products, arithmetic and copies ran while one was open for 1% of the time, Pallas kernels for 15%

profile of v4, /device:TPU:4, one launch (start us, length us, event | category | flops | bytes accessed | tf_op | source)
XLA Modules:
  0.0 169.0 jit_solution(6718600117710128847)
XLA Ops:
  6.5 0.0 copy-start
  6.5 0.0 all-gather.3.cloned.1.call-start
  6.5 0.7 all-gather.3.cloned.1.call-update
  7.3 0.6 pad_add_fusion.place_ref
  7.8 0.0 copy-start.5
  7.8 0.0 copy-start.6
  7.8 5.7 %shard_map.100 = (bf16[320,896]{1,0:T(8,128)(2,1)}, bf16[320,896]{1,0:T(8,128)(2,1)}, bf16[320,896]{1,0:T(8,128)(2,1)}, bf16[320,896]{1,0:T(8,128)(2,1)}) custom-call(s32[3]{0:T(128)} %pad_add_fusion.place_ref, s32[1,128]{1,0:T(1,128)} %rows_ref.1, bf16[256,3584]{1,0:T(8,128)(2,1)} %grad_ref.1, f32[1,64,3584]{2,1,0:T(8,128)} %master_ref.1, ...), custom_call_target="tpu_custom_call" | custom-call | flops 234881024 | bytes 7000000 | tf_op jit(solution)/shard_map/pallas_call | solution.py:89
  13.6 3.5 %collective-permute-start = (bf16[320,896]{1,0:T(8,128)(2,1)}, bf16[320,896]{1,0:T(8,128)(2,1)S(1)}, u32[]{:S(2)}, u32[]{:S(2)}) collective-permute-start(bf16[320,896]{1,0:T(8,128)(2,1)} %get-tuple-element.19), channel_id=1, source_target_pairs={{0,2},{1,3},{2,4},{3,5},{4,6},{5,7},{6,0},{7,1},{8,10},{9,11},{10,... | collective-permute-start | bytes 1720328 | tf_op jit(solution)/shard_map/ppermute | solution.py:304
  17.1 4.8 %collective-permute-start.1 = (bf16[320,896]{1,0:T(8,128)(2,1)}, bf16[320,896]{1,0:T(8,128)(2,1)}, u32[]{:S(2)}, u32[]{:S(2)}) collective-permute-start(bf16[320,896]{1,0:T(8,128)(2,1)} %get-tuple-element.20), channel_id=1, source_target_pairs={{0,4},{1,5},{2,6},{3,7},{4,0},{5,1},{6,2},{7,3},{8,12},{9,13},{10,... | collective-permute-start | bytes 1720328 | tf_op jit(solution)/shard_map/ppermute | solution.py:304
  21.9 3.3 %collective-permute-start.2 = (bf16[320,896]{1,0:T(8,128)(2,1)}, bf16[320,896]{1,0:T(8,128)(2,1)}, u32[]{:S(2)}, u32[]{:S(2)}) collective-permute-start(bf16[320,896]{1,0:T(8,128)(2,1)} %get-tuple-element.21), channel_id=1, source_target_pairs={{0,6},{1,7},{2,0},{3,1},{4,2},{5,3},{6,4},{7,5},{8,14},{9,15},{10,... | collective-permute-start | bytes 1720328 | tf_op jit(solution)/shard_map/ppermute | solution.py:304
  25.1 0.0 copy-done.5
  25.1 0.1 eq.50
  25.2 0.1 fusion.5
  25.3 0.1 reduce_window_sum.11
  25.4 0.2 select_reduce_fusion
  25.6 0.0 copy-done.6
  25.6 0.2 convolution_convert_fusion
  25.8 0.1 copy.13
  26.0 54.7 %all_to_all.20 = bf16[64,2,224]{2,1,0:T(2,128)(2,1)S(1)} all-to-all(bf16[64,2,224]{2,1,0:T(2,128)(2,1)S(1)} %reshape.62), channel_id=1, replica_groups=mesh['exp'=64,'dp'=16] {'exp'}, dimensions={0} | all-to-all | bytes 114688 | tf_op jit(solution)/shard_map/all_to_all | solution.py:325
  80.7 0.0 collective-permute-done.refs_1_
  80.8 0.0 copy-start.3
  80.8 0.0 collective-permute-done.1.refs_2_
  80.8 0.0 collective-permute-done.2.refs_3_
  80.8 0.8 copy-done.3
  81.6 5.2 %shard_map.103 = (bf16[4,320,448]{2,1,0:T(8,128)(2,1)}, bf16[4,320,448]{2,1,0:T(8,128)(2,1)}) custom-call(s32[3]{0:T(128)} %pad_add_fusion.place_ref, bf16[320,896]{1,0:T(8,128)(2,1)} %get-tuple-element.23.refs_0_, bf16[320,896]{1,0:T(8,128)(2,1)} %copy-done.3, bf16[320,896]{1,0:T(8,128)(2,1)} %collective-permute-done.1.refs_2_, ...), custom_call_target="tpu_custom_call" | custom-call | bytes 5000000 | tf_op jit(solution)/shard_map/pallas_call | solution.py:126
  86.7 1.9 %collective-permute-start.3 = (bf16[4,320,448]{2,1,0:T(8,128)(2,1)}, bf16[4,320,448]{2,1,0:T(8,128)(2,1)}, u32[]{:S(2)}, u32[]{:S(2)}) collective-permute-start(bf16[4,320,448]{2,1,0:T(8,128)(2,1)} %get-tuple-element.28), channel_id=1, source_target_pairs={{0,1},{1,0},{2,3},{3,2},{4,5},{5,4},{6,7},{7,6},{8,9},{9,8},{10,11... | collective-permute-start | bytes 3440648 | tf_op jit(solution)/shard_map/ppermute | solution.py:352
  88.7 0.1 reshape.63
  88.7 0.0 copy-done
  88.7 0.4 convolution_bitcast_fusion.mixed_ref
  89.2 1.0 shard_map.101
  90.2 5.0 %all-to-all-start.1 = ((bf16[16,2,64,128]{3,2,1,0:T(8,128)(2,1)}), bf16[16,2,64,128]{3,2,1,0:T(8,128)(2,1)S(1)}, u32[]{:S(2)}, u32[]{:S(2)}) async-start(bf16[16,2,64,128]{3,2,1,0:T(8,128)(2,1)} %shard_map.101), calls=%async_computation.1 | async-start | bytes 1048576 | tf_op jit(solution)/shard_map/all_to_all | solution.py:338
  95.2 0.0 collective-permute-done.3.near_ref
  95.2 0.0 all-gather.3.cloned.1.call-done
  95.3 3.7 %shard_map.105 = bf16[8,64,448]{2,1,0:T(8,128)(2,1)} custom-call(s32[3]{0:T(128)} %pad_add_fusion.place_ref, bf16[8,128,1024]{2,1,0:T(8,128)(2,1)} %bitcast.24, bf16[4,320,448]{2,1,0:T(8,128)(2,1)} %get-tuple-element.27.mine_ref, bf16[4,320,448]{2,1,0:T(8,128)(2,1)} %collective-permute-done.3.near_ref), custom_call_target="tpu_custom_call" | custom-call | flops 469762048 | bytes 4000000 | tf_op jit(solution)/shard_map/pallas_call | solution.py:158
  99.0 2.0 %collective-permute-start.4 = (bf16[8,64,448]{2,1,0:T(8,128)(2,1)}, bf16[8,64,448]{2,1,0:T(8,128)(2,1)S(1)}, u32[]{:S(2)}, u32[]{:S(2)}) collective-permute-start(bf16[8,64,448]{2,1,0:T(8,128)(2,1)} %shard_map.105), channel_id=1, source_target_pairs={{0,8},{1,9},{2,10},{3,11},{4,12},{5,13},{6,14},{7,15},{8,0},{9,1},... | collective-permute-start | bytes 1376264 | tf_op jit(solution)/shard_map/ppermute | solution.py:354
  101.0 3.7 %all-to-all-done.1.shares_ref = bf16[16,2,64,128]{3,2,1,0:T(8,128)(2,1)S(1)} async-done(((bf16[16,2,64,128]{3,2,1,0:T(8,128)(2,1)}), bf16[16,2,64,128]{3,2,1,0:T(8,128)(2,1)S(1)}, u32[]{:S(2)}, u32[]{:S(2)}) %all-to-all-start.1) | async-done | bytes 524320 | tf_op jit(solution)/shard_map/all_to_all | solution.py:338
  104.7 0.7 shard_map.102
  105.5 3.4 %all-to-all-start.2 = ((bf16[8,64,128]{2,1,0:T(8,128)(2,1)}), bf16[8,64,128]{2,1,0:T(8,128)(2,1)S(1)}, u32[]{:S(2)}, u32[]{:S(2)}) async-start(bf16[8,64,128]{2,1,0:T(8,128)(2,1)} %shard_map.102), calls=%async_computation.2 | async-start | bytes 262144 | tf_op jit(solution)/shard_map/all_to_all | solution.py:341
  108.8 3.8 %shard_map.104.kept_ref = f32[8,64,448]{2,1,0:T(8,128)} custom-call(s32[3]{0:T(128)} %pad_add_fusion.place_ref, bf16[8,128,1024]{2,1,0:T(8,128)(2,1)} %bitcast.25, bf16[4,320,448]{2,1,0:T(8,128)(2,1)} %get-tuple-element.27.mine_ref, bf16[4,320,448]{2,1,0:T(8,128)(2,1)} %collective-permute-done.3.near_ref), custom_call_target="tpu_custom_call" | custom-call | flops 469762048 | bytes 4000000 | tf_op jit(solution)/shard_map/pallas_call | solution.py:158
  112.7 0.0 copy-start.2
  112.7 3.9 %collective-permute-done.4.far_ref = bf16[8,64,448]{2,1,0:T(8,128)(2,1)S(1)} collective-permute-done((bf16[8,64,448]{2,1,0:T(8,128)(2,1)}, bf16[8,64,448]{2,1,0:T(8,128)(2,1)S(1)}, u32[]{:S(2)}, u32[]{:S(2)}) %collective-permute-start.4) | collective-permute-done | bytes 458784 | tf_op jit(solution)/shard_map/ppermute | solution.py:354
  116.6 0.0 copy-start.4
  116.6 0.8 copy-done.4
  117.4 0.0 copy-start.7
  117.4 4.4 %shard_map.106 = bf16[8,64,448]{2,1,0:T(8,128)(2,1)} custom-call(s32[3]{0:T(128)} %pad_add_fusion.place_ref, f32[8,64,448]{2,1,0:T(8,128)} %shard_map.104.kept_ref, bf16[8,64,448]{2,1,0:T(8,128)(2,1)} %copy-done.4, bf16[4,320,448]{2,1,0:T(8,128)(2,1)} %get-tuple-element.27.mine_ref, bf16[4,320,448]{2,1,0:T(8,128)(2,1)} %collective-permute-done.3.near_ref), custom_call_target="tpu_custom_call" | custom-call | flops 4587520 | bytes 5000000 | tf_op jit(solution)/shard_map/pallas_call | solution.py:206
  121.8 0.0 all-to-all-done.2
  121.8 0.0 copy-done.2
  121.8 0.0 copy-start.1
  121.9 1.0 copy-done.1
  122.9 1.0 shard_map.107
  123.9 2.3 %collective-permute-start.5 = (bf16[2,64,224]{2,1,0:T(8,128)(2,1)S(1)}, bf16[2,64,224]{2,1,0:T(8,128)(2,1)S(1)}, u32[]{:S(2)}, u32[]{:S(2)}) collective-permute-start(bf16[2,64,224]{2,1,0:T(8,128)(2,1)S(1)} %get-tuple-element.30), channel_id=1, source_target_pairs={{0,8},{1,9},{2,10},{3,11},{4,12},{5,13},{6,14},{7,15},{8,0},{9,1},... | collective-permute-start | bytes 172040 | tf_op jit(solution)/shard_map/ppermute | solution.py:359
  126.2 5.4 %collective-permute-done.5 = bf16[2,64,224]{2,1,0:T(8,128)(2,1)S(1)} collective-permute-done((bf16[2,64,224]{2,1,0:T(8,128)(2,1)S(1)}, bf16[2,64,224]{2,1,0:T(8,128)(2,1)S(1)}, u32[]{:S(2)}, u32[]{:S(2)}) %collective-permute-start.5) | collective-permute-done | bytes 57376 | tf_op jit(solution)/shard_map/ppermute | solution.py:359
  131.6 0.7 reshape.67
  132.2 4.6 %all-to-all-start.3 = ((bf16[64,2,224]{2,1,0:T(2,128)(2,1)}), bf16[64,2,224]{2,1,0:T(2,128)(2,1)S(1)}, u32[]{:S(2)}, u32[]{:S(2)}) async-start(bf16[64,2,224]{2,1,0:T(2,128)(2,1)} %reshape.67), calls=%async_computation.3 | async-start | bytes 131072 | tf_op jit(solution)/shard_map/all_to_all | solution.py:361
  136.8 0.1 reduce_sum.21
  136.9 24.4 %all-to-all-done.3 = bf16[64,2,224]{2,1,0:T(2,128)(2,1)S(1)} async-done(((bf16[64,2,224]{2,1,0:T(2,128)(2,1)}), bf16[64,2,224]{2,1,0:T(2,128)(2,1)S(1)}, u32[]{:S(2)}, u32[]{:S(2)}) %all-to-all-start.3) | async-done | bytes 57376 | tf_op jit(solution)/shard_map/all_to_all | solution.py:361
  161.3 0.1 reshape.68
  161.4 0.0 copy-done.7
  161.4 0.8 fusion
  (4 shorter events, 0.1 us)
Async XLA Ops:
  6.5 82.2 %copy-start = (bf16[1,224,2,1024]{3,2,1,0:T(2,128)(2,1)S(1)}, bf16[1,224,2,1024]{3,2,1,0:T(2,128)(2,1)}, u32[]{:S(2)}) copy-start(bf16[1,224,2,1024]{3,2,1,0:T(2,128)(2,1)} %param.16) | copy-start | bytes 2752516
  6.5 88.7 %all-gather.3.cloned.1.call-start = ((), (), s32[]{:S(2)}) async-start(), calls=%async_computation.4 | async-start | bytes 2359296 | tf_op jit(solution)/shard_map/all_gather | solution.py:301
  7.8 17.3 %copy-start.5 = (s32[8,8]{1,0:T(8,128)S(1)}, s32[8,8]{1,0:T(8,128)}, u32[]{:S(2)}) copy-start(s32[8,8]{1,0:T(8,128)} %param.18) | copy-start | bytes 772
  7.8 17.8 %copy-start.6 = (bf16[8,224]{1,0:T(8,128)(2,1)S(1)}, bf16[8,224]{1,0:T(8,128)(2,1)}, u32[]{:S(2)}) copy-start(bf16[8,224]{1,0:T(8,128)(2,1)} %param.17) | copy-start | bytes 10756
  13.6 67.2 %collective-permute-start = (bf16[320,896]{1,0:T(8,128)(2,1)}, bf16[320,896]{1,0:T(8,128)(2,1)S(1)}, u32[]{:S(2)}, u32[]{:S(2)}) collective-permute-start(bf16[320,896]{1,0:T(8,128)(2,1)} %get-tuple-element.19), channel_id=1, source_target_pairs={{0,2},{1,3},{2,4},{3,5},{4,6},{5,7},{6,0},{7,1},{8,10},{9,11},{10,... | collective-permute-start | bytes 1720328 | tf_op jit(solution)/shard_map/ppermute | solution.py:304
  17.1 63.7 %collective-permute-start.1 = (bf16[320,896]{1,0:T(8,128)(2,1)}, bf16[320,896]{1,0:T(8,128)(2,1)}, u32[]{:S(2)}, u32[]{:S(2)}) collective-permute-start(bf16[320,896]{1,0:T(8,128)(2,1)} %get-tuple-element.20), channel_id=1, source_target_pairs={{0,4},{1,5},{2,6},{3,7},{4,0},{5,1},{6,2},{7,3},{8,12},{9,13},{10,... | collective-permute-start | bytes 1720328 | tf_op jit(solution)/shard_map/ppermute | solution.py:304
  21.9 58.9 %collective-permute-start.2 = (bf16[320,896]{1,0:T(8,128)(2,1)}, bf16[320,896]{1,0:T(8,128)(2,1)}, u32[]{:S(2)}, u32[]{:S(2)}) collective-permute-start(bf16[320,896]{1,0:T(8,128)(2,1)} %get-tuple-element.21), channel_id=1, source_target_pairs={{0,6},{1,7},{2,0},{3,1},{4,2},{5,3},{6,4},{7,5},{8,14},{9,15},{10,... | collective-permute-start | bytes 1720328 | tf_op jit(solution)/shard_map/ppermute | solution.py:304
  80.8 0.8 copy-start.3
  86.7 8.5 %collective-permute-start.3 = (bf16[4,320,448]{2,1,0:T(8,128)(2,1)}, bf16[4,320,448]{2,1,0:T(8,128)(2,1)}, u32[]{:S(2)}, u32[]{:S(2)}) collective-permute-start(bf16[4,320,448]{2,1,0:T(8,128)(2,1)} %get-tuple-element.28), channel_id=1, source_target_pairs={{0,1},{1,0},{2,3},{3,2},{4,5},{5,4},{6,7},{7,6},{8,9},{9,8},{10,11... | collective-permute-start | bytes 3440648 | tf_op jit(solution)/shard_map/ppermute | solution.py:352
  90.2 14.5 %all-to-all-start.1 = ((bf16[16,2,64,128]{3,2,1,0:T(8,128)(2,1)}), bf16[16,2,64,128]{3,2,1,0:T(8,128)(2,1)S(1)}, u32[]{:S(2)}, u32[]{:S(2)}) async-start(bf16[16,2,64,128]{3,2,1,0:T(8,128)(2,1)} %shard_map.101), calls=%async_computation.1 | async-start | bytes 1048576 | tf_op jit(solution)/shard_map/all_to_all | solution.py:338
  99.0 17.6 %collective-permute-start.4 = (bf16[8,64,448]{2,1,0:T(8,128)(2,1)}, bf16[8,64,448]{2,1,0:T(8,128)(2,1)S(1)}, u32[]{:S(2)}, u32[]{:S(2)}) collective-permute-start(bf16[8,64,448]{2,1,0:T(8,128)(2,1)} %shard_map.105), channel_id=1, source_target_pairs={{0,8},{1,9},{2,10},{3,11},{4,12},{5,13},{6,14},{7,15},{8,0},{9,1},... | collective-permute-start | bytes 1376264 | tf_op jit(solution)/shard_map/ppermute | solution.py:354
  105.5 16.4 %all-to-all-start.2 = ((bf16[8,64,128]{2,1,0:T(8,128)(2,1)}), bf16[8,64,128]{2,1,0:T(8,128)(2,1)S(1)}, u32[]{:S(2)}, u32[]{:S(2)}) async-start(bf16[8,64,128]{2,1,0:T(8,128)(2,1)} %shard_map.102), calls=%async_computation.2 | async-start | bytes 262144 | tf_op jit(solution)/shard_map/all_to_all | solution.py:341
  112.7 9.1 %copy-start.2 = (s32[3]{0:T(128)S(1)}, s32[3]{0:T(128)}, u32[]{:S(2)}) copy-start(s32[3]{0:T(128)} %pad_add_fusion.place_ref) | copy-start | bytes 40
  116.6 0.8 copy-start.4
  117.4 44.0 %copy-start.7 = (f32[8,8]{1,0:T(8,128)S(1)}, f32[8,8]{1,0:T(8,128)}, u32[]{:S(2)}) copy-start(f32[8,8]{1,0:T(8,128)} %param.19) | copy-start | bytes 772
  121.8 1.0 copy-start.1
  123.9 7.7 %collective-permute-start.5 = (bf16[2,64,224]{2,1,0:T(8,128)(2,1)S(1)}, bf16[2,64,224]{2,1,0:T(8,128)(2,1)S(1)}, u32[]{:S(2)}, u32[]{:S(2)}) collective-permute-start(bf16[2,64,224]{2,1,0:T(8,128)(2,1)S(1)} %get-tuple-element.30), channel_id=1, source_target_pairs={{0,8},{1,9},{2,10},{3,11},{4,12},{5,13},{6,14},{7,15},{8,0},{9,1},... | collective-permute-start | bytes 172040 | tf_op jit(solution)/shard_map/ppermute | solution.py:359
  132.2 29.1 %all-to-all-start.3 = ((bf16[64,2,224]{2,1,0:T(2,128)(2,1)}), bf16[64,2,224]{2,1,0:T(2,128)(2,1)S(1)}, u32[]{:S(2)}, u32[]{:S(2)}) async-start(bf16[64,2,224]{2,1,0:T(2,128)(2,1)} %reshape.67), calls=%async_computation.3 | async-start | bytes 131072 | tf_op jit(solution)/shard_map/all_to_all | solution.py:361
Sparse Core Ops, SparseCore 0:
  10.1 50.5 all-gather.2

commit v5 on v4

--- a/solution.py
+++ b/solution.py
@@ -20,6 +20,7 @@
 SMEM = pl.BlockSpec(memory_space=pltpu.SMEM)
 VMEM = pl.BlockSpec(memory_space=pltpu.VMEM)
 PARAMS = pltpu.CompilerParams(vmem_limit_bytes=62 * 2**20)
+FINISH = pltpu.CompilerParams(vmem_limit_bytes=60 * 2**20)
 SMALL = pltpu.CompilerParams(vmem_limit_bytes=24 * 2**20)
 
 
@@ -59,6 +60,7 @@
         .astype(jnp.float32)
         .astype(jnp.bfloat16)
     )
+    selected = contract_first(onehot, grad_ref[...]).astype(jnp.bfloat16)
     ring = place_ref[1]
     for here in range(RING):
         for piece in range(PIECES):
@@ -71,9 +73,7 @@
                     out = outs[(place - here) % RING]
                     take = pl.ds(local * width, width)
                     put = pl.ds((owner % CORES * HALVES + half) * width, width)
-                    out[0:tokens, put] = contract_first(onehot, grad_ref[:, take]).astype(
-                        jnp.bfloat16
-                    )
+                    out[0:tokens, put] = selected[:, local * width : (local + 1) * width]
                     at = tokens
                     out[at : at + rows, put] = master_ref[0, :, take].astype(jnp.bfloat16)
                     out[at + rows : at + 2 * rows, put] = first_ref[0, :, take]
@@ -122,7 +122,7 @@
 
 def split_cores(place, parts):
     rows, width = parts[0].shape
-    block = 64
+    block = rows // 2
     return pl.pallas_call(
         core_kernel,
         grid=(rows // block,),
@@ -182,8 +182,11 @@
     )(place, acts.reshape(sources, tokens, units), mine, near)
 
 
-def adam_kernel(tokens, place_ref, kept_ref, far_ref, mine_ref, near_ref, tile_ref):
+def finish_kernel(
+    tokens, place_ref, kept_ref, far_ref, mine_ref, near_ref, hidden_ref, own_ref, cross_ref, sums
+):
     rows = kept_ref.shape[1]
+    total = None
     for step, states in enumerate((mine_ref, near_ref)):
         core = jnp.bitwise_xor(place_ref[2], step)
         gradient = kept_ref[core] + far_ref[core].astype(jnp.float32)
@@ -194,24 +197,53 @@
         first = beta_one * first_old + (1.0 - beta_one) * gradient
         second = beta_two * second_old + (1.0 - beta_two) * gradient * gradient
         update = first / bias_first / (jnp.sqrt(second / bias_second) + epsilon)
-        tile_ref[core] = (
-            master * (1.0 - learn_rate * weight_decay) - learn_rate * update
-        ).astype(jnp.bfloat16)
-
-
-def adam_tile(tokens, place, kept, far, mine, near):
-    sources, rows, width = kept.shape
+        tile = (master * (1.0 - learn_rate * weight_decay) - learn_rate * update).astype(
+            jnp.bfloat16
+        )
+        product = contract_first(hidden_ref[core], tile)
+        total = product if total is None else total + product
+
+    @pl.when(pl.program_id(0) == 0)
+    def _():
+        sums[...] = total
+
+    @pl.when(pl.program_id(0) > 0)
+    def _():
+        sums[...] += total
+
+    @pl.when(pl.program_id(0) == RING - 1)
+    def _():
+        own, cross = split(place_ref[0], sums[...])
+        own_ref[...] = own.reshape(own_ref.shape)
+        cross_ref[...] = cross.astype(jnp.bfloat16).reshape(cross_ref.shape)
+
+
+def finish(tokens, place, kept, far, mine, near, hidden):
+    _, rows, width = kept.shape
+    slots = hidden.shape[2]
+    shape = (2, slots // 2, width // 2)
     pair = pl.BlockSpec((CORES, rows, width), lambda i: (i, 0, 0))
     states = pl.BlockSpec((1, mine.shape[1], width), lambda i: (i, 0, 0))
     return pl.pallas_call(
-        functools.partial(adam_kernel, tokens),
+        functools.partial(finish_kernel, tokens),
         grid=(RING,),
-        out_shape=jax.ShapeDtypeStruct(kept.shape, jnp.bfloat16),
-        in_specs=[SMEM, pair, pair, states, states],
-        out_specs=pair,
-        compiler_params=PARAMS,
+        out_shape=[
+            jax.ShapeDtypeStruct(shape, jnp.float32),
+            jax.ShapeDtypeStruct(shape, jnp.bfloat16),
+        ],
+        in_specs=[
+            SMEM,
+            pair,
+            pair,
+            states,
+            states,
+            pl.BlockSpec((CORES, rows, slots), lambda i: (i, 0, 0)),
+        ],
+        out_specs=[whole(*shape)] * 2,
+        scratch_shapes=[pltpu.VMEM((slots, width), jnp.float32)],
+        compiler_params=FINISH,
         cost_estimate=cost(20 * kept.size, 5_000_000),
-    )(place, kept, far, mine, near)
+    )(place, kept, far, mine, near, hidden)
 
 
 def turn_kernel(mixed_ref, out_ref):
@@ -254,28 +286,6 @@
         compiler_params=SMALL,
         cost_estimate=cost(shares.size, 800_000),
     )(shares)
-
-
-def results_kernel(place_ref, hidden_ref, tile_ref, kept_ref, cross_ref):
-    total = contract_first(hidden_ref[...], tile_ref[...])
-    kept, cross = split(place_ref[0], total)
-    kept_ref[...] = kept.reshape(kept_ref.shape)
-    cross_ref[...] = cross.astype(jnp.bfloat16).reshape(cross_ref.shape)
-
-
-def expert_results(place, hidden, tile):
-    shape = (2, hidden.shape[1] // 2, tile.shape[1] // 2)
-    return pl.pallas_call(
-        results_kernel,
-        out_shape=[
-            jax.ShapeDtypeStruct(shape, jnp.float32),
-            jax.ShapeDtypeStruct(shape, jnp.bfloat16),
-        ],
-        in_specs=[SMEM, VMEM, VMEM],
-        out_specs=[VMEM] * 2,
-        compiler_params=SMALL,
-        cost_estimate=cost(2 * hidden.size * tile.shape[1], 900_000),
-    )(place, hidden, tile)
 
 
 def body(
@@ -345,7 +355,7 @@
         concat_axis=0,
         tiled=True,
         axis_index_groups=sides,
-    ).reshape(-1, slot_count)
+    )
 
     across_cores, across_halves = permutation(0, 0, 1), permutation(1, 0, 0)
     mine, theirs = split_cores(place, held)
@@ -353,9 +363,7 @@
     cross = gradient_rows(place, acts, mine, near, tokens, 1, jnp.bfloat16)
     far = lax.ppermute(cross, "dp", across_halves)
     kept = gradient_rows(place, acts, mine, near, tokens, 0, jnp.float32)
-    tile = adam_tile(tokens, place, kept, far, mine, near)
-
-    kept_results, cross_results = expert_results(place, hidden, tile.reshape(-1, 2 * width))
+    kept_results, cross_results = finish(tokens, place, kept, far, mine, near, hidden)
     far_results = lax.ppermute(cross_results, "dp", across_halves)
     results = (kept_results + far_results.astype(jnp.float32)).astype(jnp.bfloat16)
     returned = lax.all_to_all(

time: 170 us -> 168 us (0.988)
  the two profiles are of different devices: /device:TPU:4 before, /device:TPU:8 now
where the time goes in v5:
time: 168 us; the launch traced here: 167 us
  starting transfers between devices  49.2 us (29%)
  blocking collectives  44.8 us (27%)
  waiting for transfers between devices  30.3 us (18%)
  Pallas kernels  22.9 us (14%)
  between operations  13.6 us (8%)
  local copies, waits for them, and re-layouts  3.19 us (2%)
  other arithmetic  1.89 us (1%)
    all_to_all x1, blocking collectives, body(): lax.all_to_all(outgoing.reshape(expert_count, capacity, width), 'exp', sp...  44.8 us
    all_to_all x1, waiting for transfers between devices, body(): lax.all_to_all(results.reshape(expert_count, capacity, width), 'exp', spl...  25 us
    ppermute x3, starting transfers between devices, body(): lax.ppermute(sends[step], 'dp', permutation(0, step, 0))  20.9 us
    pallas_call x2, Pallas kernels, gradient_rows(): pl.pallas_call(gradient_kernel, out_shape=jax.ShapeDtypeStruct((sources,...  7.63 us
    all_to_all x1, starting transfers between devices, body(): lax.all_to_all(hidden_units(shares, RING * CORES), 'dp', split_axis=0, co...  6.93 us
    pallas_call x1, Pallas kernels, pack(): pl.pallas_call(pack_kernel, grid=(PIECES,), out_shape=[jax.ShapeDtypeStru...  5.73 us
    all_to_all x1, starting transfers between devices, body(): lax.all_to_all(turn(mixed, shards), 'dp', split_axis=0, concat_axis=0, ti...  5.59 us
    ppermute x1, starting transfers between devices, body(): far = lax.ppermute(cross, 'dp', across_halves)  4.86 us
  transfers between devices with their start and end apart: 10, of which 5 were waited for; matrix products, arithmetic and copies ran while one was open for 1% of the time, Pallas kernels for 11%

profile of v5, /device:TPU:8, one launch (start us, length us, event | category | flops | bytes accessed | tf_op | source)
XLA Modules:
  0.0 167.4 jit_solution(15116025200380378790)
XLA Ops:
  6.5 0.0 copy-start
  6.5 0.0 all-gather.3.cloned.1.call-start
  6.5 0.7 all-gather.3.cloned.1.call-update
  7.3 0.6 pad_add_fusion.place_ref
  7.9 0.0 copy-start.4
  7.9 0.0 copy-start.5
  7.9 5.7 %shard_map.100 = (bf16[320,896]{1,0:T(8,128)(2,1)}, bf16[320,896]{1,0:T(8,128)(2,1)}, bf16[320,896]{1,0:T(8,128)(2,1)}, bf16[320,896]{1,0:T(8,128)(2,1)}) custom-call(s32[3]{0:T(128)} %pad_add_fusion.place_ref, s32[1,128]{1,0:T(1,128)} %rows_ref.1, bf16[256,3584]{1,0:T(8,128)(2,1)} %grad_ref.1, f32[1,64,3584]{2,1,0:T(8,128)} %master_ref.1, ...), custom_call_target="tpu_custom_call" | custom-call | flops 234881024 | bytes 7000000 | tf_op jit(solution)/shard_map/pallas_call | solution.py:89
  13.6 3.5 %collective-permute-start = (bf16[320,896]{1,0:T(8,128)(2,1)}, bf16[320,896]{1,0:T(8,128)(2,1)S(1)}, u32[]{:S(2)}, u32[]{:S(2)}) collective-permute-start(bf16[320,896]{1,0:T(8,128)(2,1)} %get-tuple-element.19), channel_id=1, source_target_pairs={{0,2},{1,3},{2,4},{3,5},{4,6},{5,7},{6,0},{7,1},{8,10},{9,11},{10,... | collective-permute-start | bytes 1720328 | tf_op jit(solution)/shard_map/ppermute | solution.py:314
  17.1 15.5 %collective-permute-start.1 = (bf16[320,896]{1,0:T(8,128)(2,1)}, bf16[320,896]{1,0:T(8,128)(2,1)}, u32[]{:S(2)}, u32[]{:S(2)}) collective-permute-start(bf16[320,896]{1,0:T(8,128)(2,1)} %get-tuple-element.20), channel_id=1, source_target_pairs={{0,4},{1,5},{2,6},{3,7},{4,0},{5,1},{6,2},{7,3},{8,12},{9,13},{10,... | collective-permute-start | bytes 1720328 | tf_op jit(solution)/shard_map/ppermute | solution.py:314
  32.6 1.9 %collective-permute-start.2 = (bf16[320,896]{1,0:T(8,128)(2,1)}, bf16[320,896]{1,0:T(8,128)(2,1)}, u32[]{:S(2)}, u32[]{:S(2)}) collective-permute-start(bf16[320,896]{1,0:T(8,128)(2,1)} %get-tuple-element.21), channel_id=1, source_target_pairs={{0,6},{1,7},{2,0},{3,1},{4,2},{5,3},{6,4},{7,5},{8,14},{9,15},{10,... | collective-permute-start | bytes 1720328 | tf_op jit(solution)/shard_map/ppermute | solution.py:314
  34.6 0.0 copy-done.4
  34.6 0.1 eq.50
  34.6 0.1 fusion.5
  34.7 0.1 reduce_window_sum.11
  34.8 0.2 select_reduce_fusion
  35.0 0.0 copy-done.5
  35.0 0.2 convolution_convert_fusion
  35.3 0.1 copy.13
  35.4 44.8 %all_to_all.20 = bf16[64,2,224]{2,1,0:T(2,128)(2,1)S(1)} all-to-all(bf16[64,2,224]{2,1,0:T(2,128)(2,1)S(1)} %reshape.57), channel_id=1, replica_groups=mesh['exp'=64,'dp'=16] {'exp'}, dimensions={0} | all-to-all | bytes 114688 | tf_op jit(solution)/shard_map/all_to_all | solution.py:335
  80.2 0.0 collective-permute-done.refs_1_
  80.2 0.0 copy-start.1
  80.2 0.0 collective-permute-done.1.refs_2_
  80.2 0.0 collective-permute-done.2.refs_3_
  80.2 0.8 copy-done.1
  81.0 3.1 %shard_map.101 = (bf16[4,320,448]{2,1,0:T(8,128)(2,1)}, bf16[4,320,448]{2,1,0:T(8,128)(2,1)}) custom-call(s32[3]{0:T(128)} %pad_add_fusion.place_ref, bf16[320,896]{1,0:T(8,128)(2,1)} %get-tuple-element.22.refs_0_, bf16[320,896]{1,0:T(8,128)(2,1)} %copy-done.1, bf16[320,896]{1,0:T(8,128)(2,1)} %collective-permute-done.1.refs_2_, ...), custom_call_target="tpu_custom_call" | custom-call | bytes 5000000 | tf_op jit(solution)/shard_map/pallas_call | solution.py:126
  84.1 1.9 %collective-permute-start.3 = (bf16[4,320,448]{2,1,0:T(8,128)(2,1)}, bf16[4,320,448]{2,1,0:T(8,128)(2,1)}, u32[]{:S(2)}, u32[]{:S(2)}) collective-permute-start(bf16[4,320,448]{2,1,0:T(8,128)(2,1)} %get-tuple-element.27), channel_id=1, source_target_pairs={{0,1},{1,0},{2,3},{3,2},{4,5},{5,4},{6,7},{7,6},{8,9},{9,8},{10,11... | collective-permute-start | bytes 3440648 | tf_op jit(solution)/shard_map/ppermute | solution.py:362
  86.0 0.1 reshape.58
  86.1 0.0 copy-done
  86.1 0.4 convolution_bitcast_fusion.mixed_ref
  86.5 1.0 shard_map.104
  87.5 5.6 %all-to-all-start.1 = ((bf16[16,2,64,128]{3,2,1,0:T(8,128)(2,1)}), bf16[16,2,64,128]{3,2,1,0:T(8,128)(2,1)S(1)}, u32[]{:S(2)}, u32[]{:S(2)}) async-start(bf16[16,2,64,128]{3,2,1,0:T(8,128)(2,1)} %shard_map.104), calls=%async_computation.1 | async-start | bytes 1048576 | tf_op jit(solution)/shard_map/all_to_all | solution.py:348
  93.1 0.0 collective-permute-done.3.near_ref
  93.1 0.0 all-gather.3.cloned.1.call-done
  93.2 3.8 %shard_map.103 = bf16[8,64,448]{2,1,0:T(8,128)(2,1)} custom-call(s32[3]{0:T(128)} %pad_add_fusion.place_ref, bf16[8,128,1024]{2,1,0:T(8,128)(2,1)} %bitcast.20, bf16[4,320,448]{2,1,0:T(8,128)(2,1)} %get-tuple-element.26.mine_ref, bf16[4,320,448]{2,1,0:T(8,128)(2,1)} %collective-permute-done.3.near_ref), custom_call_target="tpu_custom_call" | custom-call | flops 469762048 | bytes 4000000 | tf_op jit(solution)/shard_map/pallas_call | solution.py:158
  96.9 4.9 %collective-permute-start.4 = (bf16[8,64,448]{2,1,0:T(8,128)(2,1)}, bf16[8,64,448]{2,1,0:T(8,128)(2,1)S(1)}, u32[]{:S(2)}, u32[]{:S(2)}) collective-permute-start(bf16[8,64,448]{2,1,0:T(8,128)(2,1)} %shard_map.103), channel_id=1, source_target_pairs={{0,8},{1,9},{2,10},{3,11},{4,12},{5,13},{6,14},{7,15},{8,0},{9,1},... | collective-permute-start | bytes 1376264 | tf_op jit(solution)/shard_map/ppermute | solution.py:364
  101.8 0.1 all-to-all-done.1.shares_ref
  101.9 0.7 shard_map.105
  102.7 6.9 %all-to-all-start.2 = ((bf16[8,64,128]{2,1,0:T(8,128)(2,1)}), bf16[8,64,128]{2,1,0:T(8,128)(2,1)S(1)}, u32[]{:S(2)}, u32[]{:S(2)}) async-start(bf16[8,64,128]{2,1,0:T(8,128)(2,1)} %shard_map.105), calls=%async_computation.2 | async-start | bytes 262144 | tf_op jit(solution)/shard_map/all_to_all | solution.py:351
  109.6 3.9 %shard_map.102.kept_ref = f32[8,64,448]{2,1,0:T(8,128)} custom-call(s32[3]{0:T(128)} %pad_add_fusion.place_ref, bf16[8,128,1024]{2,1,0:T(8,128)(2,1)} %bitcast.21, bf16[4,320,448]{2,1,0:T(8,128)(2,1)} %get-tuple-element.26.mine_ref, bf16[4,320,448]{2,1,0:T(8,128)(2,1)} %collective-permute-done.3.near_ref), custom_call_target="tpu_custom_call" | custom-call | flops 469762048 | bytes 4000000 | tf_op jit(solution)/shard_map/pallas_call | solution.py:158
  113.5 0.0 copy-start.6
  113.5 0.8 all-to-all-done.2.hidden_ref
  114.3 0.0 copy-start.3
  114.3 0.2 collective-permute-done.4.far_ref
  114.5 0.5 copy-done.3
  115.0 0.0 copy-start.2
  115.0 0.8 copy-done.2
  115.8 4.8 %shard_map.106 = (f32[2,64,224]{2,1,0:T(8,128)}, bf16[2,64,224]{2,1,0:T(8,128)(2,1)}) custom-call(s32[3]{0:T(128)} %pad_add_fusion.place_ref, f32[8,64,448]{2,1,0:T(8,128)} %shard_map.102.kept_ref, bf16[8,64,448]{2,1,0:T(8,128)(2,1)} %copy-done.2, bf16[4,320,448]{2,1,0:T(8,128)(2,1)} %get-tuple-element.26.mine_ref, ...), custom_call_target="tpu_custom_call" | custom-call | flops 4587520 | bytes 5000000 | tf_op jit(solution)/shard_map/pallas_call | solution.py:227
  120.5 4.4 %collective-permute-start.5 = (bf16[2,64,224]{2,1,0:T(8,128)(2,1)}, bf16[2,64,224]{2,1,0:T(8,128)(2,1)S(1)}, u32[]{:S(2)}, u32[]{:S(2)}) collective-permute-start(bf16[2,64,224]{2,1,0:T(8,128)(2,1)} %get-tuple-element.30), channel_id=1, source_target_pairs={{0,8},{1,9},{2,10},{3,11},{4,12},{5,13},{6,14},{7,15},{8,0},{9,1},... | collective-permute-start | bytes 172040 | tf_op jit(solution)/shard_map/ppermute | solution.py:367
  125.0 3.5 %collective-permute-done.5 = bf16[2,64,224]{2,1,0:T(8,128)(2,1)S(1)} collective-permute-done((bf16[2,64,224]{2,1,0:T(8,128)(2,1)}, bf16[2,64,224]{2,1,0:T(8,128)(2,1)S(1)}, u32[]{:S(2)}, u32[]{:S(2)}) %collective-permute-start.5) | collective-permute-done | bytes 57376 | tf_op jit(solution)/shard_map/ppermute | solution.py:367
  128.4 0.9 add_convert_fusion
  129.3 0.7 reshape.59
  130.0 4.6 %all-to-all-start.3 = ((bf16[64,2,224]{2,1,0:T(2,128)(2,1)}), bf16[64,2,224]{2,1,0:T(2,128)(2,1)S(1)}, u32[]{:S(2)}, u32[]{:S(2)}) async-start(bf16[64,2,224]{2,1,0:T(2,128)(2,1)} %reshape.59), calls=%async_computation.3 | async-start | bytes 131072 | tf_op jit(solution)/shard_map/all_to_all | solution.py:369
  134.6 0.1 reduce_sum.21
  134.7 25.0 %all-to-all-done.3 = bf16[64,2,224]{2,1,0:T(2,128)(2,1)S(1)} async-done(((bf16[64,2,224]{2,1,0:T(2,128)(2,1)}), bf16[64,2,224]{2,1,0:T(2,128)(2,1)S(1)}, u32[]{:S(2)}, u32[]{:S(2)}) %all-to-all-start.3) | async-done | bytes 57376 | tf_op jit(solution)/shard_map/all_to_all | solution.py:369
  159.7 0.1 reshape.60
  159.7 0.0 copy-done.6
  159.7 0.8 fusion
  (3 shorter events, 0.1 us)
Async XLA Ops:
  6.5 79.5 %copy-start = (bf16[1,224,2,1024]{3,2,1,0:T(2,128)(2,1)S(1)}, bf16[1,224,2,1024]{3,2,1,0:T(2,128)(2,1)}, u32[]{:S(2)}) copy-start(bf16[1,224,2,1024]{3,2,1,0:T(2,128)(2,1)} %param.16) | copy-start | bytes 2752516
  6.5 86.6 %all-gather.3.cloned.1.call-start = ((), (), s32[]{:S(2)}) async-start(), calls=%async_computation.4 | async-start | bytes 2359296 | tf_op jit(solution)/shard_map/all_gather | solution.py:311
  7.9 26.7 %copy-start.4 = (s32[8,8]{1,0:T(8,128)S(1)}, s32[8,8]{1,0:T(8,128)}, u32[]{:S(2)}) copy-start(s32[8,8]{1,0:T(8,128)} %param.18) | copy-start | bytes 772
  7.9 27.1 %copy-start.5 = (bf16[8,224]{1,0:T(8,128)(2,1)S(1)}, bf16[8,224]{1,0:T(8,128)(2,1)}, u32[]{:S(2)}) copy-start(bf16[8,224]{1,0:T(8,128)(2,1)} %param.17) | copy-start | bytes 10756
  13.6 66.6 %collective-permute-start = (bf16[320,896]{1,0:T(8,128)(2,1)}, bf16[320,896]{1,0:T(8,128)(2,1)S(1)}, u32[]{:S(2)}, u32[]{:S(2)}) collective-permute-start(bf16[320,896]{1,0:T(8,128)(2,1)} %get-tuple-element.19), channel_id=1, source_target_pairs={{0,2},{1,3},{2,4},{3,5},{4,6},{5,7},{6,0},{7,1},{8,10},{9,11},{10,... | collective-permute-start | bytes 1720328 | tf_op jit(solution)/shard_map/ppermute | solution.py:314
  17.1 63.1 %collective-permute-start.1 = (bf16[320,896]{1,0:T(8,128)(2,1)}, bf16[320,896]{1,0:T(8,128)(2,1)}, u32[]{:S(2)}, u32[]{:S(2)}) collective-permute-start(bf16[320,896]{1,0:T(8,128)(2,1)} %get-tuple-element.20), channel_id=1, source_target_pairs={{0,4},{1,5},{2,6},{3,7},{4,0},{5,1},{6,2},{7,3},{8,12},{9,13},{10,... | collective-permute-start | bytes 1720328 | tf_op jit(solution)/shard_map/ppermute | solution.py:314
  32.6 47.6 %collective-permute-start.2 = (bf16[320,896]{1,0:T(8,128)(2,1)}, bf16[320,896]{1,0:T(8,128)(2,1)}, u32[]{:S(2)}, u32[]{:S(2)}) collective-permute-start(bf16[320,896]{1,0:T(8,128)(2,1)} %get-tuple-element.21), channel_id=1, source_target_pairs={{0,6},{1,7},{2,0},{3,1},{4,2},{5,3},{6,4},{7,5},{8,14},{9,15},{10,... | collective-permute-start | bytes 1720328 | tf_op jit(solution)/shard_map/ppermute | solution.py:314
  80.2 0.8 copy-start.1
  84.1 9.0 %collective-permute-start.3 = (bf16[4,320,448]{2,1,0:T(8,128)(2,1)}, bf16[4,320,448]{2,1,0:T(8,128)(2,1)}, u32[]{:S(2)}, u32[]{:S(2)}) collective-permute-start(bf16[4,320,448]{2,1,0:T(8,128)(2,1)} %get-tuple-element.27), channel_id=1, source_target_pairs={{0,1},{1,0},{2,3},{3,2},{4,5},{5,4},{6,7},{7,6},{8,9},{9,8},{10,11... | collective-permute-start | bytes 3440648 | tf_op jit(solution)/shard_map/ppermute | solution.py:362
  87.5 14.4 %all-to-all-start.1 = ((bf16[16,2,64,128]{3,2,1,0:T(8,128)(2,1)}), bf16[16,2,64,128]{3,2,1,0:T(8,128)(2,1)S(1)}, u32[]{:S(2)}, u32[]{:S(2)}) async-start(bf16[16,2,64,128]{3,2,1,0:T(8,128)(2,1)} %shard_map.104), calls=%async_computation.1 | async-start | bytes 1048576 | tf_op jit(solution)/shard_map/all_to_all | solution.py:348
  96.9 17.6 %collective-permute-start.4 = (bf16[8,64,448]{2,1,0:T(8,128)(2,1)}, bf16[8,64,448]{2,1,0:T(8,128)(2,1)S(1)}, u32[]{:S(2)}, u32[]{:S(2)}) collective-permute-start(bf16[8,64,448]{2,1,0:T(8,128)(2,1)} %shard_map.103), channel_id=1, source_target_pairs={{0,8},{1,9},{2,10},{3,11},{4,12},{5,13},{6,14},{7,15},{8,0},{9,1},... | collective-permute-start | bytes 1376264 | tf_op jit(solution)/shard_map/ppermute | solution.py:364
  102.7 11.6 %all-to-all-start.2 = ((bf16[8,64,128]{2,1,0:T(8,128)(2,1)}), bf16[8,64,128]{2,1,0:T(8,128)(2,1)S(1)}, u32[]{:S(2)}, u32[]{:S(2)}) async-start(bf16[8,64,128]{2,1,0:T(8,128)(2,1)} %shard_map.105), calls=%async_computation.2 | async-start | bytes 262144 | tf_op jit(solution)/shard_map/all_to_all | solution.py:351
  113.5 46.3 %copy-start.6 = (f32[8,8]{1,0:T(8,128)S(1)}, f32[8,8]{1,0:T(8,128)}, u32[]{:S(2)}) copy-start(f32[8,8]{1,0:T(8,128)} %param.19) | copy-start | bytes 772
  114.3 0.7 copy-start.3
  115.0 0.8 copy-start.2
  120.5 7.9 %collective-permute-start.5 = (bf16[2,64,224]{2,1,0:T(8,128)(2,1)}, bf16[2,64,224]{2,1,0:T(8,128)(2,1)S(1)}, u32[]{:S(2)}, u32[]{:S(2)}) collective-permute-start(bf16[2,64,224]{2,1,0:T(8,128)(2,1)} %get-tuple-element.30), channel_id=1, source_target_pairs={{0,8},{1,9},{2,10},{3,11},{4,12},{5,13},{6,14},{7,15},{8,0},{9,1},... | collective-permute-start | bytes 172040 | tf_op jit(solution)/shard_map/ppermute | solution.py:367
  130.0 29.7 %all-to-all-start.3 = ((bf16[64,2,224]{2,1,0:T(2,128)(2,1)}), bf16[64,2,224]{2,1,0:T(2,128)(2,1)S(1)}, u32[]{:S(2)}, u32[]{:S(2)}) async-start(bf16[64,2,224]{2,1,0:T(2,128)(2,1)} %reshape.59), calls=%async_computation.3 | async-start | bytes 131072 | tf_op jit(solution)/shard_map/all_to_all | solution.py:369
Sparse Core Ops, SparseCore 0:
  10.1 50.8 all-gather.2

commit v6 on v5

--- a/solution.py
+++ b/solution.py
@@ -16,7 +16,7 @@
 bias_second = 1.0 - 0.95**20
 
 HALVES, RING, CORES = 2, 4, 2
-PIECES = 4
+PIECES = 2
 SMEM = pl.BlockSpec(memory_space=pltpu.SMEM)
 VMEM = pl.BlockSpec(memory_space=pltpu.VMEM)
 PARAMS = pltpu.CompilerParams(vmem_limit_bytes=62 * 2**20)
@@ -49,7 +49,7 @@
     return pairs
 
 
-def pack_kernel(place_ref, rows_ref, grad_ref, master_ref, first_ref, second_ref, *outs):
+def pack_kernel(rows_ref, grad_ref, master_ref, first_ref, second_ref, *outs):
     table, columns = grad_ref.shape
     tokens = rows_ref.shape[1]
     rows = master_ref.shape[1]
@@ -61,7 +61,7 @@
         .astype(jnp.bfloat16)
     )
     selected = contract_first(onehot, grad_ref[...]).astype(jnp.bfloat16)
-    ring = place_ref[1]
+    ring = lax.axis_index("dp") // CORES % RING
     for here in range(RING):
         for piece in range(PIECES):
 
@@ -80,7 +80,7 @@
                     out[at + 2 * rows : at + 3 * rows, put] = second_ref[0, :, take]
 
 
-def pack(place, train_rows, out_grad, master, moment1, moment2):
+def pack(train_rows, out_grad, master, moment1, moment2):
     tokens = train_rows.shape[1]
     rows = master.shape[1]
     table, columns = out_grad.shape
@@ -91,7 +91,6 @@
         grid=(PIECES,),
         out_shape=[jax.ShapeDtypeStruct(shape, jnp.bfloat16)] * RING,
         in_specs=[
-            SMEM,
             whole(1, tokens),
             pl.BlockSpec((table, columns // PIECES), lambda i: (0, i)),
             state,
@@ -101,7 +100,7 @@
         out_specs=[whole(*shape)] * RING,
         compiler_params=PARAMS,
         cost_estimate=cost(2 * tokens * out_grad.size, 7_000_000),
-    )(place, train_rows, out_grad, master, moment1, moment2)
+    )(train_rows, out_grad, master, moment1, moment2)
 
 
 def split(flag, values):
@@ -309,7 +308,7 @@
 
     sides = [[h * RING * CORES + k for k in range(RING * CORES)] for h in range(HALVES)]
     acts = lax.all_gather(hidden_acts[0], "dp", axis=0, tiled=True, axis_index_groups=sides)
-    sends = pack(place, train_rows, out_grad, master, moment1, moment2)
+    sends = pack(train_rows, out_grad, master, moment1, moment2)
     parts = [sends[0]] + [
         lax.ppermute(sends[step], "dp", permutation(0, step, 0)) for step in range(1, RING)
     ]

time: 168 us -> 167 us (level)
  blocking collectives: 44.8 us -> 0 us
  waiting for transfers between devices: 30.3 us -> 54.7 us
  starting transfers between devices: 49.2 us -> 69.2 us
    all_to_all x1 -> x0, blocking collectives: 44.8 us -> none  [body(): lax.all_to_all(outgoing.reshape(expert_count, capacity, width), 'exp', sp...]
    all_to_all x0 -> x1, waiting for transfers between devices: none -> 24.4 us  [body(): lax.all_to_all(outgoing.reshape(expert_count, capacity, width), 'exp', sp...]
    all_to_all x0 -> x1, starting transfers between devices: none -> 20 us  [body(): lax.all_to_all(outgoing.reshape(expert_count, capacity, width), 'exp', sp...]
  transfers between devices with their start and end apart: 10 -> 11, of which waited for: 5 -> 6; matrix products, arithmetic and copies ran while one was open for 1% -> 2% of each run, Pallas kernels for 11% -> 10%
where the time goes in v6:
time: 167 us
  starting transfers between devices  69.2 us (41%)
  waiting for transfers between devices  54.7 us (33%)
  Pallas kernels  22 us (13%)
  between operations  13.6 us (8%)
  local copies, waits for them, and re-layouts  3.85 us (2%)
  other arithmetic  1.87 us (1%)
    all_to_all x1, waiting for transfers between devices, body(): lax.all_to_all(results.reshape(expert_count, capacity, width), 'exp', spl...  25 us
    all_to_all x1, waiting for transfers between devices, body(): lax.all_to_all(outgoing.reshape(expert_count, capacity, width), 'exp', sp...  24.4 us
    ppermute x3, starting transfers between devices, body(): lax.ppermute(sends[step], 'dp', permutation(0, step, 0))  20.9 us
    all_to_all x1, starting transfers between devices, body(): lax.all_to_all(outgoing.reshape(expert_count, capacity, width), 'exp', sp...  20 us
    pallas_call x2, Pallas kernels, gradient_rows(): pl.pallas_call(gradient_kernel, out_shape=jax.ShapeDtypeStruct((sources,...  7.62 us
    all_to_all x1, starting transfers between devices, body(): lax.all_to_all(hidden_units(shares, RING * CORES), 'dp', split_axis=0, co...  6.93 us
    all_to_all x1, starting transfers between devices, body(): lax.all_to_all(turn(mixed, shards), 'dp', split_axis=0, concat_axis=0, ti...  5.58 us
    ppermute x1, starting transfers between devices, body(): far = lax.ppermute(cross, 'dp', across_halves)  4.87 us
  transfers between devices with their start and end apart: 11, of which 6 were waited for; matrix products, arithmetic and copies ran while one was open for 2% of the time, Pallas kernels for 10%

profile of v6, /device:TPU:8, one launch (start us, length us, event | category | flops | bytes accessed | tf_op | source)
XLA Modules:
  0.0 166.7 jit_solution(11990288355901288838)
XLA Ops:
  6.5 0.0 copy-start
  6.5 0.0 all-gather.3.cloned.1.call-start
  6.5 0.7 all-gather.3.cloned.1.call-update
  7.3 0.0 copy-start.4
  7.3 0.0 copy-start.5
  7.3 4.7 %shard_map.100 = (bf16[320,896]{1,0:T(8,128)(2,1)}, bf16[320,896]{1,0:T(8,128)(2,1)}, bf16[320,896]{1,0:T(8,128)(2,1)}, bf16[320,896]{1,0:T(8,128)(2,1)}) custom-call(s32[1,128]{1,0:T(1,128)} %rows_ref.1, bf16[256,3584]{1,0:T(8,128)(2,1)} %grad_ref.1, f32[1,64,3584]{2,1,0:T(8,128)} %master_ref.1, bf16[1,64,3584]{2,1,0:T(8,128)(2,1)} %first_ref.1, ...), custom_call_target="tpu_custom_call" | custom-call | flops 234881024 | bytes 7000000 | tf_op jit(solution)/shard_map/pallas_call | solution.py:89
  12.0 3.5 %collective-permute-start = (bf16[320,896]{1,0:T(8,128)(2,1)}, bf16[320,896]{1,0:T(8,128)(2,1)S(1)}, u32[]{:S(2)}, u32[]{:S(2)}) collective-permute-start(bf16[320,896]{1,0:T(8,128)(2,1)} %get-tuple-element.19), channel_id=1, source_target_pairs={{0,2},{1,3},{2,4},{3,5},{4,6},{5,7},{6,0},{7,1},{8,10},{9,11},{10,... | collective-permute-start | bytes 1720328 | tf_op jit(solution)/shard_map/ppermute | solution.py:313
  15.5 15.5 %collective-permute-start.1 = (bf16[320,896]{1,0:T(8,128)(2,1)}, bf16[320,896]{1,0:T(8,128)(2,1)}, u32[]{:S(2)}, u32[]{:S(2)}) collective-permute-start(bf16[320,896]{1,0:T(8,128)(2,1)} %get-tuple-element.20), channel_id=1, source_target_pairs={{0,4},{1,5},{2,6},{3,7},{4,0},{5,1},{6,2},{7,3},{8,12},{9,13},{10,... | collective-permute-start | bytes 1720328 | tf_op jit(solution)/shard_map/ppermute | solution.py:313
  31.0 1.9 %collective-permute-start.2 = (bf16[320,896]{1,0:T(8,128)(2,1)}, bf16[320,896]{1,0:T(8,128)(2,1)}, u32[]{:S(2)}, u32[]{:S(2)}) collective-permute-start(bf16[320,896]{1,0:T(8,128)(2,1)} %get-tuple-element.21), channel_id=1, source_target_pairs={{0,6},{1,7},{2,0},{3,1},{4,2},{5,3},{6,4},{7,5},{8,14},{9,15},{10,... | collective-permute-start | bytes 1720328 | tf_op jit(solution)/shard_map/ppermute | solution.py:313
  33.0 0.0 copy-done.4
  33.0 0.1 eq.50
  33.1 0.1 fusion.5
  33.1 0.1 reduce_window_sum.11
  33.2 0.2 select_reduce_fusion
  33.4 0.0 copy-done.5
  33.4 0.2 convolution_convert_fusion
  33.7 0.1 copy.13
  33.8 0.7 reshape.57
  34.4 20.0 %all-to-all-start = ((bf16[64,2,224]{2,1,0:T(2,128)(2,1)}), bf16[64,2,224]{2,1,0:T(2,128)(2,1)S(1)}, u32[]{:S(2)}, u32[]{:S(2)}) async-start(bf16[64,2,224]{2,1,0:T(2,128)(2,1)} %reshape.57), calls=%async_computation | async-start | bytes 131072 | tf_op jit(solution)/shard_map/all_to_all | solution.py:334
  54.5 0.6 pad_add_fusion.place_ref
  55.1 24.4 %all-to-all-done = bf16[64,2,224]{2,1,0:T(2,128)(2,1)S(1)} async-done(((bf16[64,2,224]{2,1,0:T(2,128)(2,1)}), bf16[64,2,224]{2,1,0:T(2,128)(2,1)S(1)}, u32[]{:S(2)}, u32[]{:S(2)}) %all-to-all-start) | async-done | bytes 57376 | tf_op jit(solution)/shard_map/all_to_all | solution.py:334
  79.4 0.0 collective-permute-done.refs_1_
  79.4 0.0 copy-start.1
  79.5 0.0 collective-permute-done.1.refs_2_
  79.5 0.0 collective-permute-done.2.refs_3_
  79.5 0.8 copy-done.1
  80.3 3.1 %shard_map.101 = (bf16[4,320,448]{2,1,0:T(8,128)(2,1)}, bf16[4,320,448]{2,1,0:T(8,128)(2,1)}) custom-call(s32[3]{0:T(128)} %pad_add_fusion.place_ref, bf16[320,896]{1,0:T(8,128)(2,1)} %get-tuple-element.22.refs_0_, bf16[320,896]{1,0:T(8,128)(2,1)} %copy-done.1, bf16[320,896]{1,0:T(8,128)(2,1)} %collective-permute-done.1.refs_2_, ...), custom_call_target="tpu_custom_call" | custom-call | bytes 5000000 | tf_op jit(solution)/shard_map/pallas_call | solution.py:125
  83.4 1.9 %collective-permute-start.3 = (bf16[4,320,448]{2,1,0:T(8,128)(2,1)}, bf16[4,320,448]{2,1,0:T(8,128)(2,1)}, u32[]{:S(2)}, u32[]{:S(2)}) collective-permute-start(bf16[4,320,448]{2,1,0:T(8,128)(2,1)} %get-tuple-element.27), channel_id=1, source_target_pairs={{0,1},{1,0},{2,3},{3,2},{4,5},{5,4},{6,7},{7,6},{8,9},{9,8},{10,11... | collective-permute-start | bytes 3440648 | tf_op jit(solution)/shard_map/ppermute | solution.py:361
  85.3 0.1 reshape.58
  85.3 0.0 copy-done
  85.3 0.4 convolution_bitcast_fusion.mixed_ref
  85.8 1.0 shard_map.104
  86.8 5.6 %all-to-all-start.1 = ((bf16[16,2,64,128]{3,2,1,0:T(8,128)(2,1)}), bf16[16,2,64,128]{3,2,1,0:T(8,128)(2,1)S(1)}, u32[]{:S(2)}, u32[]{:S(2)}) async-start(bf16[16,2,64,128]{3,2,1,0:T(8,128)(2,1)} %shard_map.104), calls=%async_computation.1 | async-start | bytes 1048576 | tf_op jit(solution)/shard_map/all_to_all | solution.py:347
  92.4 0.0 collective-permute-done.3.near_ref
  92.4 0.0 all-gather.3.cloned.1.call-done
  92.4 3.8 %shard_map.103 = bf16[8,64,448]{2,1,0:T(8,128)(2,1)} custom-call(s32[3]{0:T(128)} %pad_add_fusion.place_ref, bf16[8,128,1024]{2,1,0:T(8,128)(2,1)} %bitcast.20, bf16[4,320,448]{2,1,0:T(8,128)(2,1)} %get-tuple-element.26.mine_ref, bf16[4,320,448]{2,1,0:T(8,128)(2,1)} %collective-permute-done.3.near_ref), custom_call_target="tpu_custom_call" | custom-call | flops 469762048 | bytes 4000000 | tf_op jit(solution)/shard_map/pallas_call | solution.py:157
  96.2 4.9 %collective-permute-start.4 = (bf16[8,64,448]{2,1,0:T(8,128)(2,1)}, bf16[8,64,448]{2,1,0:T(8,128)(2,1)S(1)}, u32[]{:S(2)}, u32[]{:S(2)}) collective-permute-start(bf16[8,64,448]{2,1,0:T(8,128)(2,1)} %shard_map.103), channel_id=1, source_target_pairs={{0,8},{1,9},{2,10},{3,11},{4,12},{5,13},{6,14},{7,15},{8,0},{9,1},... | collective-permute-start | bytes 1376264 | tf_op jit(solution)/shard_map/ppermute | solution.py:363
  101.1 0.1 all-to-all-done.1.shares_ref
  101.2 0.7 shard_map.105
  101.9 6.9 %all-to-all-start.2 = ((bf16[8,64,128]{2,1,0:T(8,128)(2,1)}), bf16[8,64,128]{2,1,0:T(8,128)(2,1)S(1)}, u32[]{:S(2)}, u32[]{:S(2)}) async-start(bf16[8,64,128]{2,1,0:T(8,128)(2,1)} %shard_map.105), calls=%async_computation.2 | async-start | bytes 262144 | tf_op jit(solution)/shard_map/all_to_all | solution.py:350
  108.9 3.9 %shard_map.102.kept_ref = f32[8,64,448]{2,1,0:T(8,128)} custom-call(s32[3]{0:T(128)} %pad_add_fusion.place_ref, bf16[8,128,1024]{2,1,0:T(8,128)(2,1)} %bitcast.21, bf16[4,320,448]{2,1,0:T(8,128)(2,1)} %get-tuple-element.26.mine_ref, bf16[4,320,448]{2,1,0:T(8,128)(2,1)} %collective-permute-done.3.near_ref), custom_call_target="tpu_custom_call" | custom-call | flops 469762048 | bytes 4000000 | tf_op jit(solution)/shard_map/pallas_call | solution.py:157
  112.8 0.0 copy-start.6
  112.8 0.8 all-to-all-done.2.hidden_ref
  113.6 0.0 copy-start.3
  113.6 0.2 collective-permute-done.4.far_ref
  113.8 0.5 copy-done.3
  114.3 0.0 copy-start.2
  114.3 0.8 copy-done.2
  115.1 4.8 %shard_map.106 = (f32[2,64,224]{2,1,0:T(8,128)}, bf16[2,64,224]{2,1,0:T(8,128)(2,1)}) custom-call(s32[3]{0:T(128)} %pad_add_fusion.place_ref, f32[8,64,448]{2,1,0:T(8,128)} %shard_map.102.kept_ref, bf16[8,64,448]{2,1,0:T(8,128)(2,1)} %copy-done.2, bf16[4,320,448]{2,1,0:T(8,128)(2,1)} %get-tuple-element.26.mine_ref, ...), custom_call_target="tpu_custom_call" | custom-call | flops 4587520 | bytes 5000000 | tf_op jit(solution)/shard_map/pallas_call | solution.py:226
  119.8 4.4 %collective-permute-start.5 = (bf16[2,64,224]{2,1,0:T(8,128)(2,1)}, bf16[2,64,224]{2,1,0:T(8,128)(2,1)S(1)}, u32[]{:S(2)}, u32[]{:S(2)}) collective-permute-start(bf16[2,64,224]{2,1,0:T(8,128)(2,1)} %get-tuple-element.30), channel_id=1, source_target_pairs={{0,8},{1,9},{2,10},{3,11},{4,12},{5,13},{6,14},{7,15},{8,0},{9,1},... | collective-permute-start | bytes 172040 | tf_op jit(solution)/shard_map/ppermute | solution.py:366
  124.2 3.5 %collective-permute-done.5 = bf16[2,64,224]{2,1,0:T(8,128)(2,1)S(1)} collective-permute-done((bf16[2,64,224]{2,1,0:T(8,128)(2,1)}, bf16[2,64,224]{2,1,0:T(8,128)(2,1)S(1)}, u32[]{:S(2)}, u32[]{:S(2)}) %collective-permute-start.5) | collective-permute-done | bytes 57376 | tf_op jit(solution)/shard_map/ppermute | solution.py:366
  127.7 0.9 add_convert_fusion
  128.6 0.7 reshape.59
  129.3 4.6 %all-to-all-start.3 = ((bf16[64,2,224]{2,1,0:T(2,128)(2,1)}), bf16[64,2,224]{2,1,0:T(2,128)(2,1)S(1)}, u32[]{:S(2)}, u32[]{:S(2)}) async-start(bf16[64,2,224]{2,1,0:T(2,128)(2,1)} %reshape.59), calls=%async_computation.3 | async-start | bytes 131072 | tf_op jit(solution)/shard_map/all_to_all | solution.py:368
  133.9 0.1 reduce_sum.21
  134.0 25.0 %all-to-all-done.3 = bf16[64,2,224]{2,1,0:T(2,128)(2,1)S(1)} async-done(((bf16[64,2,224]{2,1,0:T(2,128)(2,1)}), bf16[64,2,224]{2,1,0:T(2,128)(2,1)S(1)}, u32[]{:S(2)}, u32[]{:S(2)}) %all-to-all-start.3) | async-done | bytes 57376 | tf_op jit(solution)/shard_map/all_to_all | solution.py:368
  159.0 0.1 reshape.60
  159.0 0.0 copy-done.6
  159.1 0.8 fusion
  (2 shorter events, 0.0 us)
Async XLA Ops:
  6.5 78.8 %copy-start = (bf16[1,224,2,1024]{3,2,1,0:T(2,128)(2,1)S(1)}, bf16[1,224,2,1024]{3,2,1,0:T(2,128)(2,1)}, u32[]{:S(2)}) copy-start(bf16[1,224,2,1024]{3,2,1,0:T(2,128)(2,1)} %param.16) | copy-start | bytes 2752516
  6.5 85.9 %all-gather.3.cloned.1.call-start = ((), (), s32[]{:S(2)}) async-start(), calls=%async_computation.4 | async-start | bytes 2359296 | tf_op jit(solution)/shard_map/all_gather | solution.py:310
  7.3 25.7 %copy-start.4 = (s32[8,8]{1,0:T(8,128)S(1)}, s32[8,8]{1,0:T(8,128)}, u32[]{:S(2)}) copy-start(s32[8,8]{1,0:T(8,128)} %param.18) | copy-start | bytes 772
  7.3 26.2 %copy-start.5 = (bf16[8,224]{1,0:T(8,128)(2,1)S(1)}, bf16[8,224]{1,0:T(8,128)(2,1)}, u32[]{:S(2)}) copy-start(bf16[8,224]{1,0:T(8,128)(2,1)} %param.17) | copy-start | bytes 10756
  12.0 67.4 %collective-permute-start = (bf16[320,896]{1,0:T(8,128)(2,1)}, bf16[320,896]{1,0:T(8,128)(2,1)S(1)}, u32[]{:S(2)}, u32[]{:S(2)}) collective-permute-start(bf16[320,896]{1,0:T(8,128)(2,1)} %get-tuple-element.19), channel_id=1, source_target_pairs={{0,2},{1,3},{2,4},{3,5},{4,6},{5,7},{6,0},{7,1},{8,10},{9,11},{10,... | collective-permute-start | bytes 1720328 | tf_op jit(solution)/shard_map/ppermute | solution.py:313
  15.5 64.0 %collective-permute-start.1 = (bf16[320,896]{1,0:T(8,128)(2,1)}, bf16[320,896]{1,0:T(8,128)(2,1)}, u32[]{:S(2)}, u32[]{:S(2)}) collective-permute-start(bf16[320,896]{1,0:T(8,128)(2,1)} %get-tuple-element.20), channel_id=1, source_target_pairs={{0,4},{1,5},{2,6},{3,7},{4,0},{5,1},{6,2},{7,3},{8,12},{9,13},{10,... | collective-permute-start | bytes 1720328 | tf_op jit(solution)/shard_map/ppermute | solution.py:313
  31.0 48.4 %collective-permute-start.2 = (bf16[320,896]{1,0:T(8,128)(2,1)}, bf16[320,896]{1,0:T(8,128)(2,1)}, u32[]{:S(2)}, u32[]{:S(2)}) collective-permute-start(bf16[320,896]{1,0:T(8,128)(2,1)} %get-tuple-element.21), channel_id=1, source_target_pairs={{0,6},{1,7},{2,0},{3,1},{4,2},{5,3},{6,4},{7,5},{8,14},{9,15},{10,... | collective-permute-start | bytes 1720328 | tf_op jit(solution)/shard_map/ppermute | solution.py:313
  34.4 45.0 %all-to-all-start = ((bf16[64,2,224]{2,1,0:T(2,128)(2,1)}), bf16[64,2,224]{2,1,0:T(2,128)(2,1)S(1)}, u32[]{:S(2)}, u32[]{:S(2)}) async-start(bf16[64,2,224]{2,1,0:T(2,128)(2,1)} %reshape.57), calls=%async_computation | async-start | bytes 131072 | tf_op jit(solution)/shard_map/all_to_all | solution.py:334
  79.4 0.8 copy-start.1
  83.4 9.1 %collective-permute-start.3 = (bf16[4,320,448]{2,1,0:T(8,128)(2,1)}, bf16[4,320,448]{2,1,0:T(8,128)(2,1)}, u32[]{:S(2)}, u32[]{:S(2)}) collective-permute-start(bf16[4,320,448]{2,1,0:T(8,128)(2,1)} %get-tuple-element.27), channel_id=1, source_target_pairs={{0,1},{1,0},{2,3},{3,2},{4,5},{5,4},{6,7},{7,6},{8,9},{9,8},{10,11... | collective-permute-start | bytes 3440648 | tf_op jit(solution)/shard_map/ppermute | solution.py:361
  86.8 14.4 %all-to-all-start.1 = ((bf16[16,2,64,128]{3,2,1,0:T(8,128)(2,1)}), bf16[16,2,64,128]{3,2,1,0:T(8,128)(2,1)S(1)}, u32[]{:S(2)}, u32[]{:S(2)}) async-start(bf16[16,2,64,128]{3,2,1,0:T(8,128)(2,1)} %shard_map.104), calls=%async_computation.1 | async-start | bytes 1048576 | tf_op jit(solution)/shard_map/all_to_all | solution.py:347
  96.2 17.6 %collective-permute-start.4 = (bf16[8,64,448]{2,1,0:T(8,128)(2,1)}, bf16[8,64,448]{2,1,0:T(8,128)(2,1)S(1)}, u32[]{:S(2)}, u32[]{:S(2)}) collective-permute-start(bf16[8,64,448]{2,1,0:T(8,128)(2,1)} %shard_map.103), channel_id=1, source_target_pairs={{0,8},{1,9},{2,10},{3,11},{4,12},{5,13},{6,14},{7,15},{8,0},{9,1},... | collective-permute-start | bytes 1376264 | tf_op jit(solution)/shard_map/ppermute | solution.py:363
  101.9 11.6 %all-to-all-start.2 = ((bf16[8,64,128]{2,1,0:T(8,128)(2,1)}), bf16[8,64,128]{2,1,0:T(8,128)(2,1)S(1)}, u32[]{:S(2)}, u32[]{:S(2)}) async-start(bf16[8,64,128]{2,1,0:T(8,128)(2,1)} %shard_map.105), calls=%async_computation.2 | async-start | bytes 262144 | tf_op jit(solution)/shard_map/all_to_all | solution.py:350
  112.8 46.3 %copy-start.6 = (f32[8,8]{1,0:T(8,128)S(1)}, f32[8,8]{1,0:T(8,128)}, u32[]{:S(2)}) copy-start(f32[8,8]{1,0:T(8,128)} %param.19) | copy-start | bytes 772
  113.6 0.7 copy-start.3
  114.3 0.8 copy-start.2
  119.8 7.9 %collective-permute-start.5 = (bf16[2,64,224]{2,1,0:T(8,128)(2,1)}, bf16[2,64,224]{2,1,0:T(8,128)(2,1)S(1)}, u32[]{:S(2)}, u32[]{:S(2)}) collective-permute-start(bf16[2,64,224]{2,1,0:T(8,128)(2,1)} %get-tuple-element.30), channel_id=1, source_target_pairs={{0,8},{1,9},{2,10},{3,11},{4,12},{5,13},{6,14},{7,15},{8,0},{9,1},... | collective-permute-start | bytes 172040 | tf_op jit(solution)/shard_map/ppermute | solution.py:366
  129.3 29.7 %all-to-all-start.3 = ((bf16[64,2,224]{2,1,0:T(2,128)(2,1)}), bf16[64,2,224]{2,1,0:T(2,128)(2,1)S(1)}, u32[]{:S(2)}, u32[]{:S(2)}) async-start(bf16[64,2,224]{2,1,0:T(2,128)(2,1)} %reshape.59), calls=%async_computation.3 | async-start | bytes 131072 | tf_op jit(solution)/shard_map/all_to_all | solution.py:368
Sparse Core Ops, SparseCore 0:
  10.1 49.8 all-gather.2
